TPU v7x, 32 devices: a whole 2x2x4 slice. The times are simulated.
32 devices in a mesh: batch: 2 (over x), seq: 4 (over z), pool: 4 (over y, core).
Axes of the slice: x: 2, y: 2, z: 4, core: 2. Of those that a mesh axis runs over, the one named last changes fastest.
Arguments:
- tokens: bfloat16 [8, 1024, 1024], P(('batch', 'pool'), 'seq'), may hold values from -6 to 6
- w_in: bfloat16 [1024, 4096], replicated, may hold values from -0.1875 to 0.1875
- w_out: bfloat16 [1024, 1024], replicated, may hold values from -0.1875 to 0.1875
- w_proj: bfloat16 [1024, 256], replicated, may hold values from -0.1875 to 0.1875
- pos_embed: bfloat16 [8, 1024, 256], P(('batch', 'pool'), 'seq'), may hold values from -6 to 6
- pos_ids: int32 [8, 1024], P(('batch', 'pool'), 'seq'), may hold values from 0 to 1048575
- lengths: int32 [8], P(('batch', 'pool')), may hold values from 128 to 1024, as said below
- neg_embed: bfloat16 [2, 4096, 256], P('batch', 'pool'), may hold values from -0.375 to 0.375
- neg_ids: int32 [2, 4096], P('batch', 'pool'), may hold values from 0 to 1048575
Outputs:
- loss: float32 [8, 1024], P(('batch', 'pool'), 'seq')
- d_neg: float32 [2, 4096, 256], P('batch', 'pool', 'seq')
- d_proj: float32 [1024, 256], replicated
Inputs may be any that keep to these rules, and one draw needn't show every extreme that they name: `lengths`: every history has at least one valid event; in every draw one history is valid over all 1024 events.
All inputs are finite; a program needn't handle non-finite values.
Results may differ from a plain program's by a relative error of at most 0.017.
Values may be sent and summed in bfloat16 or wider, within the bound.
No kernel may reach another device: no remote copies, remote signals or barrier semaphores. Data moves between devices by JAX's collectives and lax.ppermute only.
A program may use at most 128 MiB of HBM per device.

v0:
```python
import math

import jax
import jax.numpy as jnp
from jax import lax
from jax.sharding import PartitionSpec as P

HEADS = 8
ITEMS = 1048576


SOFTMAX_WARMTH = 0.02
NORM_EPSILON = 1e-05
UNIT_EPSILON = 1e-06


def layer_norm(inputs):
    center = inputs - jnp.mean(inputs, axis=-1, keepdims=True)
    spread = jnp.mean(center * center, axis=-1, keepdims=True)
    return center / jnp.sqrt(spread + NORM_EPSILON)


def unit_rows(inputs):
    norms = jnp.sqrt(jnp.sum(inputs * inputs, axis=-1, keepdims=True) + UNIT_EPSILON)
    return (inputs / norms, norms)


def log_sample_chance(item_ids):
    ranks = item_ids.astype(jnp.float32) + 1.0
    return jnp.log(jnp.log1p(1.0 / ranks)) - jnp.log(jnp.log(jnp.float32(ITEMS) + 1.0))


def head_split(block):
    return block.reshape(block.shape[0], HEADS, block.shape[1] // HEADS).transpose(1, 0, 2)


def attend(query_block, query_pos, key_block, value_block, key_pos, length):
    width = query_block.shape[1]
    head_width = width // HEADS
    allowed = (key_pos[None, :] <= query_pos[:, None]) & (key_pos[None, :] < length)

    def one_head(parts):
        query_head, key_head, value_head = parts
        scores = jnp.dot(query_head, key_head.T, preferred_element_type=jnp.float32) / math.sqrt(
            head_width
        )
        weights = jnp.where(allowed, jax.nn.silu(scores), 0.0).astype(jnp.bfloat16)
        return jnp.dot(weights, value_head, preferred_element_type=jnp.float32)

    result = lax.map(
        one_head, (head_split(query_block), head_split(key_block), head_split(value_block))
    )
    return result.transpose(1, 0, 2).reshape(query_block.shape[0], width)


def body(tokens, w_in, w_out, w_proj, pos_embed, pos_ids, lengths, neg_embed, neg_ids):
    rows = tokens.shape[1]
    width = tokens.shape[2]
    seq_count = lax.axis_size("seq")
    pool_count = lax.axis_size("pool")
    hist_count = lax.axis_size("batch") * pool_count
    first = lax.axis_index("seq") * rows
    length = lengths[0]
    history = tokens[0]
    own_pos = first + jnp.arange(rows, dtype=jnp.int32)
    normed = layer_norm(history.astype(jnp.float32)).astype(jnp.bfloat16)
    mixed = jax.nn.silu(jnp.dot(normed, w_in, preferred_element_type=jnp.float32))
    gate_u = mixed[:, :width].astype(jnp.bfloat16)
    values = mixed[:, width : 2 * width].astype(jnp.bfloat16)
    queries = mixed[:, 2 * width : 3 * width].astype(jnp.bfloat16)
    keys = mixed[:, 3 * width :].astype(jnp.bfloat16)
    key_block = lax.all_gather(keys, "seq", axis=0, tiled=True)
    value_block = lax.all_gather(values, "seq", axis=0, tiled=True)
    key_pos = jnp.arange(key_block.shape[0], dtype=jnp.int32)
    attn = attend(queries, own_pos, key_block, value_block, key_pos, length)
    gated = (layer_norm(attn) * gate_u.astype(jnp.float32)).astype(jnp.bfloat16)
    layer_out = (
        jnp.dot(gated, w_out, preferred_element_type=jnp.float32) + history.astype(jnp.float32)
    ).astype(jnp.bfloat16)
    out_unit, out_norms = unit_rows(jnp.dot(layer_out, w_proj, preferred_element_type=jnp.float32))
    output_estimate = out_unit.astype(jnp.bfloat16)
    positive_direction = unit_rows(pos_embed[0].astype(jnp.float32))[0]
    positive_targets = pos_ids[0]
    valid = own_pos < length
    positive_score = jnp.sum(
        output_estimate.astype(jnp.float32) * positive_direction, axis=-1
    ) / SOFTMAX_WARMTH - log_sample_chance(positive_targets)
    embed_width = output_estimate.shape[1]
    col_width = embed_width // seq_count
    table, table_ids = (
        lax.all_gather(neg_embed[0], "pool", axis=0, tiled=True),
        lax.all_gather(neg_ids[0], "pool", axis=0, tiled=True),
    )
    unit_negs, neg_norms = unit_rows(table.astype(jnp.float32))
    negative_estimate = unit_negs.astype(jnp.bfloat16)
    negative_score = (
        jnp.dot(output_estimate, negative_estimate.T, preferred_element_type=jnp.float32)
        / SOFTMAX_WARMTH
        - log_sample_chance(table_ids)[None, :]
    )
    kept = jnp.where(table_ids[None, :] != positive_targets[:, None], jnp.exp(negative_score), 0.0)
    total = jnp.exp(positive_score) + jnp.sum(kept, axis=-1)
    negative_weights = (jnp.where(valid[:, None], kept / total[:, None], 0.0) / hist_count).astype(
        jnp.bfloat16
    )
    negative_portion = (
        jnp.dot(negative_weights.T, output_estimate, preferred_element_type=jnp.float32)
        / SOFTMAX_WARMTH
    )
    neg_term = (
        negative_portion - unit_negs * jnp.sum(unit_negs * negative_portion, axis=-1, keepdims=True)
    ) / neg_norms
    shard_rows = neg_term.shape[0] // pool_count
    blocks = neg_term.reshape(pool_count, shard_rows, seq_count, col_width).transpose(2, 0, 1, 3)
    blocks = blocks.reshape(seq_count * pool_count, shard_rows, col_width)
    d_neg = lax.psum_scatter(blocks, ("seq", "pool"), scatter_dimension=0, tiled=True)
    negative_rows = jnp.dot(negative_weights, negative_estimate, preferred_element_type=jnp.float32)
    loss = jnp.where(valid, jnp.log(total) - positive_score, 0.0)
    positive_weight = jnp.where(valid, jnp.exp(positive_score) / total - 1.0, 0.0) / hist_count
    unit_gradient = (positive_weight[:, None] * positive_direction + negative_rows) / SOFTMAX_WARMTH
    d_out = (
        (unit_gradient - out_unit * jnp.sum(out_unit * unit_gradient, axis=-1, keepdims=True))
        / out_norms
    ).astype(jnp.bfloat16)
    proj_term = jnp.dot(layer_out.T, d_out, preferred_element_type=jnp.float32)
    d_proj = lax.psum(proj_term, ("batch", "seq", "pool"))
    return (loss[None, :], d_neg, d_proj)


def solution(mesh):
    placed = (
        P(("batch", "pool"), "seq", None),
        P(),
        P(),
        P(),
        P(("batch", "pool"), "seq", None),
        P(("batch", "pool"), "seq"),
        P(("batch", "pool")),
        P("batch", "pool", None),
        P("batch", "pool"),
    )
    return jax.shard_map(
        body,
        mesh=mesh,
        in_specs=placed,
        out_specs=(P(("batch", "pool"), "seq"), P("batch", "pool", "seq"), P()),
        check_vma=False,
    )
```

profile of v0, /device:TPU:0, one launch (start us, length us, event | category | flops | bytes accessed | tf_op | source)
XLA Modules:
  0.0 361.3 jit_solution(7593729018757473513)
XLA Ops:
  7.2 1.3 convert_reduce_fusion
  8.6 1.3 fusion.35
  9.9 6.1 %multiply_convert_fusion.1 = bf16[256,4096]{1,0:T(8,128)(2,1)S(1)} fusion(bf16[1024,4096]{1,0:T(8,128)(2,1)} %param.12, bf16[1,256,1024]{2,1,0:T(8,128)(2,1)} %param.11, f32[256]{0:T(256)S(1)} %add_sqrt_fusion.4, f32[256]{0:T(256)S(1)} %broadcast_multiply_fusion.2), kind=kOutput, calls=%fused_computation.33 | convolution fusion | flops 2153775104 | bytes 11012096 | tf_op jit(solution)/shard_map/dot_general | solution.py:67
  16.0 1.3 copy-done.4
  17.3 1.3 fusion.60
  20.5 1.9 copy.28
  23.3 6.2 %all-gather = s32[1,4096]{1,0:T(1,128)S(1)} all-gather(s32[1,1024]{1,0:T(1,128)S(1)} %copy-done.10), channel_id=2, replica_groups=mesh['batch'=2,'seq'=4,'pool'=4] {'pool'}, dimensions={1}, use_global_device_ids=true | all-gather | bytes 20480 | tf_op jit(solution)/shard_map/all_gather | solution.py:92
  29.6 37.8 %all-gather.8.cloned.1.call-done = bf16[1024,1024]{1,0:T(8,128)(2,1)} async-done(((bf16[256,1024]{1,0:T(8,128)(2,1)}), bf16[1024,1024]{1,0:T(8,128)(2,1)}) %all-gather.8.cloned.1.call-update) | async-done | bytes 2097168 | tf_op jit(solution)/shard_map/all_gather | solution.py:73
  67.4 3.4 bitcast_bitcast_fusion
  70.8 42.9 %all-gather.6.cloned.1.call-done = bf16[1024,1024]{1,0:T(8,128)(2,1)} async-done(((bf16[256,1024]{1,0:T(8,128)(2,1)}), bf16[1024,1024]{1,0:T(8,128)(2,1)}) %all-gather.6.cloned.1.call-update) | async-done | bytes 2097168 | tf_op jit(solution)/shard_map/all_gather | solution.py:72
  113.7 3.3 bitcast_bitcast_fusion.1
  117.0 14.4 %while.11 = (s32[]{:T(128)}, f32[8,256,128]{2,1,0:T(8,128)S(1)}, bf16[8,256,128]{2,1,0:T(8,128)(2,1)}, bf16[8,1024,128]{2,1,0:T(8,128)(2,1)}, bf16[8,1024,128]{2...) while((s32[]{:T(128)}, f32[8,256,128]{2,1,0:T(8,128)S(1)}, ...), condition=%wide.region_3.4_spmd.clone, body=%wide.region_2.3_spmd.clone.sunk | while | flops 136577024 | bytes 725077 | solution.py:50
  117.0 1.8 fusion.79
  118.8 1.8 fusion.79
  120.6 1.8 fusion.79
  122.4 1.8 fusion.79
  124.2 1.8 fusion.79
  126.0 1.8 fusion.79
  127.8 1.8 fusion.79
  129.6 1.8 fusion.79
  131.9 2.0 fusion.31
  134.7 2.4 all-gather.10.cloned.1.call-done
  137.2 2.0 fusion.28
  139.3 3.2 fusion.61
  145.1 1.3 fusion.53
  146.7 3.4 multiply_reduce_fusion
  150.1 2.9 subtract_divide_fusion
  153.0 6.0 %reshape.146 = f32[4,1024,4,64]{1,0,3,2:T(4,128)} reshape(f32[4096,256]{0,1:T(8,128)} %subtract_divide_fusion) | data formatting | bytes 8388608 | tf_op jit(solution)/shard_map/reshape | solution.py:114
  159.0 6.6 %copy.18 = f32[4,4,1024,64]{2,3,1,0:T(8,128)} copy(f32[4,4,1024,64]{2,1,3,0:T(4,128)} %bitcast.124) | data formatting | bytes 8388608 | tf_op jit(solution)/shard_map/transpose | solution.py:114
  166.3 110.2 %all-reduce.2.cloned.1.call-done = f32[1024,256]{1,0:T(8,128)} async-done(((f32[1024,256]{1,0:T(8,128)}), f32[1024,256]{1,0:T(8,128)}) %all-reduce.2.cloned.1.call-update) | async-done | bytes 1048592 | tf_op jit(solution)/shard_map/psum | solution.py:126
  276.4 76.1 %reduce-scatter.2.cloned.1.call-done = f32[1,1024,64]{1,2,0:T(8,128)} async-done(((f32[16,1024,64]{1,2,0:T(8,128)}), f32[1,1024,64]{1,2,0:T(8,128)}) %reduce-scatter.2.cloned.1.call-update) | async-done | bytes 262160 | tf_op jit(solution)/shard_map/reduce_scatter | solution.py:116
  352.5 2.3 copy.40
  (56 shorter events, 6.9 us)
Async XLA Ops:
  7.2 124.7 %copy-start = (bf16[1024,1024]{1,0:T(8,128)(2,1)S(1)}, bf16[1024,1024]{1,0:T(8,128)(2,1)}, u32[]{:S(2)}) copy-start(bf16[1024,1024]{1,0:T(8,128)(2,1)} %param.13) | copy-start | bytes 6291460
  7.2 60.2 %all-gather.8.cloned.1.call-start = ((), (), s32[]{:S(2)}) async-start(), calls=%async_computation.2 | async-start | bytes 2621440 | tf_op jit(solution)/shard_map/all_gather | solution.py:73
  16.0 1.3 copy-start.4
  17.3 2.1 copy-start.5
  17.3 5.8 %copy-start.9 = (bf16[1,256,256]{2,1,0:T(8,128)(2,1)S(1)}, bf16[1,256,256]{2,1,0:T(8,128)(2,1)}, u32[]{:S(2)}) copy-start(bf16[1,256,256]{2,1,0:T(8,128)(2,1)} %param.15) | copy-start | bytes 393220
  17.3 6.0 %copy-start.10 = (s32[1,1024]{1,0:T(1,128)S(1)}, s32[1,1024]{1,0:T(1,128)}, u32[]{:S(2)}) copy-start(s32[1,1024]{1,0:T(1,128)} %param.19) | copy-start | bytes 12292
  18.6 95.0 %all-gather.6.cloned.1.call-start = ((), (), s32[]{:S(2)}) async-start(), calls=%async_computation.1 | async-start | bytes 2621440 | tf_op jit(solution)/shard_map/all_gather | solution.py:72
  19.4 117.8 %all-gather.10.cloned.1.call-start = ((), (), s32[]{:S(2)}) async-start(), calls=%async_computation.5 | async-start | bytes 2621440 | tf_op jit(solution)/shard_map/all_gather | solution.py:91
  20.5 256.0 %all-reduce.2.cloned.1.call-start = ((), (), s32[]{:S(2)}) async-start(), calls=%async_computation.4 | async-start | bytes 2097152 | tf_op jit(solution)/shard_map/psum | solution.py:126
  131.8 2.1 copy-start.6
  131.9 7.4 %copy-start.11 = (s32[1,256]{1,0:T(1,128)S(1)}, s32[1,256]{1,0:T(1,128)}, u32[]{:S(2)}) copy-start(s32[1,256]{1,0:T(1,128)} %param.16) | copy-start | bytes 3076
  133.9 0.8 copy-start.7
  142.5 1.6 copy-start.1
  143.3 1.5 copy-start.3
  144.1 1.0 copy-start.8
  146.5 206.1 %reduce-scatter.2.cloned.1.call-start = ((), (), s32[]{:S(2)}) async-start(), calls=%async_computation.3 | async-start | bytes 4456448 | tf_op jit(solution)/shard_map/reduce_scatter | solution.py:116
  146.7 3.4 copy-start.2
Sparse Core Ops, SparseCore 0:
  18.7 48.6 all-gather.7
  69.0 44.6 all-gather.5
  115.8 21.2 all-gather.9
  146.6 129.7 all-reduce.1
  281.2 71.2 reduce-scatter.1
where the time goes:
time: 362 us; the launch traced here: 361 us
  waiting for transfers between devices  270 us (75%)
  matrix products  31.4 us (9%)
  local copies, waits for them, and re-layouts  28.7 us (8%)
  between operations  14.7 us (4%)
  other arithmetic  9.6 us (3%)
  blocking collectives  6.22 us (2%)
    psum x1, waiting for transfers between devices, body(): d_proj = lax.psum(proj_term, ('batch', 'seq', 'pool'))  110 us
    reduce_scatter x1, waiting for transfers between devices, body(): lax.psum_scatter(blocks, ('seq', 'pool'), scatter_dimension=0, tiled=True)  76.1 us
    all_gather x1, waiting for transfers between devices, body(): key_block = lax.all_gather(keys, 'seq', axis=0, tiled=True)  42.9 us
    all_gather x1, waiting for transfers between devices, body(): value_block = lax.all_gather(values, 'seq', axis=0, tiled=True)  37.8 us
    dot_general x8, matrix products, one_head(): return jnp.dot(weights, value_head, preferred_element_type=jnp.float32)  14.3 us
  transfers between devices with their start and end apart: 5, of which 5 were waited for; matrix products, arithmetic and copies ran while one was open for 13% of the time, Pallas kernels for 0%

commit v1 on v0

v1 whole, which is shorter than its diff:
```python
import functools
import itertools
import math

import jax
import jax.numpy as jnp
from jax import lax
from jax.experimental import pallas as pl
from jax.experimental.pallas import tpu as pltpu
from jax.sharding import PartitionSpec as P

HEADS = 8
ITEMS = 1048576

SOFTMAX_WARMTH = 0.02
NORM_EPSILON = 1e-05
UNIT_EPSILON = 1e-06
LOG2E = math.log2(math.e)
SCORE_SCALE = LOG2E / SOFTMAX_WARMTH
FAR = 10000.0

F32 = jnp.float32
BF16 = jnp.bfloat16
MIB = 1 << 20


def log_sample_chance(item_ids):
    x = 1.0 / (item_ids + 1.0)
    series = x * (1.0 - x * (1 / 2 - x * (1 / 3 - x * (1 / 4 - x * (1 / 5 - x * (1 / 6))))))
    return jnp.log(jnp.where(x > 1 / 16, jnp.log(1.0 + x), series)) - math.log(math.log(ITEMS + 1.0))


def column(row):
    return jnp.broadcast_to(row, (128, row.shape[1])).T[:, :1]


def dot(a, b):
    return jnp.dot(a, b, preferred_element_type=F32)


def dot_t(a, b):
    return lax.dot_general(a, b, (((1,), (1,)), ((), ())), preferred_element_type=F32)


def t_dot(a, b):
    return lax.dot_general(a, b, (((0,), (0,)), ((), ())), preferred_element_type=F32)


def silu(v):
    half = 0.5 * v
    return half + half * jnp.tanh(half)


def row_norm(x, keep=None):
    center = x - jnp.mean(x, axis=-1, keepdims=True)
    scale = lax.rsqrt(jnp.mean(center * center, axis=-1, keepdims=True) + NORM_EPSILON)
    if keep is not None:
        scale = jnp.where(keep, scale, 0.0)
    return center * scale


def norm_of(x):
    return jnp.sqrt(jnp.sum(x * x, axis=-1, keepdims=True) + UNIT_EPSILON)


def kept_rows(first, rows, length):
    return first + lax.broadcasted_iota(jnp.int32, (rows, 1), 0) < length


def attend(q_ref, keys, values, acc_ref, before_ref, causal=None):
    rows, width = q_ref.shape
    head = width // HEADS
    for h in range(HEADS):
        cols = slice(h * head, (h + 1) * head)
        half = dot_t(q_ref[:, cols], keys[:, cols]) * (0.5 / math.sqrt(head))
        weights = half + half * jnp.tanh(half)
        if causal is not None:
            weights = jnp.where(causal, weights, 0.0)
        part = dot(weights.astype(BF16), values[:, cols])
        acc_ref[:, cols] = part if before_ref is None else before_ref[:, cols] + part


def project(normed, w_ref, block):
    width = normed.shape[1]
    return silu(dot(normed, w_ref[:, block * width : (block + 1) * width])).astype(BF16)


def causal_mask(rows):
    return lax.broadcasted_iota(jnp.int32, (rows, rows), 0) >= lax.broadcasted_iota(jnp.int32, (rows, rows), 1)


def own_kernel(info_ref, x_ref, w_ref, gate_ref, q_ref, k_ref, v_ref, acc_ref):
    rows = x_ref.shape[0]
    keep = kept_rows(info_ref[0], rows, info_ref[1])
    normed = row_norm(x_ref[...].astype(F32), keep).astype(BF16)
    gate_ref[...] = project(normed, w_ref, 0)
    q_ref[...] = project(normed, w_ref, 2)
    keys, values = project(normed, w_ref, 3), project(normed, w_ref, 1)
    k_ref[...] = keys
    v_ref[...] = values
    attend(q_ref, keys, values, acc_ref, None, causal_mask(rows))


def guest_kernel(info_ref, x_ref, w_ref, k_ref, v_ref, gate_ref, q_ref, acc_ref):
    rows = x_ref.shape[0]
    keep = kept_rows(info_ref[0] + rows, rows, info_ref[1])
    normed = row_norm(x_ref[...].astype(F32), keep).astype(BF16)
    gate_ref[...] = project(normed, w_ref, 0)
    q_ref[...] = project(normed, w_ref, 2)
    attend(q_ref, project(normed, w_ref, 3), project(normed, w_ref, 1), acc_ref, None, causal_mask(rows))
    attend(q_ref, k_ref[...], v_ref[...], acc_ref, acc_ref)


def add_block(info_ref, back, x_ref, w_ref, q_refs, acc_refs, before_refs):
    keep = kept_rows(info_ref[0] - back, x_ref.shape[0], info_ref[1])
    normed = row_norm(x_ref[...].astype(F32), keep).astype(BF16)
    keys, values = project(normed, w_ref, 3), project(normed, w_ref, 1)
    for q_ref, acc_ref, before_ref in zip(q_refs, acc_refs, before_refs):
        attend(q_ref, keys, values, acc_ref, before_ref)


def step_kernel(back, info_ref, x_ref, w_ref, *refs):
    add_block(info_ref, back, x_ref, w_ref, refs[:2], refs[4:], refs[2:4])


def last_kernel(back, info_ref, x_ref, w_ref, *refs):
    q_refs, before_refs, gate_refs, own_refs = refs[:2], refs[2:4], refs[4:6], refs[6:8]
    w_out_ref, w_proj_ref, layer_ref, out_ref, hat_ref, *acc_refs = refs[8:]
    add_block(info_ref, back, x_ref, w_ref, q_refs, acc_refs, before_refs)
    gated = [
        (row_norm(acc_ref[...]) * gate_ref[...].astype(F32)).astype(BF16)
        for acc_ref, gate_ref in zip(acc_refs, gate_refs)
    ]
    rest = jnp.concatenate([own_ref[...] for own_ref in own_refs], axis=0).astype(F32)
    layer = (dot(jnp.concatenate(gated, axis=0), w_out_ref[...]) + rest).astype(BF16)
    layer_ref[...] = layer
    out = dot(layer, w_proj_ref[...])
    out_ref[...] = out
    hat_ref[...] = (out / norm_of(out)).astype(BF16)


def split3(x):
    high = x.astype(BF16).astype(F32)
    mid = (x - high).astype(BF16).astype(F32)
    return [high, mid, x - high - mid]


def id_digits(ids):
    return [(ids >> 14).astype(F32), ((ids >> 7) & 127).astype(F32), (ids & 127).astype(F32)]


def of_digits(a, b, c):
    return a * 16384.0 + b * 128.0 + c


def padded_rows(count):
    return -(-count // 16) * 16


def table_kernel(x_ref, ids_ref, pos_ref, pos_ids_ref, table_ref, message_ref):
    count, embed = x_ref.shape
    x = x_ref[...].astype(F32)
    table_ref[:count, :] = (x / norm_of(x)).astype(BF16)
    ids = jnp.concatenate([ids_ref[:, i : i + embed] for i in range(0, count, embed)], axis=0)
    parts = split3(log_sample_chance(ids.astype(F32)) * LOG2E) + id_digits(ids)
    used = len(parts) * ids.shape[0]
    pad = jnp.zeros((table_ref.shape[0] - count - used, embed), F32)
    table_ref[count:, :] = jnp.concatenate(parts + [pad], axis=0).astype(BF16)
    rows = pos_ref.shape[0]
    parts = id_digits(pos_ids_ref[...])
    pad = jnp.zeros((message_ref.shape[0] - rows - len(parts), embed), F32)
    message_ref[:rows, :] = pos_ref[...]
    message_ref[rows:, :] = jnp.concatenate(parts + [pad], axis=0).astype(BF16)


def head_kernel(
    hist_count, info_ref, hat_ref, out_ref, layer_ref, pos_ref, ids_ref, guest_ref, *rest
):
    *table_refs, loss_ref, guest_loss_ref, message_ref, keep_ref, send_ref, proj_ref = rest
    rows, embed = hat_ref.shape
    block = rows // 2
    chunks = table_refs[0].shape[0] // (embed + 6)
    count = chunks * embed
    hat = hat_ref[...]
    guest_parts = guest_ref[block:, :].astype(F32)
    id_rows = [id_digits(ids_ref[...]), [guest_parts[i : i + 1, :] for i in range(3)]]
    id_row = jnp.concatenate([of_digits(*digits) for digits in id_rows], axis=1)
    pos_id = column(id_row)
    pos = jnp.concatenate([pos_ref[...], guest_ref[:block, :]], axis=0).astype(F32)
    pos_unit = pos / norm_of(pos)
    pos_score = (
        jnp.sum(hat.astype(F32) * pos_unit, axis=-1, keepdims=True) / SOFTMAX_WARMTH - column(log_sample_chance(id_row))
    )
    lanes = jnp.zeros((rows, 128), F32)
    grads = jnp.zeros((rows, embed), F32)
    for table_ref in table_refs:
        parts = table_ref[count:, :].astype(F32)
        for chunk in range(chunks):
            bias, ids = (
                [parts[(g + j) * chunks + chunk : (g + j) * chunks + chunk + 1, :] for j in range(3)]
                for g in (0, 3)
            )
            table = table_ref[chunk * embed : (chunk + 1) * embed, :]
            scores = dot_t(hat, table) * SCORE_SCALE - (bias[0] + bias[1] + bias[2])
            kept = jnp.where(of_digits(*ids) != pos_id, jnp.exp2(scores), 0.0)
            for lane in range(0, embed, 128):
                lanes = lanes + kept[:, lane : lane + 128]
            grads = grads + dot(kept.astype(BF16), table)
    pos_part = jnp.exp(pos_score)
    total = pos_part + jnp.sum(lanes, axis=-1, keepdims=True)
    log_total = jnp.log(total)
    at = lax.broadcasted_iota(jnp.int32, (rows, 1), 0)
    valid = info_ref[0] + at < jnp.where(at < block, info_ref[5], info_ref[6])
    loss = jnp.where(valid, log_total - pos_score, 0.0)
    shift = jnp.where(valid, (log_total + math.log(hist_count)) * LOG2E, FAR)
    loss = jnp.broadcast_to(loss, (rows, 128)).T
    loss_ref[...] = loss[:1, :block]
    guest_loss_ref[...] = loss[:1, block:]
    shift = jnp.broadcast_to(shift, (rows, 128)).T
    parts = []
    for i in range(2):
        parts += split3(shift[:1, i * block : (i + 1) * block]) + id_rows[i]
    pad = jnp.zeros((message_ref.shape[0] - rows - len(parts), embed), F32)
    message_ref[:rows, :] = hat
    message_ref[rows:, :] = jnp.concatenate(parts + [pad], axis=0).astype(BF16)
    share = jnp.where(valid, 1.0 / (total * hist_count), 0.0)
    pos_weight = jnp.where(valid, pos_part / total - 1.0, 0.0) / hist_count
    d_unit = (pos_weight * pos_unit + share * grads) / SOFTMAX_WARMTH
    out = out_ref[...]
    norms = norm_of(out)
    unit = out / norms
    d_out = ((d_unit - unit * jnp.sum(unit * d_unit, axis=-1, keepdims=True)) / norms).astype(BF16)
    proj_ref[...] = t_dot(layer_ref[...], d_out)
    half = keep_ref.shape[0]
    keep_ref[...] = proj_ref[part_at(info_ref[3], half), :]
    send_ref[...] = proj_ref[part_at(1 - info_ref[3], half), :].astype(BF16)


def part_at(index, rows):
    return pl.ds(pl.multiple_of(index * rows, rows), rows)


def halved_kernel(info_ref, keep_ref, got_ref, own_ref, *rest):
    *send_refs, sum_ref = rest
    rows = own_ref.shape[0]
    sum_ref[...] = keep_ref[...] + got_ref[...].astype(F32)
    own_ref[...] = sum_ref[part_at(info_ref[4], rows), :]
    for r, send_ref in enumerate(send_refs, 1):
        send_ref[...] = sum_ref[part_at(lax.bitwise_xor(info_ref[4], r), rows), :].astype(BF16)


def sum_kernel(*refs):
    parts = [ref[...].astype(F32) for ref in refs[:-1]]
    while len(parts) > 1:
        parts = [a + b for a, b in zip(parts[::2], parts[1::2])]
    refs[-1][...] = parts[0].astype(refs[-1].dtype)


def lay_kernel(slot, info_ref, *refs):
    *part_refs, out_ref = refs
    rows = part_refs[0].shape[0]
    for r, part_ref in enumerate(part_refs):
        at = part_at(lax.bitwise_xor(info_ref[slot], r), rows)
        out_ref[at, :] = part_ref[...].astype(out_ref.dtype)


def cut_blocks(values, keep_ref, send_ref, rows):
    for i in range(values.shape[0] // rows):
        to_ref = send_ref if i % 2 else keep_ref
        to_ref[i // 2 * rows : (i // 2 + 1) * rows, :] = values[i * rows : (i + 1) * rows, :].astype(to_ref.dtype)


def halving_kernel(rows, keep_ref, got_ref, next_keep_ref, next_send_ref):
    cut_blocks(keep_ref[...] + got_ref[: keep_ref.shape[0], :].astype(F32), next_keep_ref, next_send_ref, rows)


def loss_kernel(last, info_ref, loss_ref, got_ref, own_loss_ref):
    rows = loss_ref.shape[1]
    parts = got_ref[got_ref.shape[0] - 16 :, :rows].astype(F32)
    above = parts[0:1, :] + parts[1:2, :] + parts[2:3, :]
    own_loss_ref[...] = jnp.where(info_ref[2] == last, above, loss_ref[...])


def negative_kernel(seq_count, info_ref, neg_ref, neg_id_ref, loss_ref, *rest):
    *message_refs, keep_ref, send_ref, turned_ref, sum_ref = rest
    count, embed = neg_ref.shape
    rows = embed
    blocks = message_refs[0].shape[0] // rows
    tile = min(256, count)
    neg = neg_ref[...].astype(F32)
    norms = norm_of(neg)
    unit = neg / norms
    neg_hat = unit.astype(BF16)
    id_row = neg_id_ref[...].astype(F32)
    neg_id = column(id_row)
    for i, (message_ref, block) in enumerate(itertools.product(message_refs, range(blocks))):
        hats = message_ref[block * rows : (block + 1) * rows, :]
        parts = message_ref[blocks * rows :, :].astype(F32)[6 * block : 6 * block + 6, :]
        shifts = parts[0:1, :] + parts[1:2, :] + parts[2:3, :]
        ids = of_digits(parts[3:4, :], parts[4:5, :], parts[5:6, :])
        for start in range(0, count, tile):
            cut = slice(start, start + tile)
            scores = dot_t(neg_hat[cut, :], hats) * SCORE_SCALE - shifts
            weights = jnp.where(neg_id[cut, :] != ids, jnp.exp2(scores), 0.0)
            term = dot(weights.astype(BF16), hats)
            sum_ref[cut, :] = sum_ref[cut, :] + term if i else term
    neg_sum = sum_ref[...] * column(jnp.exp2(-LOG2E * log_sample_chance(id_row)) / SOFTMAX_WARMTH)
    grad = (neg_sum - unit * jnp.sum(unit * neg_sum, axis=-1, keepdims=True)) / norms
    turned_ref[...] = grad.T
    kept = keep_ref.shape[0]
    cols = kept // (seq_count // 2)
    for r in range(seq_count):
        at = part_at(lax.bitwise_xor(info_ref[2], r), cols)
        to_ref = send_ref if r % 2 else keep_ref
        to_ref[r // 2 * cols : (r // 2 + 1) * cols, :] = turned_ref[at, :].astype(to_ref.dtype)
    parts = split3(loss_ref[...])
    pad = jnp.zeros((16 - len(parts), loss_ref.shape[1]), F32)
    send_ref[kept:, :] = jnp.zeros((16, count), BF16)
    send_ref[kept:, : loss_ref.shape[1]] = jnp.concatenate(parts + [pad], axis=0).astype(BF16)


def call(kernel, ins, outs, scratch=(), limit=24, flops=0, moved=0, name=None):
    in_specs = [pl.BlockSpec(memory_space=pltpu.SMEM if x.ndim == 1 else pltpu.VMEM) for x in ins]
    many = isinstance(outs, (list, tuple))
    out_specs = jax.tree.map(lambda _: pl.BlockSpec(memory_space=pltpu.VMEM), outs)
    return pl.pallas_call(
        kernel,
        out_shape=list(outs) if many else outs,
        in_specs=in_specs,
        out_specs=list(out_specs) if many else out_specs,
        scratch_shapes=list(scratch),
        compiler_params=pltpu.CompilerParams(vmem_limit_bytes=limit * MIB),
        cost_estimate=pl.CostEstimate(flops=flops, bytes_accessed=moved, transcendentals=0),
        name=name,
    )(*ins)


def swap(x, axis, count, r):
    return lax.ppermute(x, axis, [(i, i ^ r) for i in range(count)])


def gather_step(blocks, axis, count):
    bit = count // (2 * len(blocks))
    return blocks + [swap(block, axis, count, bit) for block in blocks] if bit else blocks


def together(*trees):
    return lax.optimization_barrier(trees)


def struct(shape, kind):
    return jax.ShapeDtypeStruct(shape, kind)


def body(tokens, w_in, w_out, w_proj, pos_embed, pos_ids, lengths, neg_embed, neg_ids):
    rows, width = tokens.shape[1:]
    embed = w_proj.shape[1]
    seq_count = lax.axis_size("seq")
    pool_count = lax.axis_size("pool")
    plane = ("batch", "pool")
    plane_count = lax.axis_size("batch") * pool_count
    seq_at = lax.axis_index("seq")
    plane_at = lax.axis_index("batch") * pool_count + lax.axis_index("pool")
    own_end = jnp.where(seq_at == seq_count - 1, 0, lengths[0])
    guest_end = jnp.where(seq_at == seq_count - 2, lengths[0], 0)
    info = jnp.stack([seq_at * rows, lengths[0], seq_at, plane_at % 2, plane_at // 2, own_end, guest_end])
    info = info.astype(jnp.int32)
    own = tokens[0]
    local_neg = neg_embed.shape[1]

    up = [(i, i + 1) for i in range(seq_count - 2)]
    down = [(seq_count - 1, seq_count - 2)]
    block = lax.ppermute(own, "seq", up)
    guest = lax.ppermute(own, "seq", down)
    kind = struct((rows, width), BF16)
    wide = struct((rows, width), F32)
    gate, queries, keys, values, acc = call(
        own_kernel,
        [info, own, w_in],
        [kind, kind, kind, kind, wide],
        flops=2 * rows * width * (w_in.shape[1] + 2 * rows),
        moved=2 * w_in.size,
        name="own_block",
    )
    table_part, pos_part = call(
        table_kernel,
        [neg_embed[0], neg_ids, pos_embed[0], pos_ids],
        [
            struct((local_neg + padded_rows(6 * local_neg // embed), embed), BF16),
            struct((rows + 16, embed), BF16),
        ],
        name="table_part",
    )
    table_part, pos_part, acc = together(table_part, pos_part, acc)
    table = gather_step([table_part], "pool", pool_count)
    block, guest, acc = together(block, guest, acc)
    for step in range(1, seq_count - 2):
        following = lax.ppermute(block, "seq", up)
        if step == 1:
            guest_gate, guest_queries, guest_acc = call(
                guest_kernel, [info, guest, w_in, keys, values], [kind, kind, wide], name="guest_block"
            )
        acc, guest_acc = call(
            functools.partial(step_kernel, step * rows),
            [info, block, w_in, queries, guest_queries, acc, guest_acc],
            [wide, wide],
            name=f"earlier_block_{step}",
        )
        acc, table, pos_part = together(acc, table, pos_part)
        if step == 1:
            guest_pos = lax.ppermute(pos_part, "seq", down)
        table = gather_step(table, "pool", pool_count)
        block, acc = together(following, acc)
    while len(table) < pool_count:
        table = gather_step(table, "pool", pool_count)
    layer, out, hat = call(
        functools.partial(last_kernel, (seq_count - 2) * rows),
        [info, block, w_in, queries, guest_queries, acc, guest_acc, gate, guest_gate, own, guest, w_out, w_proj],
        [struct((2 * rows, width), BF16), struct((2 * rows, embed), F32), struct((2 * rows, embed), BF16)],
        scratch=[pltpu.VMEM((rows, width), F32)] * 2,
        flops=2 * rows * width * (4 * width + 4 * rows + 2 * embed),
        moved=6 * width * width,
        name="last_block",
    )

    half, chips = width // 2, plane_count // 2
    loss, guest_loss, message, keep, send = call(
        functools.partial(head_kernel, plane_count),
        [info, hat, out, layer, pos_embed[0], pos_ids, guest_pos, *table],
        [
            struct((1, rows), F32), struct((1, rows), F32), struct((2 * rows + 16, embed), BF16),
            struct((half, embed), F32), struct((half, embed), BF16),
        ],
        scratch=[pltpu.VMEM((width, embed), F32)],
        flops=8 * rows * local_neg * pool_count * embed,
        moved=2 * local_neg * pool_count * embed,
        name="head",
    )
    part = struct((half // chips, embed), BF16)
    cols = embed // seq_count
    def plane_swap(parts):
        return [swap(x, plane, plane_count, 2 * r) for r, x in enumerate(parts, 1)]

    got = swap(send, plane, plane_count, 1)
    messages = gather_step([message], "pool", pool_count)
    own_part, *sends = call(
        halved_kernel,
        [info, keep, got],
        [struct(part.shape, F32)] + [part] * (chips - 1),
        scratch=[pltpu.VMEM((half, embed), F32)],
        name="halved",
    )
    own_part, messages = together(own_part, messages)
    while len(messages) < pool_count:
        messages = gather_step(messages, "pool", pool_count)
    proj_parts = [own_part] + plane_swap(sends)
    keep, send = call(
        functools.partial(negative_kernel, seq_count),
        [info, neg_embed[0], neg_ids, guest_loss, *messages],
        [struct((embed // 2, local_neg), F32), struct((embed // 2 + 16, local_neg), BF16)],
        scratch=[pltpu.VMEM((embed, local_neg), F32), pltpu.VMEM((local_neg, embed), F32)],
        name="neg_grad",
    )
    proj_parts, keep, send = together(proj_parts, keep, send)
    proj_part = call(sum_kernel, proj_parts, part, name="plane_sum")
    bit = 1
    while bit < seq_count:
        if bit == 1:
            proj_part, send = together(proj_part, send)
        proj_got, got = swap(proj_part, "seq", seq_count, bit), swap(send, "seq", seq_count, bit)
        proj_part = call(sum_kernel, [proj_part, proj_got], part, name=f"seq_sum_{bit}")
        if 2 * bit < seq_count:
            if bit == 1:
                loss = call(
                    functools.partial(loss_kernel, seq_count - 1), [info, loss, got], struct((1, rows), F32), name="loss"
                )
            size = keep.shape[0] // 2
            keep, send = call(
                functools.partial(halving_kernel, cols),
                [keep, got],
                [struct((size, local_neg), F32), struct((size, local_neg), BF16)],
                name=f"neg_halved_{bit}",
            )
        bit *= 2
    proj_parts, got = together([proj_part] + plane_swap([proj_part] * (chips - 1)), got)
    proj_half = call(
        functools.partial(lay_kernel, 4), [info, *proj_parts], struct((half, embed), BF16), name="lay_half"
    )
    other_half = swap(proj_half, plane, plane_count, 1)
    d_neg = call(sum_kernel, [keep, got], struct((cols, local_neg), F32), name="neg_sum")
    d_proj = call(
        functools.partial(lay_kernel, 3), [info, proj_half, other_half], struct((width, embed), F32), name="lay_whole"
    )
    return (loss, d_neg.T[None], d_proj)


def solution(mesh):
    placed = (
        P(("batch", "pool"), "seq", None),
        P(),
        P(),
        P(),
        P(("batch", "pool"), "seq", None),
        P(("batch", "pool"), "seq"),
        P(("batch", "pool")),
        P("batch", "pool", None),
        P("batch", "pool"),
    )
    return jax.shard_map(
        body,
        mesh=mesh,
        in_specs=placed,
        out_specs=(P(("batch", "pool"), "seq"), P("batch", "pool", "seq"), P()),
        check_vma=False,
    )
```

time: 362 us -> 92.7 us (0.26)
  waiting for transfers between devices: 270 us -> 24.1 us
  Pallas kernels: 0 us -> 32.8 us
  matrix products: 31.4 us -> 0 us
  starting transfers between devices: 0.38 us -> 26 us
  local copies, waits for them, and re-layouts: 28.7 us -> 7.86 us
  between operations: 14.7 us -> 1.57 us
  other arithmetic: 9.6 us -> 0 us
  blocking collectives: 6.22 us -> 0 us
    psum x1 -> x0, waiting for transfers between devices: 110 us -> none  [body(): d_proj = lax.psum(proj_term, ('batch', 'seq', 'pool'))]
    all_gather x3 -> x0, waiting for transfers between devices: 83.2 us -> none  [the longest x1 42.9 us: body(): key_block = lax.all_gather(keys, 'seq', axis=0, tiled=True)]
    reduce_scatter x1 -> x0, waiting for transfers between devices: 76.1 us -> none  [body(): lax.psum_scatter(blocks, ('seq', 'pool'), scatter_dimension=0, tiled=True)]
    pallas_call x0 -> x16, Pallas kernels: none -> 32.8 us  [call(): pl.pallas_call(kernel, out_shape=list(outs) if many else outs, in_specs=i...]
    dot_general x15 -> x0, matrix products: 31.4 us -> none  [the longest x8 14.3 us: one_head(): return jnp.dot(weights, value_head, preferred_element_type=jnp.float32)]
    ppermute x0 -> x22, starting transfers between devices: none -> 26 us  [the longest x18 16 us: swap(): return lax.ppermute(x, axis, [(i, i ^ r) for i in range(count)])]
    ppermute x0 -> x22, waiting for transfers between devices: none -> 24.1 us  [the longest x18 23.6 us: swap(): return lax.ppermute(x, axis, [(i, i ^ r) for i in range(count)])]
    transpose x3 -> x0, local copies, waits for them, and re-layouts: 13.3 us -> none  [the longest x2 6.68 us: head_split(): block.reshape(block.shape[0], HEADS, block.shape[1] // HEADS)]
  transfers between devices with their start and end apart: 5 -> 22, of which waited for: 5 -> 9; matrix products, arithmetic and copies ran while one was open for 13% -> 0% of each run, Pallas kernels for 0% -> 28%
where the time goes in v1:
time: 92.7 us; the launch traced here: 92.3 us
  Pallas kernels  32.8 us (35%)
  starting transfers between devices  26 us (28%)
  waiting for transfers between devices  24.1 us (26%)
  local copies, waits for them, and re-layouts  7.86 us (8%)
  between operations  1.57 us (2%)
    pallas_call x16, Pallas kernels, call(): pl.pallas_call(kernel, out_shape=list(outs) if many else outs, in_specs=i...  32.8 us
    ppermute x18, waiting for transfers between devices, swap(): return lax.ppermute(x, axis, [(i, i ^ r) for i in range(count)])  23.6 us
    ppermute x18, starting transfers between devices, swap(): return lax.ppermute(x, axis, [(i, i ^ r) for i in range(count)])  16 us
    unnamed x26, local copies, waits for them, and re-layouts  7.77 us
    ppermute x1, starting transfers between devices, body(): block = lax.ppermute(own, 'seq', up)  4.96 us
    ppermute x1, starting transfers between devices, body(): following = lax.ppermute(block, 'seq', up)  3.48 us
  transfers between devices with their start and end apart: 22, of which 9 were waited for; matrix products, arithmetic and copies ran while one was open for 0% of the time, Pallas kernels for 28%

profile of v1, /device:TPU:0, one launch (start us, length us, event | category | flops | bytes accessed | tf_op | source)
XLA Modules:
  0.0 92.3 jit_solution(16771188060734975533)
XLA Ops:
  0.6 5.0 %collective-permute-start = (bf16[256,1024]{1,0:T(8,128)(2,1)}, bf16[256,1024]{1,0:T(8,128)(2,1)S(1)}, u32[]{:S(2)}, u32[]{:S(2)}) collective-permute-start(bf16[256,1024]{1,0:T(8,128)(2,1)} %bitcast.17), channel_id=1, source_target_pairs={{0,4},{4,8},{1,5},{5,9},{2,6},{6,10},{3,7},{7,11},{16,20},{20,24},... | collective-permute-start | bytes 1572872 | tf_op jit(solution)/shard_map/ppermute | solution.py:373
  5.6 0.7 collective-permute-start.1
  7.0 1.0 %copy-done.3 = bf16[1,1024,256]{2,1,0:T(8,128)(2,1)S(1)} copy-done((bf16[1,1024,256]{2,1,0:T(8,128)(2,1)S(1)}, bf16[1,1024,256]{2,1,0:T(8,128)(2,1)}, u32[]{:S(2)}) %copy-start.3) | copy-done | bytes 524312
  8.0 0.9 copy-done.7
  10.7 3.4 %copy-done = bf16[1024,4096]{1,0:T(8,128)(2,1)S(1)} copy-done((bf16[1024,4096]{1,0:T(8,128)(2,1)S(1)}, bf16[1024,4096]{1,0:T(8,128)(2,1)}, u32[]{:S(2)}) %copy-start) | copy-done | bytes 8388632
  14.1 1.0 %copy-done.5 = bf16[1,256,1024]{2,1,0:T(8,128)(2,1)S(1)} copy-done((bf16[1,256,1024]{2,1,0:T(8,128)(2,1)S(1)}, bf16[1,256,1024]{2,1,0:T(8,128)(2,1)}, u32[]{:S(2)}) %copy-start.5) | copy-done | bytes 524312
  15.2 4.2 %own_block.1 = (bf16[256,1024]{1,0:T(8,128)(2,1)S(1)}, bf16[256,1024]{1,0:T(8,128)(2,1)S(1)}, bf16[256,1024]{1,0:T(8,128)(2,1)S(1)}, bf16[256,1024]{1,0:T(8,128)(2,1)S(1)}, f32[256,1024]{1,0:T(8,128)S(1)}) custom-call(s32[7]{0:T(128)S(1)} %stack.27.info_ref, bf16[256,1024]{1,0:T(8,128)(2,1)S(1)} %bitcast.19, bf16[1024,4096]{1,0:T(8,128)(2,1)S(1)} %copy-done), custom_call_target="tpu_custom_call" | custom-call | flops 2415919104 | bytes 8388608 | tf_op jit(solution)/shard_map/own_block/pallas_call | solution.py:326
  19.4 1.6 %collective-permute-start.3 = (bf16[1056,256]{1,0:T(8,128)(2,1)S(1)}, bf16[1056,256]{1,0:T(8,128)(2,1)S(1)}, u32[]{:S(2)}, u32[]{:S(2)}) collective-permute-start(bf16[1056,256]{1,0:T(8,128)(2,1)S(1)} %get-tuple-element.84.rest_0_), channel_id=1, source_target_pairs={{0,2},{1,3},{2,0},{3,1},{4,6},{5,7},{6,4},{7,5},{8,10},{9,11},{10,... | collective-permute-start | bytes 1622024 | tf_op jit(solution)/shard_map/ppermute | solution.py:339
  21.0 3.5 %collective-permute-start.2 = (bf16[256,1024]{1,0:T(8,128)(2,1)S(1)}, bf16[256,1024]{1,0:T(8,128)(2,1)S(1)}, u32[]{:S(2)}, u32[]{:S(2)}) collective-permute-start(bf16[256,1024]{1,0:T(8,128)(2,1)S(1)} %collective-permute-done.x_ref), channel_id=1, source_target_pairs={{0,4},{4,8},{1,5},{5,9},{2,6},{6,10},{3,7},{7,11},{16,20},{20,24},... | collective-permute-start | bytes 1572872 | tf_op jit(solution)/shard_map/ppermute | solution.py:398
  24.5 4.8 %guest_block.1 = (bf16[256,1024]{1,0:T(8,128)(2,1)S(1)}, bf16[256,1024]{1,0:T(8,128)(2,1)S(1)}, f32[256,1024]{1,0:T(8,128)S(1)}) custom-call(s32[7]{0:T(128)S(1)} %stack.27.info_ref, bf16[256,1024]{1,0:T(8,128)(2,1)S(1)} %collective-permute-done.1.x_ref.refs_7_, bf16[1024,4096]{1,0:T(8,128)(2,1)S(1)} %copy-done.1, ...), custom_call_target="tpu_custom_call" | custom-call | tf_op jit(solution)/shard_map/guest_block/pallas_call | solution.py:326
  29.3 3.6 %earlier_block_1.1 = (f32[256,1024]{1,0:T(8,128)S(1)}, f32[256,1024]{1,0:T(8,128)S(1)}) custom-call(s32[7]{0:T(128)S(1)} %stack.27.info_ref, bf16[256,1024]{1,0:T(8,128)(2,1)S(1)} %collective-permute-done.x_ref, bf16[1024,4096]{1,0:T(8,128)(2,1)S(1)} %copy-done.1, bf16[256,1024]{1,0:T(8,128)(2,1)S(1)} %get-tuple-element.64.refs_0_, ...), custom_call_target="tpu_custom_call" | custom-call | tf_op jit(solution)/shard_map/earlier_block_1/pallas_call | solution.py:326
  33.7 0.8 collective-permute-start.4
  35.0 5.8 %last_block.1 = (bf16[512,1024]{1,0:T(8,128)(2,1)S(1)}, f32[512,256]{1,0:T(8,128)S(1)}, bf16[512,256]{1,0:T(8,128)(2,1)S(1)}) custom-call(s32[7]{0:T(128)S(1)} %stack.27.info_ref, bf16[256,1024]{1,0:T(8,128)(2,1)S(1)} %collective-permute-done.2.x_ref, bf16[1024,4096]{1,0:T(8,128)(2,1)S(1)} %copy-done.1, bf16[256,1024]{1,0:T(8,128)(2,1)S(1)} %get-tuple-element.64.refs_0_, ...), custom_call_target="tpu_custom_call" | custom-call | flops 2952790016 | bytes 6291456 | tf_op jit(solution)/shard_map/last_block/pallas_call | solution.py:326
  40.9 4.8 %head.1 = (f32[1,256]{1,0:T(1,128)S(1)}, f32[1,256]{1,0:T(1,128)S(1)}, bf16[528,256]{1,0:T(8,128)(2,1)S(1)}, f32[512,256]{1,0:T(8,128)S(1)}, bf16[512,256]{1,0:T(8,128)(2,1)S(1)}) custom-call(s32[7]{0:T(128)S(1)} %stack.27.info_ref, bf16[512,256]{1,0:T(8,128)(2,1)S(1)} %get-tuple-element.80.hat_ref, f32[512,256]{1,0:T(8,128)S(1)} %get-tuple-element.81.out_ref, ...), custom_call_target="tpu_custom_call" | custom-call | flops 2147483648 | bytes 2097152 | tf_op jit(solution)/shard_map/head/pallas_call | solution.py:326
  45.7 1.1 %collective-permute-start.8 = (bf16[528,256]{1,0:T(8,128)(2,1)S(1)}, bf16[528,256]{1,0:T(8,128)(2,1)S(1)}, u32[]{:S(2)}, u32[]{:S(2)}) collective-permute-start(bf16[528,256]{1,0:T(8,128)(2,1)S(1)} %get-tuple-element.96.rest_0_), channel_id=1, source_target_pairs={{0,2},{1,3},{2,0},{3,1},{4,6},{5,7},{6,4},{7,5},{8,10},{9,11},{10,... | collective-permute-start | bytes 811016 | tf_op jit(solution)/shard_map/ppermute | solution.py:339
  46.9 1.5 %collective-permute-done.7.got_ref = bf16[512,256]{1,0:T(8,128)(2,1)S(1)} collective-permute-done((bf16[512,256]{1,0:T(8,128)(2,1)S(1)}, bf16[512,256]{1,0:T(8,128)(2,1)S(1)}, u32[]{:S(2)}, u32[]{:S(2)}) %collective-permute-start.7) | collective-permute-done | bytes 262176 | tf_op jit(solution)/shard_map/ppermute | solution.py:339
  49.0 4.7 %collective-permute-done.8.rest_1_ = bf16[528,256]{1,0:T(8,128)(2,1)S(1)} collective-permute-done((bf16[528,256]{1,0:T(8,128)(2,1)S(1)}, bf16[528,256]{1,0:T(8,128)(2,1)S(1)}, u32[]{:S(2)}, u32[]{:S(2)}) %collective-permute-start.8) | collective-permute-done | bytes 270368 | tf_op jit(solution)/shard_map/ppermute | solution.py:339
  54.2 1.5 %collective-permute-start.10 = (bf16[128,256]{1,0:T(8,128)(2,1)S(1)}, bf16[128,256]{1,0:T(8,128)(2,1)S(1)}, u32[]{:S(2)}, u32[]{:S(2)}) collective-permute-start(bf16[128,256]{1,0:T(8,128)(2,1)S(1)} %get-tuple-element.93), channel_id=1, source_target_pairs={{0,16},{1,17},{2,18},{3,19},{16,0},{17,1},{18,2},{19,3},{4,20},{5,... | collective-permute-start | bytes 196616 | tf_op jit(solution)/shard_map/ppermute | solution.py:339
  55.7 1.5 %collective-permute-start.11 = (bf16[128,256]{1,0:T(8,128)(2,1)S(1)}, bf16[128,256]{1,0:T(8,128)(2,1)S(1)}, u32[]{:S(2)}, u32[]{:S(2)}) collective-permute-start(bf16[128,256]{1,0:T(8,128)(2,1)S(1)} %get-tuple-element.94), channel_id=1, source_target_pairs={{0,18},{1,19},{2,16},{3,17},{16,2},{17,3},{18,0},{19,1},{4,22},{5,... | collective-permute-start | bytes 196616 | tf_op jit(solution)/shard_map/ppermute | solution.py:339
  57.8 4.5 %neg_grad.1 = (f32[128,1024]{1,0:T(8,128)S(1)}, bf16[144,1024]{1,0:T(8,128)(2,1)S(1)}) custom-call(s32[7]{0:T(128)S(1)} %stack.27.info_ref, bf16[1024,256]{1,0:T(8,128)(2,1)S(1)} %bitcast.16, s32[1,1024]{1,0:T(1,128)S(1)} %copy-done.10, f32[1,256]{1,0:T(1,128)S(1)} %get-tuple-element.95.loss_ref, bf16[528,256]{1,0:T(8,128)(2,1)S(1)} %get-tuple-element.96.rest_0_, ...), custom_call_target="tpu_custom_call" | custom-call | tf_op jit(solution)/shard_map/neg_grad/pallas_call | solution.py:326
  62.3 1.6 %collective-permute-start.14 = (bf16[144,1024]{1,0:T(8,128)(2,1)S(1)}, bf16[144,1024]{1,0:T(8,128)(2,1)S(1)}, u32[]{:S(2)}, u32[]{:S(2)}) collective-permute-start(bf16[144,1024]{1,0:T(8,128)(2,1)S(1)} %get-tuple-element.105), channel_id=1, source_target_pairs={{0,4},{4,0},{8,12},{12,8},{1,5},{5,1},{9,13},{13,9},{2,6},{6,2},{1... | collective-permute-start | bytes 884744 | tf_op jit(solution)/shard_map/ppermute | solution.py:339
  64.4 7.5 %collective-permute-done.15.refs_1_ = bf16[128,256]{1,0:T(8,128)(2,1)S(1)} collective-permute-done((bf16[128,256]{1,0:T(8,128)(2,1)S(1)}, bf16[128,256]{1,0:T(8,128)(2,1)S(1)}, u32[]{:S(2)}, u32[]{:S(2)}) %collective-permute-start.15) | collective-permute-done | bytes 65568 | tf_op jit(solution)/shard_map/ppermute | solution.py:339
  72.0 2.6 %collective-permute-start.16 = (bf16[128,256]{1,0:T(8,128)(2,1)S(1)}, bf16[128,256]{1,0:T(8,128)(2,1)S(1)}, u32[]{:S(2)}, u32[]{:S(2)}) collective-permute-start(bf16[128,256]{1,0:T(8,128)(2,1)S(1)} %seq_sum_1.1.refs_0_), channel_id=1, source_target_pairs={{0,8},{4,12},{8,0},{12,4},{1,9},{5,13},{9,1},{13,5},{2,10},{6,14},... | collective-permute-start | bytes 196616 | tf_op jit(solution)/shard_map/ppermute | solution.py:339
  75.1 4.9 %collective-permute-done.16.refs_1_ = bf16[128,256]{1,0:T(8,128)(2,1)S(1)} collective-permute-done((bf16[128,256]{1,0:T(8,128)(2,1)S(1)}, bf16[128,256]{1,0:T(8,128)(2,1)S(1)}, u32[]{:S(2)}, u32[]{:S(2)}) %collective-permute-start.16) | collective-permute-done | bytes 65568 | tf_op jit(solution)/shard_map/ppermute | solution.py:339
  80.0 1.5 %collective-permute-start.17 = (bf16[128,256]{1,0:T(8,128)(2,1)S(1)}, bf16[128,256]{1,0:T(8,128)(2,1)S(1)}, u32[]{:S(2)}, u32[]{:S(2)}) collective-permute-start(bf16[128,256]{1,0:T(8,128)(2,1)S(1)} %seq_sum_2.1.refs_0_), channel_id=1, source_target_pairs={{0,2},{1,3},{2,0},{3,1},{16,18},{17,19},{18,16},{19,17},{4,6},{5,7... | collective-permute-start | bytes 196616 | tf_op jit(solution)/shard_map/ppermute | solution.py:339
  81.5 1.5 %collective-permute-start.18 = (bf16[128,256]{1,0:T(8,128)(2,1)S(1)}, bf16[128,256]{1,0:T(8,128)(2,1)S(1)}, u32[]{:S(2)}, u32[]{:S(2)}) collective-permute-start(bf16[128,256]{1,0:T(8,128)(2,1)S(1)} %seq_sum_2.1.refs_0_), channel_id=1, source_target_pairs={{0,16},{1,17},{2,18},{3,19},{16,0},{17,1},{18,2},{19,3},{4,20},{5,... | collective-permute-start | bytes 196616 | tf_op jit(solution)/shard_map/ppermute | solution.py:339
  83.6 0.8 collective-permute-done.17.refs_1_
  84.3 1.4 %collective-permute-done.18.refs_2_ = bf16[128,256]{1,0:T(8,128)(2,1)S(1)} collective-permute-done((bf16[128,256]{1,0:T(8,128)(2,1)S(1)}, bf16[128,256]{1,0:T(8,128)(2,1)S(1)}, u32[]{:S(2)}, u32[]{:S(2)}) %collective-permute-start.18) | collective-permute-done | bytes 65568 | tf_op jit(solution)/shard_map/ppermute | solution.py:339
  85.8 2.4 %collective-permute-done.19.refs_3_ = bf16[128,256]{1,0:T(8,128)(2,1)S(1)} collective-permute-done((bf16[128,256]{1,0:T(8,128)(2,1)S(1)}, bf16[128,256]{1,0:T(8,128)(2,1)S(1)}, u32[]{:S(2)}, u32[]{:S(2)}) %collective-permute-start.19) | collective-permute-done | bytes 65568 | tf_op jit(solution)/shard_map/ppermute | solution.py:339
  88.8 1.1 %loss.1 = f32[1,256]{1,0:T(1,128)} custom-call(s32[7]{0:T(128)S(1)} %stack.27.info_ref, f32[1,256]{1,0:T(1,128)S(1)} %get-tuple-element.86.loss_ref, bf16[144,1024]{1,0:T(8,128)(2,1)S(1)} %collective-permute-done.14.got_ref), custom_call_target="tpu_custom_call" | custom-call | tf_op jit(solution)/shard_map/loss/pallas_call | solution.py:326
  89.9 0.7 neg_sum.1
  90.7 1.6 %lay_whole.1 = f32[1024,256]{1,0:T(8,128)} custom-call(s32[7]{0:T(128)S(1)} %stack.27.info_ref, bf16[512,256]{1,0:T(8,128)(2,1)S(1)} %lay_half.1.refs_0_, bf16[512,256]{1,0:T(8,128)(2,1)S(1)} %collective-permute-done.21.refs_1_), custom_call_target="tpu_custom_call" | custom-call | tf_op jit(solution)/shard_map/lay_whole/pallas_call | solution.py:326
  (55 shorter events, 7.0 us)
Async XLA Ops:
  0.6 20.3 %collective-permute-start = (bf16[256,1024]{1,0:T(8,128)(2,1)}, bf16[256,1024]{1,0:T(8,128)(2,1)S(1)}, u32[]{:S(2)}, u32[]{:S(2)}) collective-permute-start(bf16[256,1024]{1,0:T(8,128)(2,1)} %bitcast.17), channel_id=1, source_target_pairs={{0,4},{4,8},{1,5},{5,9},{2,6},{6,10},{3,7},{7,11},{16,20},{20,24},... | collective-permute-start | bytes 1572872 | tf_op jit(solution)/shard_map/ppermute | solution.py:373
  5.6 15.4 %collective-permute-start.1 = (bf16[256,1024]{1,0:T(8,128)(2,1)}, bf16[256,1024]{1,0:T(8,128)(2,1)S(1)}, u32[]{:S(2)}, u32[]{:S(2)}) collective-permute-start(bf16[256,1024]{1,0:T(8,128)(2,1)} %bitcast.18), channel_id=1, source_target_pairs={{12,8},{13,9},{14,10},{15,11},{28,24},{29,25},{30,26},{31,27}} | collective-permute-start | bytes 1572872 | tf_op jit(solution)/shard_map/ppermute | solution.py:374
  7.0 1.0 %copy-start.3 = (bf16[1,1024,256]{2,1,0:T(8,128)(2,1)S(1)}, bf16[1,1024,256]{2,1,0:T(8,128)(2,1)}, u32[]{:S(2)}) copy-start(bf16[1,1024,256]{2,1,0:T(8,128)(2,1)} %param.16) | copy-start | bytes 1572868
  10.7 3.4 %copy-start = (bf16[1024,4096]{1,0:T(8,128)(2,1)S(1)}, bf16[1024,4096]{1,0:T(8,128)(2,1)}, u32[]{:S(2)}) copy-start(bf16[1024,4096]{1,0:T(8,128)(2,1)} %w_ref.7) | copy-start | bytes 25165828
  14.1 1.0 %copy-start.5 = (bf16[1,256,1024]{2,1,0:T(8,128)(2,1)S(1)}, bf16[1,256,1024]{2,1,0:T(8,128)(2,1)}, u32[]{:S(2)}) copy-start(bf16[1,256,1024]{2,1,0:T(8,128)(2,1)} %param.9) | copy-start | bytes 1572868
  15.2 9.3 %copy-start.1 = (bf16[1024,4096]{1,0:T(8,128)(2,1)S(1)}, bf16[1024,4096]{1,0:T(8,128)(2,1)}, u32[]{:S(2)}) copy-start(bf16[1024,4096]{1,0:T(8,128)(2,1)} %w_ref.7) | copy-start | bytes 25165828
  19.4 13.8 %collective-permute-start.3 = (bf16[1056,256]{1,0:T(8,128)(2,1)S(1)}, bf16[1056,256]{1,0:T(8,128)(2,1)S(1)}, u32[]{:S(2)}, u32[]{:S(2)}) collective-permute-start(bf16[1056,256]{1,0:T(8,128)(2,1)S(1)} %get-tuple-element.84.rest_0_), channel_id=1, source_target_pairs={{0,2},{1,3},{2,0},{3,1},{4,6},{5,7},{6,4},{7,5},{8,10},{9,11},{10,... | collective-permute-start | bytes 1622024 | tf_op jit(solution)/shard_map/ppermute | solution.py:339
  21.0 14.1 %collective-permute-start.2 = (bf16[256,1024]{1,0:T(8,128)(2,1)S(1)}, bf16[256,1024]{1,0:T(8,128)(2,1)S(1)}, u32[]{:S(2)}, u32[]{:S(2)}) collective-permute-start(bf16[256,1024]{1,0:T(8,128)(2,1)S(1)} %collective-permute-done.x_ref), channel_id=1, source_target_pairs={{0,4},{4,8},{1,5},{5,9},{2,6},{6,10},{3,7},{7,11},{16,20},{20,24},... | collective-permute-start | bytes 1572872 | tf_op jit(solution)/shard_map/ppermute | solution.py:398
  29.3 5.7 %copy-start.2 = (bf16[1024,1024]{1,0:T(8,128)(2,1)S(1)}, bf16[1024,1024]{1,0:T(8,128)(2,1)}, u32[]{:S(2)}) copy-start(bf16[1024,1024]{1,0:T(8,128)(2,1)} %refs_8_.1) | copy-start | bytes 6291460
  29.3 5.7 %copy-start.6 = (bf16[1024,256]{1,0:T(8,128)(2,1)S(1)}, bf16[1024,256]{1,0:T(8,128)(2,1)}, u32[]{:S(2)}) copy-start(bf16[1024,256]{1,0:T(8,128)(2,1)} %refs_9_.1) | copy-start | bytes 1572868
  33.2 7.7 %collective-permute-start.5 = (bf16[1056,256]{1,0:T(8,128)(2,1)S(1)}, bf16[1056,256]{1,0:T(8,128)(2,1)S(1)}, u32[]{:S(2)}, u32[]{:S(2)}) collective-permute-start(bf16[1056,256]{1,0:T(8,128)(2,1)S(1)} %get-tuple-element.84.rest_0_), channel_id=1, source_target_pairs={{0,1},{1,0},{2,3},{3,2},{4,5},{5,4},{6,7},{7,6},{8,9},{9,8},{10,11... | collective-permute-start | bytes 1622024 | tf_op jit(solution)/shard_map/ppermute | solution.py:339
  33.2 7.7 %collective-permute-start.6 = (bf16[1056,256]{1,0:T(8,128)(2,1)S(1)}, bf16[1056,256]{1,0:T(8,128)(2,1)S(1)}, u32[]{:S(2)}, u32[]{:S(2)}) collective-permute-start(bf16[1056,256]{1,0:T(8,128)(2,1)S(1)} %collective-permute-done.3.rest_1_), channel_id=1, source_target_pairs={{0,1},{1,0},{2,3},{3,2},{4,5},{5,4},{6,7},{7,6},{8,9},{9,8},{10,11... | collective-permute-start | bytes 1622024 | tf_op jit(solution)/shard_map/ppermute | solution.py:339
  33.7 7.1 %collective-permute-start.4 = (bf16[272,256]{1,0:T(8,128)(2,1)S(1)}, bf16[272,256]{1,0:T(8,128)(2,1)S(1)}, u32[]{:S(2)}, u32[]{:S(2)}) collective-permute-start(bf16[272,256]{1,0:T(8,128)(2,1)S(1)} %get-tuple-element.83), channel_id=1, source_target_pairs={{12,8},{13,9},{14,10},{15,11},{28,24},{29,25},{30,26},{31,27}} | collective-permute-start | bytes 417800 | tf_op jit(solution)/shard_map/ppermute | solution.py:411
  35.0 5.8 %copy-start.8 = (bf16[1,256,256]{2,1,0:T(8,128)(2,1)S(1)}, bf16[1,256,256]{2,1,0:T(8,128)(2,1)}, u32[]{:S(2)}) copy-start(bf16[1,256,256]{2,1,0:T(8,128)(2,1)} %param.13) | copy-start | bytes 393220
  35.0 5.8 %copy-start.12 = (s32[1,256]{1,0:T(1,128)S(1)}, s32[1,256]{1,0:T(1,128)}, u32[]{:S(2)}) copy-start(s32[1,256]{1,0:T(1,128)} %ids_ref.3) | copy-start | bytes 3076
  40.8 16.9 %copy-start.4 = (bf16[1,1024,256]{2,1,0:T(8,128)(2,1)S(1)}, bf16[1,1024,256]{2,1,0:T(8,128)(2,1)}, u32[]{:S(2)}) copy-start(bf16[1,1024,256]{2,1,0:T(8,128)(2,1)} %param.16) | copy-start | bytes 1572868
  40.8 16.9 %copy-start.10 = (s32[1,1024]{1,0:T(1,128)S(1)}, s32[1,1024]{1,0:T(1,128)}, u32[]{:S(2)}) copy-start(s32[1,1024]{1,0:T(1,128)} %neg_id_ref.1) | copy-start | bytes 12292
  45.7 8.0 %collective-permute-start.8 = (bf16[528,256]{1,0:T(8,128)(2,1)S(1)}, bf16[528,256]{1,0:T(8,128)(2,1)S(1)}, u32[]{:S(2)}, u32[]{:S(2)}) collective-permute-start(bf16[528,256]{1,0:T(8,128)(2,1)S(1)} %get-tuple-element.96.rest_0_), channel_id=1, source_target_pairs={{0,2},{1,3},{2,0},{3,1},{4,6},{5,7},{6,4},{7,5},{8,10},{9,11},{10,... | collective-permute-start | bytes 811016 | tf_op jit(solution)/shard_map/ppermute | solution.py:339
  46.9 1.5 %collective-permute-start.7 = (bf16[512,256]{1,0:T(8,128)(2,1)S(1)}, bf16[512,256]{1,0:T(8,128)(2,1)S(1)}, u32[]{:S(2)}, u32[]{:S(2)}) collective-permute-start(bf16[512,256]{1,0:T(8,128)(2,1)S(1)} %get-tuple-element.88), channel_id=1, source_target_pairs={{0,1},{1,0},{2,3},{3,2},{16,17},{17,16},{18,19},{19,18},{4,5},{5,4... | collective-permute-start | bytes 786440 | tf_op jit(solution)/shard_map/ppermute | solution.py:339
  53.7 4.0 %collective-permute-start.12 = (bf16[528,256]{1,0:T(8,128)(2,1)S(1)}, bf16[528,256]{1,0:T(8,128)(2,1)S(1)}, u32[]{:S(2)}, u32[]{:S(2)}) collective-permute-start(bf16[528,256]{1,0:T(8,128)(2,1)S(1)} %get-tuple-element.96.rest_0_), channel_id=1, source_target_pairs={{0,1},{1,0},{2,3},{3,2},{4,5},{5,4},{6,7},{7,6},{8,9},{9,8},{10,11... | collective-permute-start | bytes 811016 | tf_op jit(solution)/shard_map/ppermute | solution.py:339
  53.7 4.0 %collective-permute-start.13 = (bf16[528,256]{1,0:T(8,128)(2,1)S(1)}, bf16[528,256]{1,0:T(8,128)(2,1)S(1)}, u32[]{:S(2)}, u32[]{:S(2)}) collective-permute-start(bf16[528,256]{1,0:T(8,128)(2,1)S(1)} %collective-permute-done.8.rest_1_), channel_id=1, source_target_pairs={{0,1},{1,0},{2,3},{3,2},{4,5},{5,4},{6,7},{7,6},{8,9},{9,8},{10,11... | collective-permute-start | bytes 811016 | tf_op jit(solution)/shard_map/ppermute | solution.py:339
  54.2 8.0 %collective-permute-start.10 = (bf16[128,256]{1,0:T(8,128)(2,1)S(1)}, bf16[128,256]{1,0:T(8,128)(2,1)S(1)}, u32[]{:S(2)}, u32[]{:S(2)}) collective-permute-start(bf16[128,256]{1,0:T(8,128)(2,1)S(1)} %get-tuple-element.93), channel_id=1, source_target_pairs={{0,16},{1,17},{2,18},{3,19},{16,0},{17,1},{18,2},{19,3},{4,20},{5,... | collective-permute-start | bytes 196616 | tf_op jit(solution)/shard_map/ppermute | solution.py:339
  55.7 6.5 %collective-permute-start.11 = (bf16[128,256]{1,0:T(8,128)(2,1)S(1)}, bf16[128,256]{1,0:T(8,128)(2,1)S(1)}, u32[]{:S(2)}, u32[]{:S(2)}) collective-permute-start(bf16[128,256]{1,0:T(8,128)(2,1)S(1)} %get-tuple-element.94), channel_id=1, source_target_pairs={{0,18},{1,19},{2,16},{3,17},{16,2},{17,3},{18,0},{19,1},{4,22},{5,... | collective-permute-start | bytes 196616 | tf_op jit(solution)/shard_map/ppermute | solution.py:339
  57.2 5.0 %collective-permute-start.9 = (bf16[128,256]{1,0:T(8,128)(2,1)S(1)}, bf16[128,256]{1,0:T(8,128)(2,1)S(1)}, u32[]{:S(2)}, u32[]{:S(2)}) collective-permute-start(bf16[128,256]{1,0:T(8,128)(2,1)S(1)} %get-tuple-element.92), channel_id=1, source_target_pairs={{0,2},{1,3},{2,0},{3,1},{16,18},{17,19},{18,16},{19,17},{4,6},{5,7... | collective-permute-start | bytes 196616 | tf_op jit(solution)/shard_map/ppermute | solution.py:339
  62.3 12.3 %collective-permute-start.14 = (bf16[144,1024]{1,0:T(8,128)(2,1)S(1)}, bf16[144,1024]{1,0:T(8,128)(2,1)S(1)}, u32[]{:S(2)}, u32[]{:S(2)}) collective-permute-start(bf16[144,1024]{1,0:T(8,128)(2,1)S(1)} %get-tuple-element.105), channel_id=1, source_target_pairs={{0,4},{4,0},{8,12},{12,8},{1,5},{5,1},{9,13},{13,9},{2,6},{6,2},{1... | collective-permute-start | bytes 884744 | tf_op jit(solution)/shard_map/ppermute | solution.py:339
  63.9 8.0 %collective-permute-start.15 = (bf16[128,256]{1,0:T(8,128)(2,1)S(1)}, bf16[128,256]{1,0:T(8,128)(2,1)S(1)}, u32[]{:S(2)}, u32[]{:S(2)}) collective-permute-start(bf16[128,256]{1,0:T(8,128)(2,1)S(1)} %plane_sum.1.refs_0_), channel_id=1, source_target_pairs={{0,4},{4,0},{8,12},{12,8},{1,5},{5,1},{9,13},{13,9},{2,6},{6,2},{1... | collective-permute-start | bytes 196616 | tf_op jit(solution)/shard_map/ppermute | solution.py:339
  72.0 8.0 %collective-permute-start.16 = (bf16[128,256]{1,0:T(8,128)(2,1)S(1)}, bf16[128,256]{1,0:T(8,128)(2,1)S(1)}, u32[]{:S(2)}, u32[]{:S(2)}) collective-permute-start(bf16[128,256]{1,0:T(8,128)(2,1)S(1)} %seq_sum_1.1.refs_0_), channel_id=1, source_target_pairs={{0,8},{4,12},{8,0},{12,4},{1,9},{5,13},{9,1},{13,5},{2,10},{6,14},... | collective-permute-start | bytes 196616 | tf_op jit(solution)/shard_map/ppermute | solution.py:339
  74.6 13.6 %collective-permute-start.20 = (bf16[64,1024]{1,0:T(8,128)(2,1)S(1)}, bf16[64,1024]{1,0:T(8,128)(2,1)S(1)}, u32[]{:S(2)}, u32[]{:S(2)}) collective-permute-start(bf16[64,1024]{1,0:T(8,128)(2,1)S(1)} %get-tuple-element.109), channel_id=1, source_target_pairs={{0,8},{4,12},{8,0},{12,4},{1,9},{5,13},{9,1},{13,5},{2,10},{6,14},... | collective-permute-start | bytes 393224 | tf_op jit(solution)/shard_map/ppermute | solution.py:339
  80.0 4.3 %collective-permute-start.17 = (bf16[128,256]{1,0:T(8,128)(2,1)S(1)}, bf16[128,256]{1,0:T(8,128)(2,1)S(1)}, u32[]{:S(2)}, u32[]{:S(2)}) collective-permute-start(bf16[128,256]{1,0:T(8,128)(2,1)S(1)} %seq_sum_2.1.refs_0_), channel_id=1, source_target_pairs={{0,2},{1,3},{2,0},{3,1},{16,18},{17,19},{18,16},{19,17},{4,6},{5,7... | collective-permute-start | bytes 196616 | tf_op jit(solution)/shard_map/ppermute | solution.py:339
  81.5 4.3 %collective-permute-start.18 = (bf16[128,256]{1,0:T(8,128)(2,1)S(1)}, bf16[128,256]{1,0:T(8,128)(2,1)S(1)}, u32[]{:S(2)}, u32[]{:S(2)}) collective-permute-start(bf16[128,256]{1,0:T(8,128)(2,1)S(1)} %seq_sum_2.1.refs_0_), channel_id=1, source_target_pairs={{0,16},{1,17},{2,18},{3,19},{16,0},{17,1},{18,2},{19,3},{4,20},{5,... | collective-permute-start | bytes 196616 | tf_op jit(solution)/shard_map/ppermute | solution.py:339
  83.0 5.2 %collective-permute-start.19 = (bf16[128,256]{1,0:T(8,128)(2,1)S(1)}, bf16[128,256]{1,0:T(8,128)(2,1)S(1)}, u32[]{:S(2)}, u32[]{:S(2)}) collective-permute-start(bf16[128,256]{1,0:T(8,128)(2,1)S(1)} %seq_sum_2.1.refs_0_), channel_id=1, source_target_pairs={{0,18},{1,19},{2,16},{3,17},{16,2},{17,3},{18,0},{19,1},{4,22},{5,... | collective-permute-start | bytes 196616 | tf_op jit(solution)/shard_map/ppermute | solution.py:339
  88.7 1.9 %collective-permute-start.21 = (bf16[512,256]{1,0:T(8,128)(2,1)S(1)}, bf16[512,256]{1,0:T(8,128)(2,1)S(1)}, u32[]{:S(2)}, u32[]{:S(2)}) collective-permute-start(bf16[512,256]{1,0:T(8,128)(2,1)S(1)} %lay_half.1.refs_0_), channel_id=1, source_target_pairs={{0,1},{1,0},{2,3},{3,2},{16,17},{17,16},{18,19},{19,18},{4,5},{5,4... | collective-permute-start | bytes 786440 | tf_op jit(solution)/shard_map/ppermute | solution.py:339
  (3 other events, 2.3 us)

commit v2 on v1

--- a/solution.py
+++ b/solution.py
@@ -89,50 +89,63 @@
     return lax.broadcasted_iota(jnp.int32, (rows, rows), 0) >= lax.broadcasted_iota(jnp.int32, (rows, rows), 1)
 
 
-def own_kernel(info_ref, x_ref, w_ref, gate_ref, q_ref, k_ref, v_ref, acc_ref):
-    rows = x_ref.shape[0]
+def fetch(pairs, sems):
+    copies = [pltpu.make_async_copy(src, dst, sems.at[i]) for i, (src, dst) in enumerate(pairs)]
+    for copy in copies:
+        copy.start()
+    return copies
+
+
+def own_kernel(info_ref, x_hbm, w_hbm, gate_ref, q_ref, k_ref, v_ref, acc_ref, x_ref, w_ref, sems):
+    rows, width = x_ref.shape
+    parts = [2, 3, 1, 0]
+    pairs = [(w_hbm.at[:, i * width : (i + 1) * width], w_ref.at[i]) for i in parts]
+    copies = fetch([(x_hbm, x_ref)] + pairs, sems)
+    copies[0].wait()
     keep = kept_rows(info_ref[0], rows, info_ref[1])
     normed = row_norm(x_ref[...].astype(F32), keep).astype(BF16)
-    gate_ref[...] = project(normed, w_ref, 0)
-    q_ref[...] = project(normed, w_ref, 2)
-    keys, values = project(normed, w_ref, 3), project(normed, w_ref, 1)
-    k_ref[...] = keys
-    v_ref[...] = values
-    attend(q_ref, keys, values, acc_ref, None, causal_mask(rows))
-
-
-def guest_kernel(info_ref, x_ref, w_ref, k_ref, v_ref, gate_ref, q_ref, acc_ref):
+    for copy, i, to_ref in zip(copies[1:], parts, [q_ref, k_ref, v_ref, gate_ref]):
+        copy.wait()
+        to_ref[...] = silu(dot(normed, w_ref[i])).astype(BF16)
+    attend(q_ref, k_ref, v_ref, acc_ref, None, causal_mask(rows))
+
+
+def guest_kernel(
+    info_ref, x_ref, w_ref, k_ref, v_ref, own_x_ref, own_gate_ref, own_q_ref, own_acc_ref,
+    all_x_ref, all_gate_ref, all_q_ref, all_acc_ref, guest_k_ref, guest_v_ref,
+):
     rows = x_ref.shape[0]
+    own, guest = slice(0, rows), slice(rows, 2 * rows)
     keep = kept_rows(info_ref[0] + rows, rows, info_ref[1])
     normed = row_norm(x_ref[...].astype(F32), keep).astype(BF16)
-    gate_ref[...] = project(normed, w_ref, 0)
-    q_ref[...] = project(normed, w_ref, 2)
-    attend(q_ref, project(normed, w_ref, 3), project(normed, w_ref, 1), acc_ref, None, causal_mask(rows))
-    attend(q_ref, k_ref[...], v_ref[...], acc_ref, acc_ref)
-
-
-def add_block(info_ref, back, x_ref, w_ref, q_refs, acc_refs, before_refs):
+    all_x_ref[own, :], all_x_ref[guest, :] = own_x_ref[...], x_ref[...]
+    all_gate_ref[own, :], all_gate_ref[guest, :] = own_gate_ref[...], project(normed, w_ref, 0)
+    all_q_ref[own, :], all_q_ref[guest, :] = own_q_ref[...], project(normed, w_ref, 2)
+    all_acc_ref[own, :] = own_acc_ref[...]
+    guest_k_ref[...] = project(normed, w_ref, 3)
+    guest_v_ref[...] = project(normed, w_ref, 1)
+    q_ref, acc_ref = all_q_ref.at[guest, :], all_acc_ref.at[guest, :]
+    attend(q_ref, guest_k_ref, guest_v_ref, acc_ref, None, causal_mask(rows))
+    attend(q_ref, k_ref, v_ref, acc_ref, acc_ref)
+
+
+def add_block(info_ref, back, x_ref, w_ref, q_ref, acc_ref, before_ref):
     keep = kept_rows(info_ref[0] - back, x_ref.shape[0], info_ref[1])
     normed = row_norm(x_ref[...].astype(F32), keep).astype(BF16)
-    keys, values = project(normed, w_ref, 3), project(normed, w_ref, 1)
-    for q_ref, acc_ref, before_ref in zip(q_refs, acc_refs, before_refs):
-        attend(q_ref, keys, values, acc_ref, before_ref)
-
-
-def step_kernel(back, info_ref, x_ref, w_ref, *refs):
-    add_block(info_ref, back, x_ref, w_ref, refs[:2], refs[4:], refs[2:4])
-
-
-def last_kernel(back, info_ref, x_ref, w_ref, *refs):
-    q_refs, before_refs, gate_refs, own_refs = refs[:2], refs[2:4], refs[4:6], refs[6:8]
-    w_out_ref, w_proj_ref, layer_ref, out_ref, hat_ref, *acc_refs = refs[8:]
-    add_block(info_ref, back, x_ref, w_ref, q_refs, acc_refs, before_refs)
-    gated = [
-        (row_norm(acc_ref[...]) * gate_ref[...].astype(F32)).astype(BF16)
-        for acc_ref, gate_ref in zip(acc_refs, gate_refs)
-    ]
-    rest = jnp.concatenate([own_ref[...] for own_ref in own_refs], axis=0).astype(F32)
-    layer = (dot(jnp.concatenate(gated, axis=0), w_out_ref[...]) + rest).astype(BF16)
+    attend(q_ref, project(normed, w_ref, 3), project(normed, w_ref, 1), acc_ref, before_ref)
+
+
+def step_kernel(back, info_ref, x_ref, w_ref, q_ref, before_ref, acc_ref):
+    add_block(info_ref, back, x_ref, w_ref, q_ref, acc_ref, before_ref)
+
+
+def last_kernel(
+    back, info_ref, x_ref, w_ref, q_ref, before_ref, gate_ref, own_ref, w_out_ref, w_proj_ref,
+    layer_ref, out_ref, hat_ref, acc_ref,
+):
+    add_block(info_ref, back, x_ref, w_ref, q_ref, acc_ref, before_ref)
+    gated = (row_norm(acc_ref[...]) * gate_ref[...].astype(F32)).astype(BF16)
+    layer = (dot(gated, w_out_ref[...]) + own_ref[...].astype(F32)).astype(BF16)
     layer_ref[...] = layer
     out = dot(layer, w_proj_ref[...])
     out_ref[...] = out
@@ -157,7 +170,12 @@
     return -(-count // 16) * 16
 
 
-def table_kernel(x_ref, ids_ref, pos_ref, pos_ids_ref, table_ref, message_ref):
+def table_kernel(
+    x_hbm, ids_hbm, pos_hbm, pos_ids_hbm, table_ref, message_ref, x_ref, ids_ref, pos_ref, pos_ids_ref, sems
+):
+    pairs = [(x_hbm, x_ref), (ids_hbm, ids_ref), (pos_hbm, pos_ref), (pos_ids_hbm, pos_ids_ref)]
+    for copy in fetch(pairs, sems):
+        copy.wait()
     count, embed = x_ref.shape
     x = x_ref[...].astype(F32)
     table_ref[:count, :] = (x / norm_of(x)).astype(BF16)
@@ -176,7 +194,7 @@
 def head_kernel(
     hist_count, info_ref, hat_ref, out_ref, layer_ref, pos_ref, ids_ref, guest_ref, *rest
 ):
-    *table_refs, loss_ref, guest_loss_ref, message_ref, keep_ref, send_ref, proj_ref = rest
+    *table_refs, loss_ref, guest_loss_ref, message_ref, keep_ref, send_ref, proj_ref, kept_ref = rest
     rows, embed = hat_ref.shape
     block = rows // 2
     chunks = table_refs[0].shape[0] // (embed + 6)
@@ -200,12 +218,13 @@
                 [parts[(g + j) * chunks + chunk : (g + j) * chunks + chunk + 1, :] for j in range(3)]
                 for g in (0, 3)
             )
-            table = table_ref[chunk * embed : (chunk + 1) * embed, :]
-            scores = dot_t(hat, table) * SCORE_SCALE - (bias[0] + bias[1] + bias[2])
+            cut = slice(chunk * embed, (chunk + 1) * embed)
+            scores = dot_t(hat, table_ref[cut, :]) * SCORE_SCALE - (bias[0] + bias[1] + bias[2])
             kept = jnp.where(of_digits(*ids) != pos_id, jnp.exp2(scores), 0.0)
             for lane in range(0, embed, 128):
                 lanes = lanes + kept[:, lane : lane + 128]
-            grads = grads + dot(kept.astype(BF16), table)
+            kept_ref[:, cut] = kept.astype(BF16)
+        grads = grads + dot(kept_ref[...], table_ref[:count, :])
     pos_part = jnp.exp(pos_score)
     total = pos_part + jnp.sum(lanes, axis=-1, keepdims=True)
     log_total = jnp.log(total)
@@ -220,9 +239,8 @@
     parts = []
     for i in range(2):
         parts += split3(shift[:1, i * block : (i + 1) * block]) + id_rows[i]
-    pad = jnp.zeros((message_ref.shape[0] - rows - len(parts), embed), F32)
-    message_ref[:rows, :] = hat
-    message_ref[rows:, :] = jnp.concatenate(parts + [pad], axis=0).astype(BF16)
+    pad = jnp.zeros((message_ref.shape[0] - len(parts), embed), F32)
+    message_ref[...] = jnp.concatenate(parts + [pad], axis=0).astype(BF16)
     share = jnp.where(valid, 1.0 / (total * hist_count), 0.0)
     pos_weight = jnp.where(valid, pos_part / total - 1.0, 0.0) / hist_count
     d_unit = (pos_weight * pos_unit + share * grads) / SOFTMAX_WARMTH
@@ -282,10 +300,11 @@
 
 
 def negative_kernel(seq_count, info_ref, neg_ref, neg_id_ref, loss_ref, *rest):
-    *message_refs, keep_ref, send_ref, turned_ref, sum_ref = rest
+    *gathered, keep_ref, send_ref, turned_ref, sum_ref, weight_ref = rest
+    pool_count = len(gathered) // 2
     count, embed = neg_ref.shape
     rows = embed
-    blocks = message_refs[0].shape[0] // rows
+    blocks = gathered[0].shape[0] // rows
     tile = min(256, count)
     neg = neg_ref[...].astype(F32)
     norms = norm_of(neg)
@@ -293,16 +312,18 @@
     neg_hat = unit.astype(BF16)
     id_row = neg_id_ref[...].astype(F32)
     neg_id = column(id_row)
-    for i, (message_ref, block) in enumerate(itertools.product(message_refs, range(blocks))):
-        hats = message_ref[block * rows : (block + 1) * rows, :]
-        parts = message_ref[blocks * rows :, :].astype(F32)[6 * block : 6 * block + 6, :]
-        shifts = parts[0:1, :] + parts[1:2, :] + parts[2:3, :]
-        ids = of_digits(parts[3:4, :], parts[4:5, :], parts[5:6, :])
+    for i, (hats_ref, message_ref) in enumerate(zip(gathered[:pool_count], gathered[pool_count:])):
+        parts = message_ref[...].astype(F32)
+        for block, start in itertools.product(range(blocks), range(0, count, tile)):
+            own = slice(block * rows, (block + 1) * rows)
+            cut = slice(start, start + tile)
+            shift = [parts[6 * block + j : 6 * block + j + 1, :] for j in range(6)]
+            scores = dot_t(neg_hat[cut, :], hats_ref[own, :]) * SCORE_SCALE - (shift[0] + shift[1] + shift[2])
+            weights = jnp.where(neg_id[cut, :] != of_digits(*shift[3:]), jnp.exp2(scores), 0.0)
+            weight_ref[cut, own] = weights.astype(BF16)
         for start in range(0, count, tile):
             cut = slice(start, start + tile)
-            scores = dot_t(neg_hat[cut, :], hats) * SCORE_SCALE - shifts
-            weights = jnp.where(neg_id[cut, :] != ids, jnp.exp2(scores), 0.0)
-            term = dot(weights.astype(BF16), hats)
+            term = dot(weight_ref[cut, :], hats_ref[...])
             sum_ref[cut, :] = sum_ref[cut, :] + term if i else term
     neg_sum = sum_ref[...] * column(jnp.exp2(-LOG2E * log_sample_chance(id_row)) / SOFTMAX_WARMTH)
     grad = (neg_sum - unit * jnp.sum(unit * neg_sum, axis=-1, keepdims=True)) / norms
@@ -319,8 +340,8 @@
     send_ref[kept:, : loss_ref.shape[1]] = jnp.concatenate(parts + [pad], axis=0).astype(BF16)
 
 
-def call(kernel, ins, outs, scratch=(), limit=24, flops=0, moved=0, name=None):
-    in_specs = [pl.BlockSpec(memory_space=pltpu.SMEM if x.ndim == 1 else pltpu.VMEM) for x in ins]
+def call(kernel, ins, outs, scratch=(), limit=24, flops=0, moved=0, name=None, place=pltpu.VMEM):
+    in_specs = [pl.BlockSpec(memory_space=pltpu.SMEM if x.ndim == 1 else place) for x in ins]
     many = isinstance(outs, (list, tuple))
     out_specs = jax.tree.map(lambda _: pl.BlockSpec(memory_space=pltpu.VMEM), outs)
     return pl.pallas_call(
@@ -378,8 +399,9 @@
         own_kernel,
         [info, own, w_in],
         [kind, kind, kind, kind, wide],
-        flops=2 * rows * width * (w_in.shape[1] + 2 * rows),
-        moved=2 * w_in.size,
+        scratch=[pltpu.VMEM((rows, width), BF16), pltpu.VMEM((4, width, width), BF16), pltpu.SemaphoreType.DMA((5,))],
+        place=pl.ANY,
+        limit=44,
         name="own_block",
     )
     table_part, pos_part = call(
@@ -389,21 +411,33 @@
             struct((local_neg + padded_rows(6 * local_neg // embed), embed), BF16),
             struct((rows + 16, embed), BF16),
         ],
+        scratch=[
+            pltpu.VMEM((local_neg, embed), BF16), pltpu.VMEM((1, local_neg), jnp.int32),
+            pltpu.VMEM((rows, embed), BF16), pltpu.VMEM((1, rows), jnp.int32), pltpu.SemaphoreType.DMA((4,)),
+        ],
+        place=pl.ANY,
+        limit=24,
         name="table_part",
     )
     table_part, pos_part, acc = together(table_part, pos_part, acc)
     table = gather_step([table_part], "pool", pool_count)
     block, guest, acc = together(block, guest, acc)
+    tall = struct((2 * rows, width), BF16)
+    tall_wide = struct((2 * rows, width), F32)
     for step in range(1, seq_count - 2):
         following = lax.ppermute(block, "seq", up)
         if step == 1:
-            guest_gate, guest_queries, guest_acc = call(
-                guest_kernel, [info, guest, w_in, keys, values], [kind, kind, wide], name="guest_block"
+            own, gate, queries, acc = call(
+                guest_kernel,
+                [info, guest, w_in, keys, values, own, gate, queries, acc],
+                [tall, tall, tall, tall_wide],
+                scratch=[pltpu.VMEM((rows, width), BF16)] * 2,
+                name="guest_block",
             )
-        acc, guest_acc = call(
+        acc = call(
             functools.partial(step_kernel, step * rows),
-            [info, block, w_in, queries, guest_queries, acc, guest_acc],
-            [wide, wide],
+            [info, block, w_in, queries, acc],
+            tall_wide,
             name=f"earlier_block_{step}",
         )
         acc, table, pos_part = together(acc, table, pos_part)
@@ -415,25 +449,22 @@
         table = gather_step(table, "pool", pool_count)
     layer, out, hat = call(
         functools.partial(last_kernel, (seq_count - 2) * rows),
-        [info, block, w_in, queries, guest_queries, acc, guest_acc, gate, guest_gate, own, guest, w_out, w_proj],
-        [struct((2 * rows, width), BF16), struct((2 * rows, embed), F32), struct((2 * rows, embed), BF16)],
-        scratch=[pltpu.VMEM((rows, width), F32)] * 2,
-        flops=2 * rows * width * (4 * width + 4 * rows + 2 * embed),
-        moved=6 * width * width,
+        [info, block, w_in, queries, acc, gate, own, w_out, w_proj],
+        [tall, struct((2 * rows, embed), F32), struct((2 * rows, embed), BF16)],
+        scratch=[pltpu.VMEM((2 * rows, width), F32)],
         name="last_block",
     )
+    hats = gather_step([hat], "pool", pool_count)
 
     half, chips = width // 2, plane_count // 2
     loss, guest_loss, message, keep, send = call(
         functools.partial(head_kernel, plane_count),
         [info, hat, out, layer, pos_embed[0], pos_ids, guest_pos, *table],
         [
-            struct((1, rows), F32), struct((1, rows), F32), struct((2 * rows + 16, embed), BF16),
+            struct((1, rows), F32), struct((1, rows), F32), struct((16, embed), BF16),
             struct((half, embed), F32), struct((half, embed), BF16),
         ],
-        scratch=[pltpu.VMEM((width, embed), F32)],
-        flops=8 * rows * local_neg * pool_count * embed,
-        moved=2 * local_neg * pool_count * embed,
+        scratch=[pltpu.VMEM((width, embed), F32), pltpu.VMEM((2 * rows, local_neg), BF16)],
         name="head",
     )
     part = struct((half // chips, embed), BF16)
@@ -441,8 +472,7 @@
     def plane_swap(parts):
         return [swap(x, plane, plane_count, 2 * r) for r, x in enumerate(parts, 1)]
 
-    got = swap(send, plane, plane_count, 1)
-    messages = gather_step([message], "pool", pool_count)
+    got, messages = together(swap(send, plane, plane_count, 1), gather_step([message], "pool", pool_count))
     own_part, *sends = call(
         halved_kernel,
         [info, keep, got],
@@ -450,39 +480,46 @@
         scratch=[pltpu.VMEM((half, embed), F32)],
         name="halved",
     )
-    own_part, messages = together(own_part, messages)
+    hats, _ = together(hats, own_part)
+    while len(hats) < pool_count:
+        hats = gather_step(hats, "pool", pool_count)
     while len(messages) < pool_count:
         messages = gather_step(messages, "pool", pool_count)
-    proj_parts = [own_part] + plane_swap(sends)
+    proj_parts, messages = together([own_part] + plane_swap(sends), messages)
+    proj_part = call(sum_kernel, proj_parts, part, name="plane_sum")
+    bit = 1
+    while 2 * bit < seq_count:
+        got = swap(proj_part, "seq", seq_count, bit)
+        proj_part = call(sum_kernel, [proj_part, got], part, name=f"seq_sum_{bit}")
+        bit *= 2
+    hats, messages, _ = together(hats, messages, proj_part)
     keep, send = call(
         functools.partial(negative_kernel, seq_count),
-        [info, neg_embed[0], neg_ids, guest_loss, *messages],
+        [info, neg_embed[0], neg_ids, guest_loss, *hats, *messages],
         [struct((embed // 2, local_neg), F32), struct((embed // 2 + 16, local_neg), BF16)],
-        scratch=[pltpu.VMEM((embed, local_neg), F32), pltpu.VMEM((local_neg, embed), F32)],
+        scratch=[
+            pltpu.VMEM((embed, local_neg), F32), pltpu.VMEM((local_neg, embed), F32),
+            pltpu.VMEM((local_neg, 2 * rows), BF16),
+        ],
         name="neg_grad",
     )
-    proj_parts, keep, send = together(proj_parts, keep, send)
-    proj_part = call(sum_kernel, proj_parts, part, name="plane_sum")
-    bit = 1
+    got, keep, send = together(swap(proj_part, "seq", seq_count, bit), keep, send)
+    proj_part = call(sum_kernel, [proj_part, got], part, name=f"seq_sum_{bit}")
+    got = swap(send, "seq", seq_count, 1)
+    got, _ = together(got, proj_part)
+    loss = call(functools.partial(loss_kernel, seq_count - 1), [info, loss, got], struct((1, rows), F32), name="loss")
+    bit = 2
     while bit < seq_count:
-        if bit == 1:
-            proj_part, send = together(proj_part, send)
-        proj_got, got = swap(proj_part, "seq", seq_count, bit), swap(send, "seq", seq_count, bit)
-        proj_part = call(sum_kernel, [proj_part, proj_got], part, name=f"seq_sum_{bit}")
-        if 2 * bit < seq_count:
-            if bit == 1:
-                loss = call(
-                    functools.partial(loss_kernel, seq_count - 1), [info, loss, got], struct((1, rows), F32), name="loss"
-                )
-            size = keep.shape[0] // 2
-            keep, send = call(
-                functools.partial(halving_kernel, cols),
-                [keep, got],
-                [struct((size, local_neg), F32), struct((size, local_neg), BF16)],
-                name=f"neg_halved_{bit}",
-            )
+        size = keep.shape[0] // 2
+        keep, send = call(
+            functools.partial(halving_kernel, cols),
+            [keep, got],
+            [struct((size, local_neg), F32), struct((size, local_neg), BF16)],
+            name=f"neg_halved_{bit}",
+        )
+        got = swap(send, "seq", seq_count, bit)
         bit *= 2
-    proj_parts, got = together([proj_part] + plane_swap([proj_part] * (chips - 1)), got)
+    proj_parts, send = together([proj_part] + plane_swap([proj_part] * (chips - 1)), send)
     proj_half = call(
         functools.partial(lay_kernel, 4), [info, *proj_parts], struct((half, embed), BF16), name="lay_half"
     )

time: 92.7 us -> 116 us (1.25)
  waiting for transfers between devices: 24.1 us -> 44.2 us
  starting transfers between devices: 26 us -> 32.1 us
  local copies, waits for them, and re-layouts: 7.86 us -> 3.11 us
  Pallas kernels: 32.8 us -> 34.8 us
    ppermute x1, waiting for transfers between devices: 0.01 us -> 10.2 us  [body(): block = lax.ppermute(own, 'seq', up)]
    ppermute x1, waiting for transfers between devices: 0.49 us -> 10.5 us  [body(): following = lax.ppermute(block, 'seq', up)]
    ppermute x18 -> x21, starting transfers between devices: 16 us -> 22.7 us  [swap(): return lax.ppermute(x, axis, [(i, i ^ r) for i in range(count)])]
    unnamed x26 -> x22, local copies, waits for them, and re-layouts: 7.77 us -> 3.02 us
    pallas_call x16, Pallas kernels: 32.8 us -> 34.8 us  [call(): pl.pallas_call(kernel, out_shape=list(outs) if many else outs, in_specs=i...]
    ppermute x1, starting transfers between devices: 4.96 us -> 3.5 us  [body(): block = lax.ppermute(own, 'seq', up)]
    ppermute x18 -> x21, waiting for transfers between devices: 23.6 us -> 23.6 us  [swap(): return lax.ppermute(x, axis, [(i, i ^ r) for i in range(count)])]
  transfers between devices with their start and end apart: 22 -> 25, of which waited for: 9 -> 9; matrix products, arithmetic and copies ran while one was open for 0% -> 0% of each run, Pallas kernels for 28% -> 18%
where the time goes in v2:
time: 116 us
  waiting for transfers between devices  44.2 us (38%)
  Pallas kernels  34.8 us (30%)
  starting transfers between devices  32.1 us (28%)
  local copies, waits for them, and re-layouts  3.11 us (3%)
  between operations  1.6 us (1%)
    pallas_call x16, Pallas kernels, call(): pl.pallas_call(kernel, out_shape=list(outs) if many else outs, in_specs=i...  34.8 us
    ppermute x21, waiting for transfers between devices, swap(): return lax.ppermute(x, axis, [(i, i ^ r) for i in range(count)])  23.6 us
    ppermute x21, starting transfers between devices, swap(): return lax.ppermute(x, axis, [(i, i ^ r) for i in range(count)])  22.7 us
    ppermute x1, waiting for transfers between devices, body(): following = lax.ppermute(block, 'seq', up)  10.5 us
    ppermute x1, waiting for transfers between devices, body(): block = lax.ppermute(own, 'seq', up)  10.2 us
    ppermute x1, starting transfers between devices, body(): following = lax.ppermute(block, 'seq', up)  4.41 us
    ppermute x1, starting transfers between devices, body(): block = lax.ppermute(own, 'seq', up)  3.5 us
    unnamed x22, local copies, waits for them, and re-layouts  3.02 us
  transfers between devices with their start and end apart: 25, of which 9 were waited for; matrix products, arithmetic and copies ran while one was open for 0% of the time, Pallas kernels for 18%

profile of v2, /device:TPU:0, one launch (start us, length us, event | category | flops | bytes accessed | tf_op | source)
XLA Modules:
  0.0 115.9 jit_solution(17837267495453680498)
XLA Ops:
  1.4 1.0 copy-done.2
  2.4 6.3 %own_block.1 = (bf16[256,1024]{1,0:T(8,128)(2,1)S(1)}, bf16[256,1024]{1,0:T(8,128)(2,1)S(1)}, bf16[256,1024]{1,0:T(8,128)(2,1)S(1)}, bf16[256,1024]{1,0:T(8,128)(2,1)S(1)}, f32[256,1024]{1,0:T(8,128)S(1)}) custom-call(s32[7]{0:T(128)S(1)} %stack.27.info_ref, bf16[256,1024]{1,0:T(8,128)(2,1)S(1)} %bitcast.15, bf16[1024,4096]{1,0:T(8,128)(2,1)} %w_ref.5), custom_call_target="tpu_custom_call" | custom-call | tf_op jit(solution)/shard_map/own_block/pallas_call | solution.py:347
  8.8 1.0 copy-done.4
  9.8 0.9 copy-done.7
  11.3 3.0 %collective-permute-start.3 = (bf16[1056,256]{1,0:T(8,128)(2,1)S(1)}, bf16[1056,256]{1,0:T(8,128)(2,1)S(1)}, u32[]{:S(2)}, u32[]{:S(2)}) collective-permute-start(bf16[1056,256]{1,0:T(8,128)(2,1)S(1)} %get-tuple-element.95.rest_0_), channel_id=1, source_target_pairs={{0,2},{1,3},{2,0},{3,1},{4,6},{5,7},{6,4},{7,5},{8,10},{9,11},{10,... | collective-permute-start | bytes 1622024 | tf_op jit(solution)/shard_map/ppermute | solution.py:360
  14.3 3.5 %collective-permute-start = (bf16[256,1024]{1,0:T(8,128)(2,1)S(1)}, bf16[256,1024]{1,0:T(8,128)(2,1)S(1)}, u32[]{:S(2)}, u32[]{:S(2)}) collective-permute-start(bf16[256,1024]{1,0:T(8,128)(2,1)S(1)} %bitcast.16), channel_id=1, source_target_pairs={{0,4},{4,8},{1,5},{5,9},{2,6},{6,10},{3,7},{7,11},{16,20},{20,24},... | collective-permute-start | bytes 1572872 | tf_op jit(solution)/shard_map/ppermute | solution.py:394
  18.5 10.2 %collective-permute-done.x_ref = bf16[256,1024]{1,0:T(8,128)(2,1)S(1)} collective-permute-done((bf16[256,1024]{1,0:T(8,128)(2,1)S(1)}, bf16[256,1024]{1,0:T(8,128)(2,1)S(1)}, u32[]{:S(2)}, u32[]{:S(2)}) %collective-permute-start) | collective-permute-done | bytes 524320 | tf_op jit(solution)/shard_map/ppermute | solution.py:394
  28.7 4.8 %guest_block.1 = (bf16[512,1024]{1,0:T(8,128)(2,1)S(1)}, bf16[512,1024]{1,0:T(8,128)(2,1)S(1)}, bf16[512,1024]{1,0:T(8,128)(2,1)S(1)}, f32[512,1024]{1,0:T(8,128)S(1)}) custom-call(s32[7]{0:T(128)S(1)} %stack.27.info_ref, bf16[256,1024]{1,0:T(8,128)(2,1)S(1)} %collective-permute-done.1.x_ref, bf16[1024,4096]{1,0:T(8,128)(2,1)S(1)} %copy-done, ...), custom_call_target="tpu_custom_call" | custom-call | tf_op jit(solution)/shard_map/guest_block/pallas_call | solution.py:347
  33.5 3.6 %earlier_block_1.1.before_ref = f32[512,1024]{1,0:T(8,128)S(1)} custom-call(s32[7]{0:T(128)S(1)} %stack.27.info_ref, bf16[256,1024]{1,0:T(8,128)(2,1)S(1)} %collective-permute-done.x_ref, bf16[1024,4096]{1,0:T(8,128)(2,1)S(1)} %copy-done, bf16[512,1024]{1,0:T(8,128)(2,1)S(1)} %get-tuple-element.82.q_ref, f32[512,1024]{1,0:T(8,128)S(1)} %get-tuple-element.83.before_ref), custom_call_target="tpu_custom_call" | custom-call | tf_op jit(solution)/shard_map/earlier_block_1/pallas_call | solution.py:347
  37.7 4.4 %collective-permute-start.2 = (bf16[256,1024]{1,0:T(8,128)(2,1)S(1)}, bf16[256,1024]{1,0:T(8,128)(2,1)S(1)}, u32[]{:S(2)}, u32[]{:S(2)}) collective-permute-start(bf16[256,1024]{1,0:T(8,128)(2,1)S(1)} %collective-permute-done.x_ref), channel_id=1, source_target_pairs={{0,4},{4,8},{1,5},{5,9},{2,6},{6,10},{3,7},{7,11},{16,20},{20,24},... | collective-permute-start | bytes 1572872 | tf_op jit(solution)/shard_map/ppermute | solution.py:428
  42.1 0.8 collective-permute-start.4
  43.0 10.5 %collective-permute-done.2.x_ref = bf16[256,1024]{1,0:T(8,128)(2,1)S(1)} collective-permute-done((bf16[256,1024]{1,0:T(8,128)(2,1)S(1)}, bf16[256,1024]{1,0:T(8,128)(2,1)S(1)}, u32[]{:S(2)}, u32[]{:S(2)}) %collective-permute-start.2) | collective-permute-done | bytes 524320 | tf_op jit(solution)/shard_map/ppermute | solution.py:428
  53.5 6.2 %last_block.1 = (bf16[512,1024]{1,0:T(8,128)(2,1)S(1)}, f32[512,256]{1,0:T(8,128)S(1)}, bf16[512,256]{1,0:T(8,128)(2,1)S(1)}) custom-call(s32[7]{0:T(128)S(1)} %stack.27.info_ref, bf16[256,1024]{1,0:T(8,128)(2,1)S(1)} %collective-permute-done.2.x_ref, bf16[1024,4096]{1,0:T(8,128)(2,1)S(1)} %copy-done, bf16[512,1024]{1,0:T(8,128)(2,1)S(1)} %get-tuple-element.82.q_ref, ...), custom_call_target="tpu_custom_call" | custom-call | tf_op jit(solution)/shard_map/last_block/pallas_call | solution.py:347
  59.7 4.9 %head.1 = (f32[1,256]{1,0:T(1,128)S(1)}, f32[1,256]{1,0:T(1,128)S(1)}, bf16[16,256]{1,0:T(8,128)(2,1)S(1)}, f32[512,256]{1,0:T(8,128)S(1)}, bf16[512,256]{1,0:T(8,128)(2,1)S(1)}) custom-call(s32[7]{0:T(128)S(1)} %stack.27.info_ref, bf16[512,256]{1,0:T(8,128)(2,1)S(1)} %get-tuple-element.119.hat_ref.rest_0_, f32[512,256]{1,0:T(8,128)S(1)} %get-tuple-element.92.out_ref, ...), custom_call_target="tpu_custom_call" | custom-call | tf_op jit(solution)/shard_map/head/pallas_call | solution.py:347
  65.3 1.5 %collective-permute-start.8 = (bf16[16,256]{1,0:T(8,128)(2,1)S(1)}, bf16[16,256]{1,0:T(8,128)(2,1)S(1)}, u32[]{:S(2)}, u32[]{:S(2)}) collective-permute-start(bf16[16,256]{1,0:T(8,128)(2,1)S(1)} %get-tuple-element.123.rest_4_), channel_id=1, source_target_pairs={{0,2},{1,3},{2,0},{3,1},{4,6},{5,7},{6,4},{7,5},{8,10},{9,11},{10,... | collective-permute-start | bytes 24584 | tf_op jit(solution)/shard_map/ppermute | solution.py:360
  66.8 6.8 %collective-permute-done.8.rest_5_ = bf16[16,256]{1,0:T(8,128)(2,1)S(1)} collective-permute-done((bf16[16,256]{1,0:T(8,128)(2,1)S(1)}, bf16[16,256]{1,0:T(8,128)(2,1)S(1)}, u32[]{:S(2)}, u32[]{:S(2)}) %collective-permute-start.8) | collective-permute-done | bytes 8224 | tf_op jit(solution)/shard_map/ppermute | solution.py:360
  75.3 1.5 %collective-permute-start.10 = (bf16[128,256]{1,0:T(8,128)(2,1)S(1)}, bf16[128,256]{1,0:T(8,128)(2,1)S(1)}, u32[]{:S(2)}, u32[]{:S(2)}) collective-permute-start(bf16[128,256]{1,0:T(8,128)(2,1)S(1)} %get-tuple-element.104), channel_id=1, source_target_pairs={{0,16},{1,17},{2,18},{3,19},{16,0},{17,1},{18,2},{19,3},{4,20},{5,... | collective-permute-start | bytes 196616 | tf_op jit(solution)/shard_map/ppermute | solution.py:360
  77.7 1.5 %collective-permute-start.9 = (bf16[128,256]{1,0:T(8,128)(2,1)S(1)}, bf16[128,256]{1,0:T(8,128)(2,1)S(1)}, u32[]{:S(2)}, u32[]{:S(2)}) collective-permute-start(bf16[128,256]{1,0:T(8,128)(2,1)S(1)} %get-tuple-element.103), channel_id=1, source_target_pairs={{0,2},{1,3},{2,0},{3,1},{16,18},{17,19},{18,16},{19,17},{4,6},{5,7... | collective-permute-start | bytes 196616 | tf_op jit(solution)/shard_map/ppermute | solution.py:360
  80.0 2.0 %collective-permute-done.11.refs_3_ = bf16[128,256]{1,0:T(8,128)(2,1)S(1)} collective-permute-done((bf16[128,256]{1,0:T(8,128)(2,1)S(1)}, bf16[128,256]{1,0:T(8,128)(2,1)S(1)}, u32[]{:S(2)}, u32[]{:S(2)}) %collective-permute-start.11) | collective-permute-done | bytes 65568 | tf_op jit(solution)/shard_map/ppermute | solution.py:360
  82.1 0.9 collective-permute-done.9.refs_1_
  83.0 2.9 %collective-permute-start.14 = (bf16[128,256]{1,0:T(8,128)(2,1)S(1)}, bf16[128,256]{1,0:T(8,128)(2,1)S(1)}, u32[]{:S(2)}, u32[]{:S(2)}) collective-permute-start(bf16[128,256]{1,0:T(8,128)(2,1)S(1)} %plane_sum.1.refs_0_), channel_id=1, source_target_pairs={{0,4},{4,0},{8,12},{12,8},{1,5},{5,1},{9,13},{13,9},{2,6},{6,2},{1... | collective-permute-start | bytes 196616 | tf_op jit(solution)/shard_map/ppermute | solution.py:360
  85.9 2.2 %collective-permute-done.14.refs_1_ = bf16[128,256]{1,0:T(8,128)(2,1)S(1)} collective-permute-done((bf16[128,256]{1,0:T(8,128)(2,1)S(1)}, bf16[128,256]{1,0:T(8,128)(2,1)S(1)}, u32[]{:S(2)}, u32[]{:S(2)}) %collective-permute-start.14) | collective-permute-done | bytes 65568 | tf_op jit(solution)/shard_map/ppermute | solution.py:360
  88.2 4.0 %collective-permute-start.15 = (bf16[128,256]{1,0:T(8,128)(2,1)S(1)}, bf16[128,256]{1,0:T(8,128)(2,1)S(1)}, u32[]{:S(2)}, u32[]{:S(2)}) collective-permute-start(bf16[128,256]{1,0:T(8,128)(2,1)S(1)} %seq_sum_1.1.refs_0_), channel_id=1, source_target_pairs={{0,8},{4,12},{8,0},{12,4},{1,9},{5,13},{9,1},{13,5},{2,10},{6,14},... | collective-permute-start | bytes 196616 | tf_op jit(solution)/shard_map/ppermute | solution.py:360
  92.2 3.7 %neg_grad.1 = (f32[128,1024]{1,0:T(8,128)S(1)}, bf16[144,1024]{1,0:T(8,128)(2,1)S(1)}) custom-call(s32[7]{0:T(128)S(1)} %stack.27.info_ref, bf16[1024,256]{1,0:T(8,128)(2,1)S(1)} %bitcast.20, s32[1,1024]{1,0:T(1,128)S(1)} %copy-done.9, f32[1,256]{1,0:T(1,128)S(1)} %get-tuple-element.112.loss_ref, bf16[512,256]{1,0:T(8,128)(2,1)S(1)} %get-tuple-element.119.hat_ref.rest_0_, ...), custom_call_target="tpu_custom_call" | custom-call | tf_op jit(solution)/shard_map/neg_grad/pallas_call | solution.py:347
  96.0 1.0 collective-permute-start.21
  97.0 1.1 collective-permute-start.22
  98.1 1.5 %collective-permute-start.23 = (bf16[128,256]{1,0:T(8,128)(2,1)S(1)}, bf16[128,256]{1,0:T(8,128)(2,1)S(1)}, u32[]{:S(2)}, u32[]{:S(2)}) collective-permute-start(bf16[128,256]{1,0:T(8,128)(2,1)S(1)} %seq_sum_2.1.refs_0_), channel_id=1, source_target_pairs={{0,18},{1,19},{2,16},{3,17},{16,2},{17,3},{18,0},{19,1},{4,22},{5,... | collective-permute-start | bytes 196616 | tf_op jit(solution)/shard_map/ppermute | solution.py:360
  99.6 3.6 %collective-permute-done.19.got_ref = bf16[144,1024]{1,0:T(8,128)(2,1)S(1)} collective-permute-done((bf16[144,1024]{1,0:T(8,128)(2,1)S(1)}, bf16[144,1024]{1,0:T(8,128)(2,1)S(1)}, u32[]{:S(2)}, u32[]{:S(2)}) %collective-permute-start.19) | collective-permute-done | bytes 294944 | tf_op jit(solution)/shard_map/ppermute | solution.py:360
  103.9 1.4 %collective-permute-start.20 = (bf16[64,1024]{1,0:T(8,128)(2,1)S(1)}, bf16[64,1024]{1,0:T(8,128)(2,1)S(1)}, u32[]{:S(2)}, u32[]{:S(2)}) collective-permute-start(bf16[64,1024]{1,0:T(8,128)(2,1)S(1)} %get-tuple-element.134), channel_id=1, source_target_pairs={{0,8},{4,12},{8,0},{12,4},{1,9},{5,13},{9,1},{13,5},{2,10},{6,14},... | collective-permute-start | bytes 393224 | tf_op jit(solution)/shard_map/ppermute | solution.py:360
  105.3 1.1 loss.1
  106.4 7.1 %collective-permute-done.20.refs_1_ = bf16[64,1024]{1,0:T(8,128)(2,1)S(1)} collective-permute-done((bf16[64,1024]{1,0:T(8,128)(2,1)S(1)}, bf16[64,1024]{1,0:T(8,128)(2,1)S(1)}, u32[]{:S(2)}, u32[]{:S(2)}) %collective-permute-start.20) | collective-permute-done | bytes 131104 | tf_op jit(solution)/shard_map/ppermute | solution.py:360
  114.3 1.6 %lay_whole.1 = f32[1024,256]{1,0:T(8,128)} custom-call(s32[7]{0:T(128)S(1)} %stack.27.info_ref, bf16[512,256]{1,0:T(8,128)(2,1)S(1)} %lay_half.1.refs_0_, bf16[512,256]{1,0:T(8,128)(2,1)S(1)} %collective-permute-done.24.refs_1_), custom_call_target="tpu_custom_call" | custom-call | tf_op jit(solution)/shard_map/lay_whole/pallas_call | solution.py:347
  (57 shorter events, 7.7 us)
Async XLA Ops:
  0.6 8.1 %copy-start.10 = (s32[1,256]{1,0:T(1,128)S(1)}, s32[1,256]{1,0:T(1,128)}, u32[]{:S(2)}) copy-start(s32[1,256]{1,0:T(1,128)} %ids_ref.1) | copy-start | bytes 3076
  2.4 6.3 %copy-start.9 = (s32[1,1024]{1,0:T(1,128)S(1)}, s32[1,1024]{1,0:T(1,128)}, u32[]{:S(2)}) copy-start(s32[1,1024]{1,0:T(1,128)} %neg_id_ref.1) | copy-start | bytes 12292
  2.4 26.2 %copy-start = (bf16[1024,4096]{1,0:T(8,128)(2,1)S(1)}, bf16[1024,4096]{1,0:T(8,128)(2,1)}, u32[]{:S(2)}) copy-start(bf16[1024,4096]{1,0:T(8,128)(2,1)} %w_ref.5) | copy-start | bytes 25165828
  2.4 26.2 %copy-start.3 = (bf16[1,256,1024]{2,1,0:T(8,128)(2,1)S(1)}, bf16[1,256,1024]{2,1,0:T(8,128)(2,1)}, u32[]{:S(2)}) copy-start(bf16[1,256,1024]{2,1,0:T(8,128)(2,1)} %param.9) | copy-start | bytes 1572868
  11.3 25.8 %collective-permute-start.3 = (bf16[1056,256]{1,0:T(8,128)(2,1)S(1)}, bf16[1056,256]{1,0:T(8,128)(2,1)S(1)}, u32[]{:S(2)}, u32[]{:S(2)}) collective-permute-start(bf16[1056,256]{1,0:T(8,128)(2,1)S(1)} %get-tuple-element.95.rest_0_), channel_id=1, source_target_pairs={{0,2},{1,3},{2,0},{3,1},{4,6},{5,7},{6,4},{7,5},{8,10},{9,11},{10,... | collective-permute-start | bytes 1622024 | tf_op jit(solution)/shard_map/ppermute | solution.py:360
  14.3 14.4 %collective-permute-start = (bf16[256,1024]{1,0:T(8,128)(2,1)S(1)}, bf16[256,1024]{1,0:T(8,128)(2,1)S(1)}, u32[]{:S(2)}, u32[]{:S(2)}) collective-permute-start(bf16[256,1024]{1,0:T(8,128)(2,1)S(1)} %bitcast.16), channel_id=1, source_target_pairs={{0,4},{4,8},{1,5},{5,9},{2,6},{6,10},{3,7},{7,11},{16,20},{20,24},... | collective-permute-start | bytes 1572872 | tf_op jit(solution)/shard_map/ppermute | solution.py:394
  17.8 10.9 %collective-permute-start.1 = (bf16[256,1024]{1,0:T(8,128)(2,1)S(1)}, bf16[256,1024]{1,0:T(8,128)(2,1)S(1)}, u32[]{:S(2)}, u32[]{:S(2)}) collective-permute-start(bf16[256,1024]{1,0:T(8,128)(2,1)S(1)} %bitcast.17), channel_id=1, source_target_pairs={{12,8},{13,9},{14,10},{15,11},{28,24},{29,25},{30,26},{31,27}} | collective-permute-start | bytes 1572872 | tf_op jit(solution)/shard_map/ppermute | solution.py:395
  33.5 20.0 %copy-start.1 = (bf16[1024,1024]{1,0:T(8,128)(2,1)S(1)}, bf16[1024,1024]{1,0:T(8,128)(2,1)}, u32[]{:S(2)}) copy-start(bf16[1024,1024]{1,0:T(8,128)(2,1)} %w_out_ref.1) | copy-start | bytes 6291460
  33.5 20.0 %copy-start.6 = (bf16[1024,256]{1,0:T(8,128)(2,1)S(1)}, bf16[1024,256]{1,0:T(8,128)(2,1)}, u32[]{:S(2)}) copy-start(bf16[1024,256]{1,0:T(8,128)(2,1)} %w_proj_ref.1) | copy-start | bytes 1572868
  37.1 22.6 %collective-permute-start.5 = (bf16[1056,256]{1,0:T(8,128)(2,1)S(1)}, bf16[1056,256]{1,0:T(8,128)(2,1)S(1)}, u32[]{:S(2)}, u32[]{:S(2)}) collective-permute-start(bf16[1056,256]{1,0:T(8,128)(2,1)S(1)} %get-tuple-element.95.rest_0_), channel_id=1, source_target_pairs={{0,1},{1,0},{2,3},{3,2},{4,5},{5,4},{6,7},{7,6},{8,9},{9,8},{10,11... | collective-permute-start | bytes 1622024 | tf_op jit(solution)/shard_map/ppermute | solution.py:360
  37.2 22.5 %collective-permute-start.6 = (bf16[1056,256]{1,0:T(8,128)(2,1)S(1)}, bf16[1056,256]{1,0:T(8,128)(2,1)S(1)}, u32[]{:S(2)}, u32[]{:S(2)}) collective-permute-start(bf16[1056,256]{1,0:T(8,128)(2,1)S(1)} %collective-permute-done.3.rest_1_), channel_id=1, source_target_pairs={{0,1},{1,0},{2,3},{3,2},{4,5},{5,4},{6,7},{7,6},{8,9},{9,8},{10,11... | collective-permute-start | bytes 1622024 | tf_op jit(solution)/shard_map/ppermute | solution.py:360
  37.7 15.8 %collective-permute-start.2 = (bf16[256,1024]{1,0:T(8,128)(2,1)S(1)}, bf16[256,1024]{1,0:T(8,128)(2,1)S(1)}, u32[]{:S(2)}, u32[]{:S(2)}) collective-permute-start(bf16[256,1024]{1,0:T(8,128)(2,1)S(1)} %collective-permute-done.x_ref), channel_id=1, source_target_pairs={{0,4},{4,8},{1,5},{5,9},{2,6},{6,10},{3,7},{7,11},{16,20},{20,24},... | collective-permute-start | bytes 1572872 | tf_op jit(solution)/shard_map/ppermute | solution.py:428
  42.1 17.6 %collective-permute-start.4 = (bf16[272,256]{1,0:T(8,128)(2,1)S(1)}, bf16[272,256]{1,0:T(8,128)(2,1)S(1)}, u32[]{:S(2)}, u32[]{:S(2)}) collective-permute-start(bf16[272,256]{1,0:T(8,128)(2,1)S(1)} %get-tuple-element.94), channel_id=1, source_target_pairs={{12,8},{13,9},{14,10},{15,11},{28,24},{29,25},{30,26},{31,27}} | collective-permute-start | bytes 417800 | tf_op jit(solution)/shard_map/ppermute | solution.py:445
  59.7 32.5 %copy-start.5 = (bf16[1,1024,256]{2,1,0:T(8,128)(2,1)S(1)}, bf16[1,1024,256]{2,1,0:T(8,128)(2,1)}, u32[]{:S(2)}) copy-start(bf16[1,1024,256]{2,1,0:T(8,128)(2,1)} %param.16) | copy-start | bytes 1572868
  64.6 9.0 %collective-permute-start.7 = (bf16[512,256]{1,0:T(8,128)(2,1)S(1)}, bf16[512,256]{1,0:T(8,128)(2,1)S(1)}, u32[]{:S(2)}, u32[]{:S(2)}) collective-permute-start(bf16[512,256]{1,0:T(8,128)(2,1)S(1)} %get-tuple-element.99), channel_id=1, source_target_pairs={{0,1},{1,0},{2,3},{3,2},{16,17},{17,16},{18,19},{19,18},{4,5},{5,4... | collective-permute-start | bytes 786440 | tf_op jit(solution)/shard_map/ppermute | solution.py:360
  64.7 9.5 %collective-permute-start.16 = (bf16[512,256]{1,0:T(8,128)(2,1)S(1)}, bf16[512,256]{1,0:T(8,128)(2,1)S(1)}, u32[]{:S(2)}, u32[]{:S(2)}) collective-permute-start(bf16[512,256]{1,0:T(8,128)(2,1)S(1)} %get-tuple-element.119.hat_ref.rest_0_), channel_id=1, source_target_pairs={{0,2},{1,3},{2,0},{3,1},{4,6},{5,7},{6,4},{7,5},{8,10},{9,11},{10,... | collective-permute-start | bytes 786440 | tf_op jit(solution)/shard_map/ppermute | solution.py:360
  65.3 8.3 %collective-permute-start.8 = (bf16[16,256]{1,0:T(8,128)(2,1)S(1)}, bf16[16,256]{1,0:T(8,128)(2,1)S(1)}, u32[]{:S(2)}, u32[]{:S(2)}) collective-permute-start(bf16[16,256]{1,0:T(8,128)(2,1)S(1)} %get-tuple-element.123.rest_4_), channel_id=1, source_target_pairs={{0,2},{1,3},{2,0},{3,1},{4,6},{5,7},{6,4},{7,5},{8,10},{9,11},{10,... | collective-permute-start | bytes 24584 | tf_op jit(solution)/shard_map/ppermute | solution.py:360
  74.3 17.9 %collective-permute-start.17 = (bf16[512,256]{1,0:T(8,128)(2,1)S(1)}, bf16[512,256]{1,0:T(8,128)(2,1)S(1)}, u32[]{:S(2)}, u32[]{:S(2)}) collective-permute-start(bf16[512,256]{1,0:T(8,128)(2,1)S(1)} %get-tuple-element.119.hat_ref.rest_0_), channel_id=1, source_target_pairs={{0,1},{1,0},{2,3},{3,2},{4,5},{5,4},{6,7},{7,6},{8,9},{9,8},{10,11... | collective-permute-start | bytes 786440 | tf_op jit(solution)/shard_map/ppermute | solution.py:360
  74.3 17.8 %collective-permute-start.18 = (bf16[512,256]{1,0:T(8,128)(2,1)S(1)}, bf16[512,256]{1,0:T(8,128)(2,1)S(1)}, u32[]{:S(2)}, u32[]{:S(2)}) collective-permute-start(bf16[512,256]{1,0:T(8,128)(2,1)S(1)} %collective-permute-done.16.rest_1_), channel_id=1, source_target_pairs={{0,1},{1,0},{2,3},{3,2},{4,5},{5,4},{6,7},{7,6},{8,9},{9,8},{10,11... | collective-permute-start | bytes 786440 | tf_op jit(solution)/shard_map/ppermute | solution.py:360
  74.8 2.0 %collective-permute-start.12 = (bf16[16,256]{1,0:T(8,128)(2,1)S(1)}, bf16[16,256]{1,0:T(8,128)(2,1)S(1)}, u32[]{:S(2)}, u32[]{:S(2)}) collective-permute-start(bf16[16,256]{1,0:T(8,128)(2,1)S(1)} %get-tuple-element.123.rest_4_), channel_id=1, source_target_pairs={{0,1},{1,0},{2,3},{3,2},{4,5},{5,4},{6,7},{7,6},{8,9},{9,8},{10,11... | collective-permute-start | bytes 24584 | tf_op jit(solution)/shard_map/ppermute | solution.py:360
  74.9 2.8 %collective-permute-start.13 = (bf16[16,256]{1,0:T(8,128)(2,1)S(1)}, bf16[16,256]{1,0:T(8,128)(2,1)S(1)}, u32[]{:S(2)}, u32[]{:S(2)}) collective-permute-start(bf16[16,256]{1,0:T(8,128)(2,1)S(1)} %collective-permute-done.8.rest_5_), channel_id=1, source_target_pairs={{0,1},{1,0},{2,3},{3,2},{4,5},{5,4},{6,7},{7,6},{8,9},{9,8},{10,11... | collective-permute-start | bytes 24584 | tf_op jit(solution)/shard_map/ppermute | solution.py:360
  75.3 4.7 %collective-permute-start.10 = (bf16[128,256]{1,0:T(8,128)(2,1)S(1)}, bf16[128,256]{1,0:T(8,128)(2,1)S(1)}, u32[]{:S(2)}, u32[]{:S(2)}) collective-permute-start(bf16[128,256]{1,0:T(8,128)(2,1)S(1)} %get-tuple-element.104), channel_id=1, source_target_pairs={{0,16},{1,17},{2,18},{3,19},{16,0},{17,1},{18,2},{19,3},{4,20},{5,... | collective-permute-start | bytes 196616 | tf_op jit(solution)/shard_map/ppermute | solution.py:360
  76.8 5.2 %collective-permute-start.11 = (bf16[128,256]{1,0:T(8,128)(2,1)S(1)}, bf16[128,256]{1,0:T(8,128)(2,1)S(1)}, u32[]{:S(2)}, u32[]{:S(2)}) collective-permute-start(bf16[128,256]{1,0:T(8,128)(2,1)S(1)} %get-tuple-element.105), channel_id=1, source_target_pairs={{0,18},{1,19},{2,16},{3,17},{16,2},{17,3},{18,0},{19,1},{4,22},{5,... | collective-permute-start | bytes 196616 | tf_op jit(solution)/shard_map/ppermute | solution.py:360
  77.7 5.3 %collective-permute-start.9 = (bf16[128,256]{1,0:T(8,128)(2,1)S(1)}, bf16[128,256]{1,0:T(8,128)(2,1)S(1)}, u32[]{:S(2)}, u32[]{:S(2)}) collective-permute-start(bf16[128,256]{1,0:T(8,128)(2,1)S(1)} %get-tuple-element.103), channel_id=1, source_target_pairs={{0,2},{1,3},{2,0},{3,1},{16,18},{17,19},{18,16},{19,17},{4,6},{5,7... | collective-permute-start | bytes 196616 | tf_op jit(solution)/shard_map/ppermute | solution.py:360
  83.0 5.2 %collective-permute-start.14 = (bf16[128,256]{1,0:T(8,128)(2,1)S(1)}, bf16[128,256]{1,0:T(8,128)(2,1)S(1)}, u32[]{:S(2)}, u32[]{:S(2)}) collective-permute-start(bf16[128,256]{1,0:T(8,128)(2,1)S(1)} %plane_sum.1.refs_0_), channel_id=1, source_target_pairs={{0,4},{4,0},{8,12},{12,8},{1,5},{5,1},{9,13},{13,9},{2,6},{6,2},{1... | collective-permute-start | bytes 196616 | tf_op jit(solution)/shard_map/ppermute | solution.py:360
  88.2 7.8 %collective-permute-start.15 = (bf16[128,256]{1,0:T(8,128)(2,1)S(1)}, bf16[128,256]{1,0:T(8,128)(2,1)S(1)}, u32[]{:S(2)}, u32[]{:S(2)}) collective-permute-start(bf16[128,256]{1,0:T(8,128)(2,1)S(1)} %seq_sum_1.1.refs_0_), channel_id=1, source_target_pairs={{0,8},{4,12},{8,0},{12,4},{1,9},{5,13},{9,1},{13,5},{2,10},{6,14},... | collective-permute-start | bytes 196616 | tf_op jit(solution)/shard_map/ppermute | solution.py:360
  95.9 7.2 %collective-permute-start.19 = (bf16[144,1024]{1,0:T(8,128)(2,1)S(1)}, bf16[144,1024]{1,0:T(8,128)(2,1)S(1)}, u32[]{:S(2)}, u32[]{:S(2)}) collective-permute-start(bf16[144,1024]{1,0:T(8,128)(2,1)S(1)} %get-tuple-element.129), channel_id=1, source_target_pairs={{0,4},{4,0},{8,12},{12,8},{1,5},{5,1},{9,13},{13,9},{2,6},{6,2},{1... | collective-permute-start | bytes 884744 | tf_op jit(solution)/shard_map/ppermute | solution.py:360
  96.0 7.2 %collective-permute-start.21 = (bf16[128,256]{1,0:T(8,128)(2,1)S(1)}, bf16[128,256]{1,0:T(8,128)(2,1)S(1)}, u32[]{:S(2)}, u32[]{:S(2)}) collective-permute-start(bf16[128,256]{1,0:T(8,128)(2,1)S(1)} %seq_sum_2.1.refs_0_), channel_id=1, source_target_pairs={{0,2},{1,3},{2,0},{3,1},{16,18},{17,19},{18,16},{19,17},{4,6},{5,7... | collective-permute-start | bytes 196616 | tf_op jit(solution)/shard_map/ppermute | solution.py:360
  97.0 6.2 %collective-permute-start.22 = (bf16[128,256]{1,0:T(8,128)(2,1)S(1)}, bf16[128,256]{1,0:T(8,128)(2,1)S(1)}, u32[]{:S(2)}, u32[]{:S(2)}) collective-permute-start(bf16[128,256]{1,0:T(8,128)(2,1)S(1)} %seq_sum_2.1.refs_0_), channel_id=1, source_target_pairs={{0,16},{1,17},{2,18},{3,19},{16,0},{17,1},{18,2},{19,3},{4,20},{5,... | collective-permute-start | bytes 196616 | tf_op jit(solution)/shard_map/ppermute | solution.py:360
  98.1 5.2 %collective-permute-start.23 = (bf16[128,256]{1,0:T(8,128)(2,1)S(1)}, bf16[128,256]{1,0:T(8,128)(2,1)S(1)}, u32[]{:S(2)}, u32[]{:S(2)}) collective-permute-start(bf16[128,256]{1,0:T(8,128)(2,1)S(1)} %seq_sum_2.1.refs_0_), channel_id=1, source_target_pairs={{0,18},{1,19},{2,16},{3,17},{16,2},{17,3},{18,0},{19,1},{4,22},{5,... | collective-permute-start | bytes 196616 | tf_op jit(solution)/shard_map/ppermute | solution.py:360
  103.9 10.4 %collective-permute-start.24 = (bf16[512,256]{1,0:T(8,128)(2,1)S(1)}, bf16[512,256]{1,0:T(8,128)(2,1)S(1)}, u32[]{:S(2)}, u32[]{:S(2)}) collective-permute-start(bf16[512,256]{1,0:T(8,128)(2,1)S(1)} %lay_half.1.refs_0_), channel_id=1, source_target_pairs={{0,1},{1,0},{2,3},{3,2},{16,17},{17,16},{18,19},{19,18},{4,5},{5,4... | collective-permute-start | bytes 786440 | tf_op jit(solution)/shard_map/ppermute | solution.py:360
  103.9 9.6 %collective-permute-start.20 = (bf16[64,1024]{1,0:T(8,128)(2,1)S(1)}, bf16[64,1024]{1,0:T(8,128)(2,1)S(1)}, u32[]{:S(2)}, u32[]{:S(2)}) collective-permute-start(bf16[64,1024]{1,0:T(8,128)(2,1)S(1)} %get-tuple-element.134), channel_id=1, source_target_pairs={{0,8},{4,12},{8,0},{12,4},{1,9},{5,13},{9,1},{13,5},{2,10},{6,14},... | collective-permute-start | bytes 393224 | tf_op jit(solution)/shard_map/ppermute | solution.py:360
  (4 other events, 9.2 us)

commit v3 on v2

--- a/solution.py
+++ b/solution.py
@@ -258,38 +258,33 @@
     return pl.ds(pl.multiple_of(index * rows, rows), rows)
 
 
-def halved_kernel(info_ref, keep_ref, got_ref, own_ref, *rest):
+def halved_kernel(chip, info_ref, keep_ref, got_ref, message_ref, own_ref, *rest):
     *send_refs, sum_ref = rest
     rows = own_ref.shape[0]
     sum_ref[...] = keep_ref[...] + got_ref[...].astype(F32)
     own_ref[...] = sum_ref[part_at(info_ref[4], rows), :]
     for r, send_ref in enumerate(send_refs, 1):
-        send_ref[...] = sum_ref[part_at(lax.bitwise_xor(info_ref[4], r), rows), :].astype(BF16)
+        send_ref[:rows, :] = sum_ref[part_at(lax.bitwise_xor(info_ref[4], r), rows), :].astype(BF16)
+        if r == chip:
+            send_ref[rows:, :] = message_ref[...]
 
 
 def sum_kernel(*refs):
-    parts = [ref[...].astype(F32) for ref in refs[:-1]]
+    rows = refs[0].shape[0]
+    parts = [ref[:rows, :].astype(F32) for ref in refs[:-1]]
     while len(parts) > 1:
         parts = [a + b for a, b in zip(parts[::2], parts[1::2])]
     refs[-1][...] = parts[0].astype(refs[-1].dtype)
 
 
-def lay_kernel(slot, info_ref, *refs):
+def lay_kernel(info_ref, *refs):
     *part_refs, out_ref = refs
     rows = part_refs[0].shape[0]
-    for r, part_ref in enumerate(part_refs):
-        at = part_at(lax.bitwise_xor(info_ref[slot], r), rows)
-        out_ref[at, :] = part_ref[...].astype(out_ref.dtype)
-
-
-def cut_blocks(values, keep_ref, send_ref, rows):
-    for i in range(values.shape[0] // rows):
-        to_ref = send_ref if i % 2 else keep_ref
-        to_ref[i // 2 * rows : (i // 2 + 1) * rows, :] = values[i * rows : (i + 1) * rows, :].astype(to_ref.dtype)
-
-
-def halving_kernel(rows, keep_ref, got_ref, next_keep_ref, next_send_ref):
-    cut_blocks(keep_ref[...] + got_ref[: keep_ref.shape[0], :].astype(F32), next_keep_ref, next_send_ref, rows)
+    chips = len(part_refs) // 2
+    for i, part_ref in enumerate(part_refs):
+        core, r = divmod(i, chips)
+        at = lax.bitwise_xor(info_ref[3], core) * chips + lax.bitwise_xor(info_ref[4], r)
+        out_ref[part_at(at, rows), :] = part_ref[...].astype(out_ref.dtype)
 
 
 def loss_kernel(last, info_ref, loss_ref, got_ref, own_loss_ref):
@@ -299,9 +294,9 @@
     own_loss_ref[...] = jnp.where(info_ref[2] == last, above, loss_ref[...])
 
 
-def negative_kernel(seq_count, info_ref, neg_ref, neg_id_ref, loss_ref, *rest):
-    *gathered, keep_ref, send_ref, turned_ref, sum_ref, weight_ref = rest
-    pool_count = len(gathered) // 2
+def negative_kernel(pool_count, info_ref, neg_ref, neg_id_ref, loss_ref, *rest):
+    gathered, rest = rest[: 2 * pool_count], rest[2 * pool_count :]
+    own_ref, *send_refs, turned_ref, sum_ref, weight_ref = rest
     count, embed = neg_ref.shape
     rows = embed
     blocks = gathered[0].shape[0] // rows
@@ -313,7 +308,7 @@
     id_row = neg_id_ref[...].astype(F32)
     neg_id = column(id_row)
     for i, (hats_ref, message_ref) in enumerate(zip(gathered[:pool_count], gathered[pool_count:])):
-        parts = message_ref[...].astype(F32)
+        parts = message_ref[message_ref.shape[0] - 16 :, :].astype(F32)
         for block, start in itertools.product(range(blocks), range(0, count, tile)):
             own = slice(block * rows, (block + 1) * rows)
             cut = slice(start, start + tile)
@@ -328,19 +323,17 @@
     neg_sum = sum_ref[...] * column(jnp.exp2(-LOG2E * log_sample_chance(id_row)) / SOFTMAX_WARMTH)
     grad = (neg_sum - unit * jnp.sum(unit * neg_sum, axis=-1, keepdims=True)) / norms
     turned_ref[...] = grad.T
-    kept = keep_ref.shape[0]
-    cols = kept // (seq_count // 2)
-    for r in range(seq_count):
-        at = part_at(lax.bitwise_xor(info_ref[2], r), cols)
-        to_ref = send_ref if r % 2 else keep_ref
-        to_ref[r // 2 * cols : (r // 2 + 1) * cols, :] = turned_ref[at, :].astype(to_ref.dtype)
+    cols = own_ref.shape[0]
+    own_ref[...] = turned_ref[part_at(info_ref[2], cols), :]
+    for r, send_ref in enumerate(send_refs, 1):
+        send_ref[:cols, :] = turned_ref[part_at(lax.bitwise_xor(info_ref[2], r), cols), :].astype(BF16)
     parts = split3(loss_ref[...])
     pad = jnp.zeros((16 - len(parts), loss_ref.shape[1]), F32)
-    send_ref[kept:, :] = jnp.zeros((16, count), BF16)
-    send_ref[kept:, : loss_ref.shape[1]] = jnp.concatenate(parts + [pad], axis=0).astype(BF16)
-
-
-def call(kernel, ins, outs, scratch=(), limit=24, flops=0, moved=0, name=None, place=pltpu.VMEM):
+    send_refs[0][cols:, :] = jnp.zeros((16, count), BF16)
+    send_refs[0][cols:, : loss_ref.shape[1]] = jnp.concatenate(parts + [pad], axis=0).astype(BF16)
+
+
+def call(kernel, ins, outs, scratch=(), limit=24, micros=0.5, name=None, place=pltpu.VMEM):
     in_specs = [pl.BlockSpec(memory_space=pltpu.SMEM if x.ndim == 1 else place) for x in ins]
     many = isinstance(outs, (list, tuple))
     out_specs = jax.tree.map(lambda _: pl.BlockSpec(memory_space=pltpu.VMEM), outs)
@@ -351,7 +344,7 @@
         out_specs=list(out_specs) if many else out_specs,
         scratch_shapes=list(scratch),
         compiler_params=pltpu.CompilerParams(vmem_limit_bytes=limit * MIB),
-        cost_estimate=pl.CostEstimate(flops=flops, bytes_accessed=moved, transcendentals=0),
+        cost_estimate=pl.CostEstimate(flops=int(micros * 5.75e8), bytes_accessed=0, transcendentals=0),
         name=name,
     )(*ins)
 
@@ -402,7 +395,7 @@
         scratch=[pltpu.VMEM((rows, width), BF16), pltpu.VMEM((4, width, width), BF16), pltpu.SemaphoreType.DMA((5,))],
         place=pl.ANY,
         limit=44,
-        name="own_block",
+        micros=6, name="own_block",
     )
     table_part, pos_part = call(
         table_kernel,
@@ -417,7 +410,7 @@
         ],
         place=pl.ANY,
         limit=24,
-        name="table_part",
+        micros=0.6, name="table_part",
     )
     table_part, pos_part, acc = together(table_part, pos_part, acc)
     table = gather_step([table_part], "pool", pool_count)
@@ -432,13 +425,13 @@
                 [info, guest, w_in, keys, values, own, gate, queries, acc],
                 [tall, tall, tall, tall_wide],
                 scratch=[pltpu.VMEM((rows, width), BF16)] * 2,
-                name="guest_block",
+                micros=4.8, name="guest_block",
             )
         acc = call(
             functools.partial(step_kernel, step * rows),
             [info, block, w_in, queries, acc],
             tall_wide,
-            name=f"earlier_block_{step}",
+            micros=3.6, name=f"earlier_block_{step}",
         )
         acc, table, pos_part = together(acc, table, pos_part)
         if step == 1:
@@ -452,7 +445,7 @@
         [info, block, w_in, queries, acc, gate, own, w_out, w_proj],
         [tall, struct((2 * rows, embed), F32), struct((2 * rows, embed), BF16)],
         scratch=[pltpu.VMEM((2 * rows, width), F32)],
-        name="last_block",
+        micros=6, name="last_block",
     )
     hats = gather_step([hat], "pool", pool_count)
 
@@ -465,69 +458,60 @@
             struct((half, embed), F32), struct((half, embed), BF16),
         ],
         scratch=[pltpu.VMEM((width, embed), F32), pltpu.VMEM((2 * rows, local_neg), BF16)],
-        name="head",
+        micros=5, name="head",
     )
     part = struct((half // chips, embed), BF16)
     cols = embed // seq_count
     def plane_swap(parts):
         return [swap(x, plane, plane_count, 2 * r) for r, x in enumerate(parts, 1)]
 
-    got, messages = together(swap(send, plane, plane_count, 1), gather_step([message], "pool", pool_count))
+    chip = pool_count // 4
+    sizes = [part.shape[0] + 16 * (r == chip) for r in range(1, chips)]
     own_part, *sends = call(
-        halved_kernel,
-        [info, keep, got],
-        [struct(part.shape, F32)] + [part] * (chips - 1),
+        functools.partial(halved_kernel, chip),
+        [info, keep, swap(send, plane, plane_count, 1), message],
+        [struct(part.shape, F32)] + [struct((size, embed), BF16) for size in sizes],
         scratch=[pltpu.VMEM((half, embed), F32)],
-        name="halved",
-    )
-    hats, _ = together(hats, own_part)
+        micros=0.6, name="halved",
+    )
+    proj_parts = plane_swap(sends)
+    proj_part = call(sum_kernel, [own_part] + proj_parts, part, name="plane_sum")
     while len(hats) < pool_count:
         hats = gather_step(hats, "pool", pool_count)
+    messages = [message, proj_parts[chip - 1]]
     while len(messages) < pool_count:
         messages = gather_step(messages, "pool", pool_count)
-    proj_parts, messages = together([own_part] + plane_swap(sends), messages)
-    proj_part = call(sum_kernel, proj_parts, part, name="plane_sum")
-    bit = 1
-    while 2 * bit < seq_count:
-        got = swap(proj_part, "seq", seq_count, bit)
-        proj_part = call(sum_kernel, [proj_part, got], part, name=f"seq_sum_{bit}")
-        bit *= 2
     hats, messages, _ = together(hats, messages, proj_part)
-    keep, send = call(
-        functools.partial(negative_kernel, seq_count),
+    d_part, *sends = call(
+        functools.partial(negative_kernel, pool_count),
         [info, neg_embed[0], neg_ids, guest_loss, *hats, *messages],
-        [struct((embed // 2, local_neg), F32), struct((embed // 2 + 16, local_neg), BF16)],
+        [struct((cols, local_neg), F32)]
+        + [struct((cols + 16 * (r == 1), local_neg), BF16) for r in range(1, seq_count)],
         scratch=[
             pltpu.VMEM((embed, local_neg), F32), pltpu.VMEM((local_neg, embed), F32),
             pltpu.VMEM((local_neg, 2 * rows), BF16),
         ],
-        name="neg_grad",
-    )
-    got, keep, send = together(swap(proj_part, "seq", seq_count, bit), keep, send)
-    proj_part = call(sum_kernel, [proj_part, got], part, name=f"seq_sum_{bit}")
-    got = swap(send, "seq", seq_count, 1)
-    got, _ = together(got, proj_part)
-    loss = call(functools.partial(loss_kernel, seq_count - 1), [info, loss, got], struct((1, rows), F32), name="loss")
+        micros=3.7, name="neg_grad",
+    )
+    got = swap(proj_part, "seq", seq_count, 1)
+    got, sends = together(got, sends)
+    proj_part = call(sum_kernel, [proj_part, got], part, name="seq_sum_1")
     bit = 2
     while bit < seq_count:
-        size = keep.shape[0] // 2
-        keep, send = call(
-            functools.partial(halving_kernel, cols),
-            [keep, got],
-            [struct((size, local_neg), F32), struct((size, local_neg), BF16)],
-            name=f"neg_halved_{bit}",
+        proj_part = call(
+            sum_kernel, [proj_part, swap(proj_part, "seq", seq_count, bit)], part, name=f"seq_sum_{bit}"
         )
-        got = swap(send, "seq", seq_count, bit)
         bit *= 2
-    proj_parts, send = together([proj_part] + plane_swap([proj_part] * (chips - 1)), send)
-    proj_half = call(
-        functools.partial(lay_kernel, 4), [info, *proj_parts], struct((half, embed), BF16), name="lay_half"
-    )
-    other_half = swap(proj_half, plane, plane_count, 1)
-    d_neg = call(sum_kernel, [keep, got], struct((cols, local_neg), F32), name="neg_sum")
-    d_proj = call(
-        functools.partial(lay_kernel, 3), [info, proj_half, other_half], struct((width, embed), F32), name="lay_whole"
-    )
+    gots = [swap(x, "seq", seq_count, r) for r, x in enumerate(sends, 1)]
+    others, gots = together(plane_swap([proj_part] * (chips - 1)), gots)
+    proj_parts = [proj_part] + others
+    proj_parts += [swap(x, plane, plane_count, 1) for x in proj_parts]
+    d_proj = call(lay_kernel, [info, *proj_parts], struct((width, embed), F32), micros=0, name="lay_whole")
+    loss = call(
+        functools.partial(loss_kernel, seq_count - 1), [info, loss, gots[0]], struct((1, rows), F32),
+        micros=1, name="loss",
+    )
+    d_neg = call(sum_kernel, [d_part, *gots], struct((cols, local_neg), F32), micros=0.7, name="neg_sum")
     return (loss, d_neg.T[None], d_proj)
 
 

time: 116 us -> 85.2 us (0.73)
  waiting for transfers between devices: 44.2 us -> 14.6 us
  starting transfers between devices: 32.1 us -> 29.3 us
  local copies, waits for them, and re-layouts: 3.11 us -> 4.47 us
    ppermute x1, waiting for transfers between devices: 10.2 us -> 0.01 us  [body(): block = lax.ppermute(own, 'seq', up)]
    ppermute x1, waiting for transfers between devices: 10.5 us -> 0.49 us  [body(): following = lax.ppermute(block, 'seq', up)]
    ppermute x21 -> x24, waiting for transfers between devices: 23.6 us -> 14.1 us  [swap(): return lax.ppermute(x, axis, [(i, i ^ r) for i in range(count)])]
    ppermute x21 -> x24, starting transfers between devices: 22.7 us -> 19.3 us  [swap(): return lax.ppermute(x, axis, [(i, i ^ r) for i in range(count)])]
    ppermute x1, starting transfers between devices: 3.5 us -> 4.96 us  [body(): block = lax.ppermute(own, 'seq', up)]
    unnamed x22 -> x24, local copies, waits for them, and re-layouts: 3.02 us -> 4.38 us
    pallas_call x16 -> x14, Pallas kernels: 34.8 us -> 34.2 us  [call(): pl.pallas_call(kernel, out_shape=list(outs) if many else outs, in_specs=i...]
  transfers between devices with their start and end apart: 25 -> 28, of which waited for: 9 -> 10; matrix products, arithmetic and copies ran while one was open for 0% -> 0% of each run, Pallas kernels for 18% -> 39%
where the time goes in v3:
time: 85.2 us; the launch traced here: 84.1 us
  Pallas kernels  34.2 us (40%)
  starting transfers between devices  29.3 us (34%)
  waiting for transfers between devices  14.6 us (17%)
  local copies, waits for them, and re-layouts  4.47 us (5%)
  between operations  1.56 us (2%)
    pallas_call x14, Pallas kernels, call(): pl.pallas_call(kernel, out_shape=list(outs) if many else outs, in_specs=i...  34.2 us
    ppermute x24, starting transfers between devices, swap(): return lax.ppermute(x, axis, [(i, i ^ r) for i in range(count)])  19.3 us
    ppermute x24, waiting for transfers between devices, swap(): return lax.ppermute(x, axis, [(i, i ^ r) for i in range(count)])  14.1 us
    ppermute x1, starting transfers between devices, body(): block = lax.ppermute(own, 'seq', up)  4.96 us
    unnamed x24, local copies, waits for them, and re-layouts  4.38 us
    ppermute x1, starting transfers between devices, body(): following = lax.ppermute(block, 'seq', up)  3.47 us
  transfers between devices with their start and end apart: 28, of which 10 were waited for; matrix products, arithmetic and copies ran while one was open for 0% of the time, Pallas kernels for 39%

profile of v3, /device:TPU:0, one launch (start us, length us, event | category | flops | bytes accessed | tf_op | source)
XLA Modules:
  0.0 84.1 jit_solution(1573788187966186496)
XLA Ops:
  0.6 5.0 %collective-permute-start = (bf16[256,1024]{1,0:T(8,128)(2,1)}, bf16[256,1024]{1,0:T(8,128)(2,1)S(1)}, u32[]{:S(2)}, u32[]{:S(2)}) collective-permute-start(bf16[256,1024]{1,0:T(8,128)(2,1)} %bitcast.15), channel_id=1, source_target_pairs={{0,4},{4,8},{1,5},{5,9},{2,6},{6,10},{3,7},{7,11},{16,20},{20,24},... | collective-permute-start | bytes 1572872 | tf_op jit(solution)/shard_map/ppermute | solution.py:387
  7.1 1.0 %copy-done.5 = bf16[1,1024,256]{2,1,0:T(8,128)(2,1)S(1)} copy-done((bf16[1,1024,256]{2,1,0:T(8,128)(2,1)S(1)}, bf16[1,1024,256]{2,1,0:T(8,128)(2,1)}, u32[]{:S(2)}) %copy-start.5) | copy-done | bytes 524312
  8.1 0.9 %copy-done.7 = bf16[1,256,256]{2,1,0:T(8,128)(2,1)S(1)} copy-done((bf16[1,256,256]{2,1,0:T(8,128)(2,1)S(1)}, bf16[1,256,256]{2,1,0:T(8,128)(2,1)}, u32[]{:S(2)}) %copy-start.7) | copy-done | bytes 131096
  11.0 1.0 %copy-done.2 = bf16[1,256,1024]{2,1,0:T(8,128)(2,1)S(1)} copy-done((bf16[1,256,1024]{2,1,0:T(8,128)(2,1)S(1)}, bf16[1,256,1024]{2,1,0:T(8,128)(2,1)}, u32[]{:S(2)}) %copy-start.2) | copy-done | bytes 524312
  12.0 6.3 %own_block.1 = (bf16[256,1024]{1,0:T(8,128)(2,1)S(1)}, bf16[256,1024]{1,0:T(8,128)(2,1)S(1)}, bf16[256,1024]{1,0:T(8,128)(2,1)S(1)}, bf16[256,1024]{1,0:T(8,128)(2,1)S(1)}, f32[256,1024]{1,0:T(8,128)S(1)}) custom-call(s32[7]{0:T(128)S(1)} %stack.27.info_ref, bf16[256,1024]{1,0:T(8,128)(2,1)S(1)} %bitcast.17, bf16[1024,4096]{1,0:T(8,128)(2,1)} %w_ref.5), custom_call_target="tpu_custom_call" | custom-call | flops 3449999872 | tf_op jit(solution)/shard_map/own_block/pallas_call | solution.py:340
  18.3 1.6 %collective-permute-start.3 = (bf16[1056,256]{1,0:T(8,128)(2,1)S(1)}, bf16[1056,256]{1,0:T(8,128)(2,1)S(1)}, u32[]{:S(2)}, u32[]{:S(2)}) collective-permute-start(bf16[1056,256]{1,0:T(8,128)(2,1)S(1)} %get-tuple-element.84.rest_0_), channel_id=1, source_target_pairs={{0,2},{1,3},{2,0},{3,1},{4,6},{5,7},{6,4},{7,5},{8,10},{9,11},{10,... | collective-permute-start | bytes 1622024 | tf_op jit(solution)/shard_map/ppermute | solution.py:353
  19.9 3.5 %collective-permute-start.2 = (bf16[256,1024]{1,0:T(8,128)(2,1)S(1)}, bf16[256,1024]{1,0:T(8,128)(2,1)S(1)}, u32[]{:S(2)}, u32[]{:S(2)}) collective-permute-start(bf16[256,1024]{1,0:T(8,128)(2,1)S(1)} %collective-permute-done.x_ref), channel_id=1, source_target_pairs={{0,4},{4,8},{1,5},{5,9},{2,6},{6,10},{3,7},{7,11},{16,20},{20,24},... | collective-permute-start | bytes 1572872 | tf_op jit(solution)/shard_map/ppermute | solution.py:421
  23.4 4.8 %guest_block.1 = (bf16[512,1024]{1,0:T(8,128)(2,1)S(1)}, bf16[512,1024]{1,0:T(8,128)(2,1)S(1)}, bf16[512,1024]{1,0:T(8,128)(2,1)S(1)}, f32[512,1024]{1,0:T(8,128)S(1)}) custom-call(s32[7]{0:T(128)S(1)} %stack.27.info_ref, bf16[256,1024]{1,0:T(8,128)(2,1)S(1)} %collective-permute-done.1.x_ref, bf16[1024,4096]{1,0:T(8,128)(2,1)S(1)} %copy-done, ...), custom_call_target="tpu_custom_call" | custom-call | flops 2760000000 | tf_op jit(solution)/shard_map/guest_block/pallas_call | solution.py:340
  28.2 3.6 %earlier_block_1.1.before_ref = f32[512,1024]{1,0:T(8,128)S(1)} custom-call(s32[7]{0:T(128)S(1)} %stack.27.info_ref, bf16[256,1024]{1,0:T(8,128)(2,1)S(1)} %collective-permute-done.x_ref, bf16[1024,4096]{1,0:T(8,128)(2,1)S(1)} %copy-done, bf16[512,1024]{1,0:T(8,128)(2,1)S(1)} %get-tuple-element.71.q_ref, f32[512,1024]{1,0:T(8,128)S(1)} %get-tuple-element.72.before_ref), custom_call_target="tpu_custom_call" | custom-call | flops 2070000000 | tf_op jit(solution)/shard_map/earlier_block_1/pallas_call | solution.py:340
  32.6 0.8 collective-permute-start.4
  33.9 6.2 %last_block.1 = (bf16[512,1024]{1,0:T(8,128)(2,1)S(1)}, f32[512,256]{1,0:T(8,128)S(1)}, bf16[512,256]{1,0:T(8,128)(2,1)S(1)}) custom-call(s32[7]{0:T(128)S(1)} %stack.27.info_ref, bf16[256,1024]{1,0:T(8,128)(2,1)S(1)} %collective-permute-done.2.x_ref, bf16[1024,4096]{1,0:T(8,128)(2,1)S(1)} %copy-done, bf16[512,1024]{1,0:T(8,128)(2,1)S(1)} %get-tuple-element.71.q_ref, ...), custom_call_target="tpu_custom_call" | custom-call | flops 3449999872 | tf_op jit(solution)/shard_map/last_block/pallas_call | solution.py:340
  40.1 1.1 %collective-permute-start.12 = (bf16[512,256]{1,0:T(8,128)(2,1)S(1)}, bf16[512,256]{1,0:T(8,128)(2,1)S(1)}, u32[]{:S(2)}, u32[]{:S(2)}) collective-permute-start(bf16[512,256]{1,0:T(8,128)(2,1)S(1)} %get-tuple-element.95.hat_ref.rest_0_), channel_id=1, source_target_pairs={{0,2},{1,3},{2,0},{3,1},{4,6},{5,7},{6,4},{7,5},{8,10},{9,11},{10,... | collective-permute-start | bytes 786440 | tf_op jit(solution)/shard_map/ppermute | solution.py:353
  41.3 4.9 %head.1 = (f32[1,256]{1,0:T(1,128)S(1)}, f32[1,256]{1,0:T(1,128)S(1)}, bf16[16,256]{1,0:T(8,128)(2,1)S(1)}, f32[512,256]{1,0:T(8,128)S(1)}, bf16[512,256]{1,0:T(8,128)(2,1)S(1)}) custom-call(s32[7]{0:T(128)S(1)} %stack.27.info_ref, bf16[512,256]{1,0:T(8,128)(2,1)S(1)} %get-tuple-element.95.hat_ref.rest_0_, f32[512,256]{1,0:T(8,128)S(1)} %get-tuple-element.81.out_ref, ...), custom_call_target="tpu_custom_call" | custom-call | flops 2875000064 | tf_op jit(solution)/shard_map/head/pallas_call | solution.py:340
  46.8 1.2 %collective-permute-done.12.rest_1_ = bf16[512,256]{1,0:T(8,128)(2,1)S(1)} collective-permute-done((bf16[512,256]{1,0:T(8,128)(2,1)S(1)}, bf16[512,256]{1,0:T(8,128)(2,1)S(1)}, u32[]{:S(2)}, u32[]{:S(2)}) %collective-permute-start.12) | collective-permute-done | bytes 262176 | tf_op jit(solution)/shard_map/ppermute | solution.py:353
  48.6 1.6 %collective-permute-start.8 = (bf16[144,256]{1,0:T(8,128)(2,1)S(1)}, bf16[144,256]{1,0:T(8,128)(2,1)S(1)}, u32[]{:S(2)}, u32[]{:S(2)}) collective-permute-start(bf16[144,256]{1,0:T(8,128)(2,1)S(1)} %get-tuple-element.91), channel_id=1, source_target_pairs={{0,2},{1,3},{2,0},{3,1},{16,18},{17,19},{18,16},{19,17},{4,6},{5,7... | collective-permute-start | bytes 221192 | tf_op jit(solution)/shard_map/ppermute | solution.py:353
  50.2 1.4 %collective-permute-start.10 = (bf16[128,256]{1,0:T(8,128)(2,1)S(1)}, bf16[128,256]{1,0:T(8,128)(2,1)S(1)}, u32[]{:S(2)}, u32[]{:S(2)}) collective-permute-start(bf16[128,256]{1,0:T(8,128)(2,1)S(1)} %get-tuple-element.93), channel_id=1, source_target_pairs={{0,18},{1,19},{2,16},{3,17},{16,2},{17,3},{18,0},{19,1},{4,22},{5,... | collective-permute-start | bytes 196616 | tf_op jit(solution)/shard_map/ppermute | solution.py:353
  52.1 1.6 %collective-permute-done.8.refs_1_.rest_5_ = bf16[144,256]{1,0:T(8,128)(2,1)S(1)} collective-permute-done((bf16[144,256]{1,0:T(8,128)(2,1)S(1)}, bf16[144,256]{1,0:T(8,128)(2,1)S(1)}, u32[]{:S(2)}, u32[]{:S(2)}) %collective-permute-start.8) | collective-permute-done | bytes 73760 | tf_op jit(solution)/shard_map/ppermute | solution.py:353
  53.7 1.9 %collective-permute-done.10.refs_3_ = bf16[128,256]{1,0:T(8,128)(2,1)S(1)} collective-permute-done((bf16[128,256]{1,0:T(8,128)(2,1)S(1)}, bf16[128,256]{1,0:T(8,128)(2,1)S(1)}, u32[]{:S(2)}, u32[]{:S(2)}) %collective-permute-start.10) | collective-permute-done | bytes 65568 | tf_op jit(solution)/shard_map/ppermute | solution.py:353
  55.9 1.8 %collective-permute-start.11 = (bf16[128,256]{1,0:T(8,128)(2,1)S(1)}, bf16[128,256]{1,0:T(8,128)(2,1)S(1)}, u32[]{:S(2)}, u32[]{:S(2)}) collective-permute-start(bf16[128,256]{1,0:T(8,128)(2,1)S(1)} %plane_sum.1.refs_0_), channel_id=1, source_target_pairs={{0,4},{4,0},{8,12},{12,8},{1,5},{5,1},{9,13},{13,9},{2,6},{6,2},{1... | collective-permute-start | bytes 196616 | tf_op jit(solution)/shard_map/ppermute | solution.py:353
  57.8 3.7 %neg_grad.1 = (f32[64,1024]{1,0:T(8,128)S(1)}, bf16[80,1024]{1,0:T(8,128)(2,1)S(1)}, bf16[64,1024]{1,0:T(8,128)(2,1)S(1)}, bf16[64,1024]{1,0:T(8,128)(2,1)S(1)}) custom-call(s32[7]{0:T(128)S(1)} %stack.27.info_ref, bf16[1024,256]{1,0:T(8,128)(2,1)S(1)} %bitcast.20, s32[1,1024]{1,0:T(1,128)S(1)} %copy-done.10, f32[1,256]{1,0:T(1,128)S(1)} %get-tuple-element.94.loss_ref, ...), custom_call_target="tpu_custom_call" | custom-call | flops 2127500032 | tf_op jit(solution)/shard_map/neg_grad/pallas_call | solution.py:340
  61.5 2.7 %collective-permute-start.17 = (bf16[128,256]{1,0:T(8,128)(2,1)S(1)}, bf16[128,256]{1,0:T(8,128)(2,1)S(1)}, u32[]{:S(2)}, u32[]{:S(2)}) collective-permute-start(bf16[128,256]{1,0:T(8,128)(2,1)S(1)} %seq_sum_1.1.refs_0_), channel_id=1, source_target_pairs={{0,8},{4,12},{8,0},{12,4},{1,9},{5,13},{9,1},{13,5},{2,10},{6,14},... | collective-permute-start | bytes 196616 | tf_op jit(solution)/shard_map/ppermute | solution.py:353
  64.9 3.2 %collective-permute-done.17.refs_1_ = bf16[128,256]{1,0:T(8,128)(2,1)S(1)} collective-permute-done((bf16[128,256]{1,0:T(8,128)(2,1)S(1)}, bf16[128,256]{1,0:T(8,128)(2,1)S(1)}, u32[]{:S(2)}, u32[]{:S(2)}) %collective-permute-start.17) | collective-permute-done | bytes 65568 | tf_op jit(solution)/shard_map/ppermute | solution.py:353
  68.2 0.9 %collective-permute-start.18 = (bf16[128,256]{1,0:T(8,128)(2,1)S(1)}, bf16[128,256]{1,0:T(8,128)(2,1)S(1)}, u32[]{:S(2)}, u32[]{:S(2)}) collective-permute-start(bf16[128,256]{1,0:T(8,128)(2,1)S(1)} %seq_sum_2.1.refs_0_), channel_id=1, source_target_pairs={{0,2},{1,3},{2,0},{3,1},{16,18},{17,19},{18,16},{19,17},{4,6},{5,7... | collective-permute-start | bytes 196616 | tf_op jit(solution)/shard_map/ppermute | solution.py:353
  69.1 2.5 %collective-permute-start.22 = (bf16[64,1024]{1,0:T(8,128)(2,1)S(1)}, bf16[64,1024]{1,0:T(8,128)(2,1)S(1)}, u32[]{:S(2)}, u32[]{:S(2)}) collective-permute-start(bf16[64,1024]{1,0:T(8,128)(2,1)S(1)} %get-tuple-element.108), channel_id=1, source_target_pairs={{0,8},{4,12},{8,0},{12,4},{1,9},{5,13},{9,1},{13,5},{2,10},{6,14},... | collective-permute-start | bytes 393224 | tf_op jit(solution)/shard_map/ppermute | solution.py:353
  71.9 1.1 %collective-permute-start.19 = (bf16[128,256]{1,0:T(8,128)(2,1)S(1)}, bf16[128,256]{1,0:T(8,128)(2,1)S(1)}, u32[]{:S(2)}, u32[]{:S(2)}) collective-permute-start(bf16[128,256]{1,0:T(8,128)(2,1)S(1)} %seq_sum_2.1.refs_0_), channel_id=1, source_target_pairs={{0,16},{1,17},{2,18},{3,19},{16,0},{17,1},{18,2},{19,3},{4,20},{5,... | collective-permute-start | bytes 196616 | tf_op jit(solution)/shard_map/ppermute | solution.py:353
  73.1 1.3 %collective-permute-start.20 = (bf16[128,256]{1,0:T(8,128)(2,1)S(1)}, bf16[128,256]{1,0:T(8,128)(2,1)S(1)}, u32[]{:S(2)}, u32[]{:S(2)}) collective-permute-start(bf16[128,256]{1,0:T(8,128)(2,1)S(1)} %seq_sum_2.1.refs_0_), channel_id=1, source_target_pairs={{0,18},{1,19},{2,16},{3,17},{16,2},{17,3},{18,0},{19,1},{4,22},{5,... | collective-permute-start | bytes 196616 | tf_op jit(solution)/shard_map/ppermute | solution.py:353
  74.4 2.2 %collective-permute-done.19.refs_2_ = bf16[128,256]{1,0:T(8,128)(2,1)S(1)} collective-permute-done((bf16[128,256]{1,0:T(8,128)(2,1)S(1)}, bf16[128,256]{1,0:T(8,128)(2,1)S(1)}, u32[]{:S(2)}, u32[]{:S(2)}) %collective-permute-start.19) | collective-permute-done | bytes 65568 | tf_op jit(solution)/shard_map/ppermute | solution.py:353
  76.6 1.6 %collective-permute-done.20.refs_3_ = bf16[128,256]{1,0:T(8,128)(2,1)S(1)} collective-permute-done((bf16[128,256]{1,0:T(8,128)(2,1)S(1)}, bf16[128,256]{1,0:T(8,128)(2,1)S(1)}, u32[]{:S(2)}, u32[]{:S(2)}) %collective-permute-start.20) | collective-permute-done | bytes 65568 | tf_op jit(solution)/shard_map/ppermute | solution.py:353
  78.2 1.7 %collective-permute-done.22.refs_2_ = bf16[64,1024]{1,0:T(8,128)(2,1)S(1)} collective-permute-done((bf16[64,1024]{1,0:T(8,128)(2,1)S(1)}, bf16[64,1024]{1,0:T(8,128)(2,1)S(1)}, u32[]{:S(2)}, u32[]{:S(2)}) %collective-permute-start.22) | collective-permute-done | bytes 131104 | tf_op jit(solution)/shard_map/ppermute | solution.py:353
  80.6 0.8 neg_sum.1
  81.3 1.1 %loss.1 = f32[1,256]{1,0:T(1,128)} custom-call(s32[7]{0:T(128)S(1)} %stack.27.info_ref, f32[1,256]{1,0:T(1,128)S(1)} %get-tuple-element.86.loss_ref, bf16[80,1024]{1,0:T(8,128)(2,1)S(1)} %collective-permute-done.21.got_ref.refs_1_), custom_call_target="tpu_custom_call" | custom-call | flops 575000000 | tf_op jit(solution)/shard_map/loss/pallas_call | solution.py:340
  82.5 1.6 %lay_whole.1 = f32[1024,256]{1,0:T(8,128)} custom-call(s32[7]{0:T(128)S(1)} %stack.27.info_ref, bf16[128,256]{1,0:T(8,128)(2,1)S(1)} %seq_sum_2.1.refs_0_, bf16[128,256]{1,0:T(8,128)(2,1)S(1)} %collective-permute-done.18.refs_1_, bf16[128,256]{1,0:T(8,128)(2,1)S(1)} %collective-permute-done.19.refs_2_, bf16[128,256]{1,0:T(8,128)(2,1)S(1)} %collective-permute-done.20.refs_3_, ...), custom_call_target="tpu_custom_call" | custom-call | tf_op jit(solution)/shard_map/lay_whole/pallas_call | solution.py:340
  (63 shorter events, 7.8 us)
Async XLA Ops:
  0.6 19.2 %collective-permute-start = (bf16[256,1024]{1,0:T(8,128)(2,1)}, bf16[256,1024]{1,0:T(8,128)(2,1)S(1)}, u32[]{:S(2)}, u32[]{:S(2)}) collective-permute-start(bf16[256,1024]{1,0:T(8,128)(2,1)} %bitcast.15), channel_id=1, source_target_pairs={{0,4},{4,8},{1,5},{5,9},{2,6},{6,10},{3,7},{7,11},{16,20},{20,24},... | collective-permute-start | bytes 1572872 | tf_op jit(solution)/shard_map/ppermute | solution.py:387
  5.6 14.3 %collective-permute-start.1 = (bf16[256,1024]{1,0:T(8,128)(2,1)}, bf16[256,1024]{1,0:T(8,128)(2,1)S(1)}, u32[]{:S(2)}, u32[]{:S(2)}) collective-permute-start(bf16[256,1024]{1,0:T(8,128)(2,1)} %bitcast.16), channel_id=1, source_target_pairs={{12,8},{13,9},{14,10},{15,11},{28,24},{29,25},{30,26},{31,27}} | collective-permute-start | bytes 1572872 | tf_op jit(solution)/shard_map/ppermute | solution.py:388
  12.0 11.3 %copy-start = (bf16[1024,4096]{1,0:T(8,128)(2,1)S(1)}, bf16[1024,4096]{1,0:T(8,128)(2,1)}, u32[]{:S(2)}) copy-start(bf16[1024,4096]{1,0:T(8,128)(2,1)} %w_ref.5) | copy-start | bytes 25165828
  12.0 11.4 %copy-start.3 = (bf16[1,256,1024]{2,1,0:T(8,128)(2,1)S(1)}, bf16[1,256,1024]{2,1,0:T(8,128)(2,1)}, u32[]{:S(2)}) copy-start(bf16[1,256,1024]{2,1,0:T(8,128)(2,1)} %param.9) | copy-start | bytes 1572868
  18.3 13.8 %collective-permute-start.3 = (bf16[1056,256]{1,0:T(8,128)(2,1)S(1)}, bf16[1056,256]{1,0:T(8,128)(2,1)S(1)}, u32[]{:S(2)}, u32[]{:S(2)}) collective-permute-start(bf16[1056,256]{1,0:T(8,128)(2,1)S(1)} %get-tuple-element.84.rest_0_), channel_id=1, source_target_pairs={{0,2},{1,3},{2,0},{3,1},{4,6},{5,7},{6,4},{7,5},{8,10},{9,11},{10,... | collective-permute-start | bytes 1622024 | tf_op jit(solution)/shard_map/ppermute | solution.py:353
  19.9 14.1 %collective-permute-start.2 = (bf16[256,1024]{1,0:T(8,128)(2,1)S(1)}, bf16[256,1024]{1,0:T(8,128)(2,1)S(1)}, u32[]{:S(2)}, u32[]{:S(2)}) collective-permute-start(bf16[256,1024]{1,0:T(8,128)(2,1)S(1)} %collective-permute-done.x_ref), channel_id=1, source_target_pairs={{0,4},{4,8},{1,5},{5,9},{2,6},{6,10},{3,7},{7,11},{16,20},{20,24},... | collective-permute-start | bytes 1572872 | tf_op jit(solution)/shard_map/ppermute | solution.py:421
  32.1 9.2 %collective-permute-start.5 = (bf16[1056,256]{1,0:T(8,128)(2,1)S(1)}, bf16[1056,256]{1,0:T(8,128)(2,1)S(1)}, u32[]{:S(2)}, u32[]{:S(2)}) collective-permute-start(bf16[1056,256]{1,0:T(8,128)(2,1)S(1)} %get-tuple-element.84.rest_0_), channel_id=1, source_target_pairs={{0,1},{1,0},{2,3},{3,2},{4,5},{5,4},{6,7},{7,6},{8,9},{9,8},{10,11... | collective-permute-start | bytes 1622024 | tf_op jit(solution)/shard_map/ppermute | solution.py:353
  32.1 9.2 %collective-permute-start.6 = (bf16[1056,256]{1,0:T(8,128)(2,1)S(1)}, bf16[1056,256]{1,0:T(8,128)(2,1)S(1)}, u32[]{:S(2)}, u32[]{:S(2)}) collective-permute-start(bf16[1056,256]{1,0:T(8,128)(2,1)S(1)} %collective-permute-done.3.rest_1_), channel_id=1, source_target_pairs={{0,1},{1,0},{2,3},{3,2},{4,5},{5,4},{6,7},{7,6},{8,9},{9,8},{10,11... | collective-permute-start | bytes 1622024 | tf_op jit(solution)/shard_map/ppermute | solution.py:353
  32.6 8.7 %collective-permute-start.4 = (bf16[272,256]{1,0:T(8,128)(2,1)S(1)}, bf16[272,256]{1,0:T(8,128)(2,1)S(1)}, u32[]{:S(2)}, u32[]{:S(2)}) collective-permute-start(bf16[272,256]{1,0:T(8,128)(2,1)S(1)} %get-tuple-element.83), channel_id=1, source_target_pairs={{12,8},{13,9},{14,10},{15,11},{28,24},{29,25},{30,26},{31,27}} | collective-permute-start | bytes 417800 | tf_op jit(solution)/shard_map/ppermute | solution.py:438
  40.1 7.8 %collective-permute-start.12 = (bf16[512,256]{1,0:T(8,128)(2,1)S(1)}, bf16[512,256]{1,0:T(8,128)(2,1)S(1)}, u32[]{:S(2)}, u32[]{:S(2)}) collective-permute-start(bf16[512,256]{1,0:T(8,128)(2,1)S(1)} %get-tuple-element.95.hat_ref.rest_0_), channel_id=1, source_target_pairs={{0,2},{1,3},{2,0},{3,1},{4,6},{5,7},{6,4},{7,5},{8,10},{9,11},{10,... | collective-permute-start | bytes 786440 | tf_op jit(solution)/shard_map/ppermute | solution.py:353
  46.2 11.6 %copy-start.6 = (bf16[1,1024,256]{2,1,0:T(8,128)(2,1)S(1)}, bf16[1,1024,256]{2,1,0:T(8,128)(2,1)}, u32[]{:S(2)}) copy-start(bf16[1,1024,256]{2,1,0:T(8,128)(2,1)} %param.16) | copy-start | bytes 1572868
  46.2 11.6 %copy-start.10 = (s32[1,1024]{1,0:T(1,128)S(1)}, s32[1,1024]{1,0:T(1,128)}, u32[]{:S(2)}) copy-start(s32[1,1024]{1,0:T(1,128)} %neg_id_ref.1) | copy-start | bytes 12292
  46.2 1.8 %collective-permute-start.7 = (bf16[512,256]{1,0:T(8,128)(2,1)S(1)}, bf16[512,256]{1,0:T(8,128)(2,1)S(1)}, u32[]{:S(2)}, u32[]{:S(2)}) collective-permute-start(bf16[512,256]{1,0:T(8,128)(2,1)S(1)} %get-tuple-element.88), channel_id=1, source_target_pairs={{0,1},{1,0},{2,3},{3,2},{16,17},{17,16},{18,19},{19,18},{4,5},{5,4... | collective-permute-start | bytes 786440 | tf_op jit(solution)/shard_map/ppermute | solution.py:353
  46.3 11.5 %collective-permute-start.13 = (bf16[512,256]{1,0:T(8,128)(2,1)S(1)}, bf16[512,256]{1,0:T(8,128)(2,1)S(1)}, u32[]{:S(2)}, u32[]{:S(2)}) collective-permute-start(bf16[512,256]{1,0:T(8,128)(2,1)S(1)} %get-tuple-element.95.hat_ref.rest_0_), channel_id=1, source_target_pairs={{0,1},{1,0},{2,3},{3,2},{4,5},{5,4},{6,7},{7,6},{8,9},{9,8},{10,11... | collective-permute-start | bytes 786440 | tf_op jit(solution)/shard_map/ppermute | solution.py:353
  47.9 9.8 %collective-permute-start.14 = (bf16[512,256]{1,0:T(8,128)(2,1)S(1)}, bf16[512,256]{1,0:T(8,128)(2,1)S(1)}, u32[]{:S(2)}, u32[]{:S(2)}) collective-permute-start(bf16[512,256]{1,0:T(8,128)(2,1)S(1)} %collective-permute-done.12.rest_1_), channel_id=1, source_target_pairs={{0,1},{1,0},{2,3},{3,2},{4,5},{5,4},{6,7},{7,6},{8,9},{9,8},{10,11... | collective-permute-start | bytes 786440 | tf_op jit(solution)/shard_map/ppermute | solution.py:353
  48.6 5.1 %collective-permute-start.8 = (bf16[144,256]{1,0:T(8,128)(2,1)S(1)}, bf16[144,256]{1,0:T(8,128)(2,1)S(1)}, u32[]{:S(2)}, u32[]{:S(2)}) collective-permute-start(bf16[144,256]{1,0:T(8,128)(2,1)S(1)} %get-tuple-element.91), channel_id=1, source_target_pairs={{0,2},{1,3},{2,0},{3,1},{16,18},{17,19},{18,16},{19,17},{4,6},{5,7... | collective-permute-start | bytes 221192 | tf_op jit(solution)/shard_map/ppermute | solution.py:353
  50.2 5.5 %collective-permute-start.10 = (bf16[128,256]{1,0:T(8,128)(2,1)S(1)}, bf16[128,256]{1,0:T(8,128)(2,1)S(1)}, u32[]{:S(2)}, u32[]{:S(2)}) collective-permute-start(bf16[128,256]{1,0:T(8,128)(2,1)S(1)} %get-tuple-element.93), channel_id=1, source_target_pairs={{0,18},{1,19},{2,16},{3,17},{16,2},{17,3},{18,0},{19,1},{4,22},{5,... | collective-permute-start | bytes 196616 | tf_op jit(solution)/shard_map/ppermute | solution.py:353
  51.6 4.3 %collective-permute-start.9 = (bf16[128,256]{1,0:T(8,128)(2,1)S(1)}, bf16[128,256]{1,0:T(8,128)(2,1)S(1)}, u32[]{:S(2)}, u32[]{:S(2)}) collective-permute-start(bf16[128,256]{1,0:T(8,128)(2,1)S(1)} %get-tuple-element.92), channel_id=1, source_target_pairs={{0,16},{1,17},{2,18},{3,19},{16,0},{17,1},{18,2},{19,3},{4,20},{5,... | collective-permute-start | bytes 196616 | tf_op jit(solution)/shard_map/ppermute | solution.py:353
  53.7 4.0 %collective-permute-start.16 = (bf16[144,256]{1,0:T(8,128)(2,1)S(1)}, bf16[144,256]{1,0:T(8,128)(2,1)S(1)}, u32[]{:S(2)}, u32[]{:S(2)}) collective-permute-start(bf16[144,256]{1,0:T(8,128)(2,1)S(1)} %collective-permute-done.8.refs_1_.rest_5_), channel_id=1, source_target_pairs={{0,1},{1,0},{2,3},{3,2},{4,5},{5,4},{6,7},{7,6},{8,9},{9,8},{10,11... | collective-permute-start | bytes 221192 | tf_op jit(solution)/shard_map/ppermute | solution.py:353
  55.6 2.1 %collective-permute-start.15 = (bf16[16,256]{1,0:T(8,128)(2,1)S(1)}, bf16[16,256]{1,0:T(8,128)(2,1)S(1)}, u32[]{:S(2)}, u32[]{:S(2)}) collective-permute-start(bf16[16,256]{1,0:T(8,128)(2,1)S(1)} %get-tuple-element.99.message_ref.rest_4_), channel_id=1, source_target_pairs={{0,1},{1,0},{2,3},{3,2},{4,5},{5,4},{6,7},{7,6},{8,9},{9,8},{10,11... | collective-permute-start | bytes 24584 | tf_op jit(solution)/shard_map/ppermute | solution.py:353
  55.9 5.6 %collective-permute-start.11 = (bf16[128,256]{1,0:T(8,128)(2,1)S(1)}, bf16[128,256]{1,0:T(8,128)(2,1)S(1)}, u32[]{:S(2)}, u32[]{:S(2)}) collective-permute-start(bf16[128,256]{1,0:T(8,128)(2,1)S(1)} %plane_sum.1.refs_0_), channel_id=1, source_target_pairs={{0,4},{4,0},{8,12},{12,8},{1,5},{5,1},{9,13},{13,9},{2,6},{6,2},{1... | collective-permute-start | bytes 196616 | tf_op jit(solution)/shard_map/ppermute | solution.py:353
  61.5 6.6 %collective-permute-start.17 = (bf16[128,256]{1,0:T(8,128)(2,1)S(1)}, bf16[128,256]{1,0:T(8,128)(2,1)S(1)}, u32[]{:S(2)}, u32[]{:S(2)}) collective-permute-start(bf16[128,256]{1,0:T(8,128)(2,1)S(1)} %seq_sum_1.1.refs_0_), channel_id=1, source_target_pairs={{0,8},{4,12},{8,0},{12,4},{1,9},{5,13},{9,1},{13,5},{2,10},{6,14},... | collective-permute-start | bytes 196616 | tf_op jit(solution)/shard_map/ppermute | solution.py:353
  64.2 15.8 %collective-permute-start.21 = (bf16[80,1024]{1,0:T(8,128)(2,1)S(1)}, bf16[80,1024]{1,0:T(8,128)(2,1)S(1)}, u32[]{:S(2)}, u32[]{:S(2)}) collective-permute-start(bf16[80,1024]{1,0:T(8,128)(2,1)S(1)} %get-tuple-element.107), channel_id=1, source_target_pairs={{0,4},{4,0},{8,12},{12,8},{1,5},{5,1},{9,13},{13,9},{2,6},{6,2},{1... | collective-permute-start | bytes 491528 | tf_op jit(solution)/shard_map/ppermute | solution.py:353
  68.2 4.9 %collective-permute-start.18 = (bf16[128,256]{1,0:T(8,128)(2,1)S(1)}, bf16[128,256]{1,0:T(8,128)(2,1)S(1)}, u32[]{:S(2)}, u32[]{:S(2)}) collective-permute-start(bf16[128,256]{1,0:T(8,128)(2,1)S(1)} %seq_sum_2.1.refs_0_), channel_id=1, source_target_pairs={{0,2},{1,3},{2,0},{3,1},{16,18},{17,19},{18,16},{19,17},{4,6},{5,7... | collective-permute-start | bytes 196616 | tf_op jit(solution)/shard_map/ppermute | solution.py:353
  69.1 10.9 %collective-permute-start.22 = (bf16[64,1024]{1,0:T(8,128)(2,1)S(1)}, bf16[64,1024]{1,0:T(8,128)(2,1)S(1)}, u32[]{:S(2)}, u32[]{:S(2)}) collective-permute-start(bf16[64,1024]{1,0:T(8,128)(2,1)S(1)} %get-tuple-element.108), channel_id=1, source_target_pairs={{0,8},{4,12},{8,0},{12,4},{1,9},{5,13},{9,1},{13,5},{2,10},{6,14},... | collective-permute-start | bytes 393224 | tf_op jit(solution)/shard_map/ppermute | solution.py:353
  71.6 8.4 %collective-permute-start.23 = (bf16[64,1024]{1,0:T(8,128)(2,1)S(1)}, bf16[64,1024]{1,0:T(8,128)(2,1)S(1)}, u32[]{:S(2)}, u32[]{:S(2)}) collective-permute-start(bf16[64,1024]{1,0:T(8,128)(2,1)S(1)} %get-tuple-element.109), channel_id=1, source_target_pairs={{0,12},{4,8},{8,4},{12,0},{1,13},{5,9},{9,5},{13,1},{2,14},{6,10},... | collective-permute-start | bytes 393224 | tf_op jit(solution)/shard_map/ppermute | solution.py:353
  71.9 4.7 %collective-permute-start.19 = (bf16[128,256]{1,0:T(8,128)(2,1)S(1)}, bf16[128,256]{1,0:T(8,128)(2,1)S(1)}, u32[]{:S(2)}, u32[]{:S(2)}) collective-permute-start(bf16[128,256]{1,0:T(8,128)(2,1)S(1)} %seq_sum_2.1.refs_0_), channel_id=1, source_target_pairs={{0,16},{1,17},{2,18},{3,19},{16,0},{17,1},{18,2},{19,3},{4,20},{5,... | collective-permute-start | bytes 196616 | tf_op jit(solution)/shard_map/ppermute | solution.py:353
  73.1 5.2 %collective-permute-start.20 = (bf16[128,256]{1,0:T(8,128)(2,1)S(1)}, bf16[128,256]{1,0:T(8,128)(2,1)S(1)}, u32[]{:S(2)}, u32[]{:S(2)}) collective-permute-start(bf16[128,256]{1,0:T(8,128)(2,1)S(1)} %seq_sum_2.1.refs_0_), channel_id=1, source_target_pairs={{0,18},{1,19},{2,16},{3,17},{16,2},{17,3},{18,0},{19,1},{4,22},{5,... | collective-permute-start | bytes 196616 | tf_op jit(solution)/shard_map/ppermute | solution.py:353
  76.6 5.8 %collective-permute-start.24 = (bf16[128,256]{1,0:T(8,128)(2,1)S(1)}, bf16[128,256]{1,0:T(8,128)(2,1)S(1)}, u32[]{:S(2)}, u32[]{:S(2)}) collective-permute-start(bf16[128,256]{1,0:T(8,128)(2,1)S(1)} %seq_sum_2.1.refs_0_), channel_id=1, source_target_pairs={{0,1},{1,0},{2,3},{3,2},{16,17},{17,16},{18,19},{19,18},{4,5},{5,4... | collective-permute-start | bytes 196616 | tf_op jit(solution)/shard_map/ppermute | solution.py:353
  80.0 2.5 %collective-permute-start.25 = (bf16[128,256]{1,0:T(8,128)(2,1)S(1)}, bf16[128,256]{1,0:T(8,128)(2,1)S(1)}, u32[]{:S(2)}, u32[]{:S(2)}) collective-permute-start(bf16[128,256]{1,0:T(8,128)(2,1)S(1)} %collective-permute-done.18.refs_1_), channel_id=1, source_target_pairs={{0,1},{1,0},{2,3},{3,2},{16,17},{17,16},{18,19},{19,18},{4,5},{5,4... | collective-permute-start | bytes 196616 | tf_op jit(solution)/shard_map/ppermute | solution.py:353
  80.0 2.5 %collective-permute-start.26 = (bf16[128,256]{1,0:T(8,128)(2,1)S(1)}, bf16[128,256]{1,0:T(8,128)(2,1)S(1)}, u32[]{:S(2)}, u32[]{:S(2)}) collective-permute-start(bf16[128,256]{1,0:T(8,128)(2,1)S(1)} %collective-permute-done.19.refs_2_), channel_id=1, source_target_pairs={{0,1},{1,0},{2,3},{3,2},{16,17},{17,16},{18,19},{19,18},{4,5},{5,4... | collective-permute-start | bytes 196616 | tf_op jit(solution)/shard_map/ppermute | solution.py:353
  80.5 2.0 %collective-permute-start.27 = (bf16[128,256]{1,0:T(8,128)(2,1)S(1)}, bf16[128,256]{1,0:T(8,128)(2,1)S(1)}, u32[]{:S(2)}, u32[]{:S(2)}) collective-permute-start(bf16[128,256]{1,0:T(8,128)(2,1)S(1)} %collective-permute-done.20.refs_3_), channel_id=1, source_target_pairs={{0,1},{1,0},{2,3},{3,2},{16,17},{17,16},{18,19},{19,18},{4,5},{5,4... | collective-permute-start | bytes 196616 | tf_op jit(solution)/shard_map/ppermute | solution.py:353
  (8 other events, 23.2 us)

commit v4 on v3

--- a/solution.py
+++ b/solution.py
@@ -70,9 +70,12 @@
 def attend(q_ref, keys, values, acc_ref, before_ref, causal=None):
     rows, width = q_ref.shape
     head = width // HEADS
-    for h in range(HEADS):
-        cols = slice(h * head, (h + 1) * head)
-        half = dot_t(q_ref[:, cols], keys[:, cols]) * (0.5 / math.sqrt(head))
+    spans = [slice(h * head, (h + 1) * head) for h in range(HEADS)]
+    following = dot_t(q_ref[:, spans[0]], keys[:, spans[0]])
+    for h, cols in enumerate(spans):
+        half = following * (0.5 / math.sqrt(head))
+        if h + 1 < HEADS:
+            following = dot_t(q_ref[:, spans[h + 1]], keys[:, spans[h + 1]])
         weights = half + half * jnp.tanh(half)
         if causal is not None:
             weights = jnp.where(causal, weights, 0.0)
@@ -211,20 +214,23 @@
     )
     lanes = jnp.zeros((rows, 128), F32)
     grads = jnp.zeros((rows, embed), F32)
-    for table_ref in table_refs:
-        parts = table_ref[count:, :].astype(F32)
-        for chunk in range(chunks):
-            bias, ids = (
-                [parts[(g + j) * chunks + chunk : (g + j) * chunks + chunk + 1, :] for j in range(3)]
-                for g in (0, 3)
-            )
-            cut = slice(chunk * embed, (chunk + 1) * embed)
-            scores = dot_t(hat, table_ref[cut, :]) * SCORE_SCALE - (bias[0] + bias[1] + bias[2])
-            kept = jnp.where(of_digits(*ids) != pos_id, jnp.exp2(scores), 0.0)
-            for lane in range(0, embed, 128):
-                lanes = lanes + kept[:, lane : lane + 128]
-            kept_ref[:, cut] = kept.astype(BF16)
-        grads = grads + dot(kept_ref[...], table_ref[:count, :])
+    steps = [(table_ref, chunk) for table_ref in table_refs for chunk in range(chunks)]
+
+    def table_scores(table_ref, chunk):
+        return dot_t(hat, table_ref[chunk * embed : (chunk + 1) * embed, :])
+
+    following = table_scores(*steps[0])
+    for step, (table_ref, chunk) in enumerate(steps):
+        scores = following * SCORE_SCALE
+        if step + 1 < len(steps):
+            following = table_scores(*steps[step + 1])
+        row = [table_ref[count:, :][i : i + 1, :].astype(F32) for i in range(chunk, 6 * chunks, chunks)]
+        kept = jnp.where(of_digits(*row[3:]) != pos_id, jnp.exp2(scores - (row[0] + row[1] + row[2])), 0.0)
+        for lane in range(0, embed, 128):
+            lanes = lanes + kept[:, lane : lane + 128]
+        kept_ref[:, chunk * embed : (chunk + 1) * embed] = kept.astype(BF16)
+        if chunk == chunks - 1:
+            grads = grads + dot(kept_ref[...], table_ref[:count, :])
     pos_part = jnp.exp(pos_score)
     total = pos_part + jnp.sum(lanes, axis=-1, keepdims=True)
     log_total = jnp.log(total)
@@ -270,7 +276,7 @@
 
 
 def sum_kernel(*refs):
-    rows = refs[0].shape[0]
+    rows = refs[-1].shape[0]
     parts = [ref[:rows, :].astype(F32) for ref in refs[:-1]]
     while len(parts) > 1:
         parts = [a + b for a, b in zip(parts[::2], parts[1::2])]
@@ -287,14 +293,24 @@
         out_ref[part_at(at, rows), :] = part_ref[...].astype(out_ref.dtype)
 
 
-def loss_kernel(last, info_ref, loss_ref, got_ref, own_loss_ref):
-    rows = loss_ref.shape[1]
-    parts = got_ref[got_ref.shape[0] - 16 :, :rows].astype(F32)
+def loss_sum_kernel(loss_ref, *refs):
+    *part_refs, out_ref = refs
+    rows, events = part_refs[0].shape[0], loss_ref.shape[1]
+    sum_kernel(*part_refs, out_ref.at[:rows, :])
+    parts = split3(loss_ref[...])
+    pad = jnp.zeros((16 - len(parts), events), F32)
+    out_ref[rows:, :] = jnp.concatenate(parts + [pad], axis=0).astype(BF16)
+
+
+def last_sum_kernel(last, info_ref, loss_ref, got_ref, part_ref, *rest):
+    *got_refs, own_loss_ref, sum_ref = rest
+    parts = got_ref[got_ref.shape[0] - 16 :, :].astype(F32)
     above = parts[0:1, :] + parts[1:2, :] + parts[2:3, :]
     own_loss_ref[...] = jnp.where(info_ref[2] == last, above, loss_ref[...])
-
-
-def negative_kernel(pool_count, info_ref, neg_ref, neg_id_ref, loss_ref, *rest):
+    sum_kernel(part_ref, *got_refs, sum_ref)
+
+
+def negative_kernel(pool_count, info_ref, neg_ref, neg_id_ref, *rest):
     gathered, rest = rest[: 2 * pool_count], rest[2 * pool_count :]
     own_ref, *send_refs, turned_ref, sum_ref, weight_ref = rest
     count, embed = neg_ref.shape
@@ -326,11 +342,7 @@
     cols = own_ref.shape[0]
     own_ref[...] = turned_ref[part_at(info_ref[2], cols), :]
     for r, send_ref in enumerate(send_refs, 1):
-        send_ref[:cols, :] = turned_ref[part_at(lax.bitwise_xor(info_ref[2], r), cols), :].astype(BF16)
-    parts = split3(loss_ref[...])
-    pad = jnp.zeros((16 - len(parts), loss_ref.shape[1]), F32)
-    send_refs[0][cols:, :] = jnp.zeros((16, count), BF16)
-    send_refs[0][cols:, : loss_ref.shape[1]] = jnp.concatenate(parts + [pad], axis=0).astype(BF16)
+        send_ref[...] = turned_ref[part_at(lax.bitwise_xor(info_ref[2], r), cols), :].astype(BF16)
 
 
 def call(kernel, ins, outs, scratch=(), limit=24, micros=0.5, name=None, place=pltpu.VMEM):
@@ -382,9 +394,9 @@
     own = tokens[0]
     local_neg = neg_embed.shape[1]
 
-    up = [(i, i + 1) for i in range(seq_count - 2)]
+    ups = [[(i, i + 1) for i in range(hop, seq_count - 2)] for hop in range(seq_count - 2)]
     down = [(seq_count - 1, seq_count - 2)]
-    block = lax.ppermute(own, "seq", up)
+    block = lax.ppermute(own, "seq", ups[0])
     guest = lax.ppermute(own, "seq", down)
     kind = struct((rows, width), BF16)
     wide = struct((rows, width), F32)
@@ -418,7 +430,7 @@
     tall = struct((2 * rows, width), BF16)
     tall_wide = struct((2 * rows, width), F32)
     for step in range(1, seq_count - 2):
-        following = lax.ppermute(block, "seq", up)
+        following = lax.ppermute(block, "seq", ups[step])
         if step == 1:
             own, gate, queries, acc = call(
                 guest_kernel,
@@ -484,34 +496,43 @@
     hats, messages, _ = together(hats, messages, proj_part)
     d_part, *sends = call(
         functools.partial(negative_kernel, pool_count),
-        [info, neg_embed[0], neg_ids, guest_loss, *hats, *messages],
+        [info, neg_embed[0], neg_ids, *hats, *messages],
         [struct((cols, local_neg), F32)]
-        + [struct((cols + 16 * (r == 1), local_neg), BF16) for r in range(1, seq_count)],
+        + [struct((cols, local_neg), BF16)] * (seq_count - 1),
         scratch=[
             pltpu.VMEM((embed, local_neg), F32), pltpu.VMEM((local_neg, embed), F32),
             pltpu.VMEM((local_neg, 2 * rows), BF16),
         ],
         micros=3.7, name="neg_grad",
     )
-    got = swap(proj_part, "seq", seq_count, 1)
-    got, sends = together(got, sends)
-    proj_part = call(sum_kernel, [proj_part, got], part, name="seq_sum_1")
-    bit = 2
-    while bit < seq_count:
-        proj_part = call(
-            sum_kernel, [proj_part, swap(proj_part, "seq", seq_count, bit)], part, name=f"seq_sum_{bit}"
-        )
-        bit *= 2
-    gots = [swap(x, "seq", seq_count, r) for r, x in enumerate(sends, 1)]
-    others, gots = together(plane_swap([proj_part] * (chips - 1)), gots)
+    bit = seq_count // 2
+    got, sends = together(swap(proj_part, "seq", seq_count, bit), sends)
+    while bit > 2:
+        proj_part = call(sum_kernel, [proj_part, got], part, name=f"seq_sum_{bit}")
+        bit //= 2
+        got = swap(proj_part, "seq", seq_count, bit)
+    proj_part = call(
+        loss_sum_kernel,
+        [guest_loss, proj_part, got],
+        struct((part.shape[0] + 16, embed), BF16),
+        name="seq_sum_2",
+    )
+    loss_got = swap(proj_part, "seq", seq_count, 1)
+    proj_part = call(sum_kernel, [proj_part, loss_got], part, name="seq_sum_1")
+    gots = [swap(x, "seq", seq_count, r) for r, x in enumerate(sends[1:], 2)]
+    others = plane_swap([proj_part] * (chips - 1))
+    first, _ = together(sends[0], others)
+    others, gots = together(others, gots)
+    gots = [swap(first, "seq", seq_count, 1)] + gots
     proj_parts = [proj_part] + others
     proj_parts += [swap(x, plane, plane_count, 1) for x in proj_parts]
     d_proj = call(lay_kernel, [info, *proj_parts], struct((width, embed), F32), micros=0, name="lay_whole")
-    loss = call(
-        functools.partial(loss_kernel, seq_count - 1), [info, loss, gots[0]], struct((1, rows), F32),
-        micros=1, name="loss",
-    )
-    d_neg = call(sum_kernel, [d_part, *gots], struct((cols, local_neg), F32), micros=0.7, name="neg_sum")
+    loss, d_neg = call(
+        functools.partial(last_sum_kernel, seq_count - 1),
+        [info, loss, loss_got, d_part, *gots],
+        [struct((1, rows), F32), struct((cols, local_neg), F32)],
+        micros=0.9, name="neg_sum",
+    )
     return (loss, d_neg.T[None], d_proj)
 
 

time: 85.2 us -> 81.6 us (0.958)
  waiting for transfers between devices: 14.6 us -> 12.7 us
    ppermute x2, starting transfers between devices: 8.44 us -> 5.65 us  [the longest x1 4.96 us: body(): block = lax.ppermute(own, 'seq', ups[0])]
    ppermute x24, starting transfers between devices: 19.3 us -> 21.5 us  [swap(): return lax.ppermute(x, axis, [(i, i ^ r) for i in range(count)])]
    ppermute x24, waiting for transfers between devices: 14.1 us -> 12.7 us  [swap(): return lax.ppermute(x, axis, [(i, i ^ r) for i in range(count)])]
    pallas_call x14 -> x13, Pallas kernels: 34.2 us -> 33.9 us  [call(): pl.pallas_call(kernel, out_shape=list(outs) if many else outs, in_specs=i...]
  transfers between devices with their start and end apart: 28 -> 28, of which waited for: 10 -> 13; matrix products, arithmetic and copies ran while one was open for 0% -> 0% of each run, Pallas kernels for 39% -> 40%
where the time goes in v4:
time: 81.6 us; the launch traced here: 81.3 us
  Pallas kernels  33.9 us (42%)
  starting transfers between devices  28.7 us (35%)
  waiting for transfers between devices  12.7 us (16%)
  local copies, waits for them, and re-layouts  4.47 us (5%)
  between operations  1.57 us (2%)
    pallas_call x13, Pallas kernels, call(): pl.pallas_call(kernel, out_shape=list(outs) if many else outs, in_specs=i...  33.9 us
    ppermute x24, starting transfers between devices, swap(): return lax.ppermute(x, axis, [(i, i ^ r) for i in range(count)])  21.5 us
    ppermute x24, waiting for transfers between devices, swap(): return lax.ppermute(x, axis, [(i, i ^ r) for i in range(count)])  12.7 us
    ppermute x1, starting transfers between devices, body(): block = lax.ppermute(own, 'seq', ups[0])  4.96 us
    unnamed x24, local copies, waits for them, and re-layouts  4.39 us
  transfers between devices with their start and end apart: 28, of which 13 were waited for; matrix products, arithmetic and copies ran while one was open for 0% of the time, Pallas kernels for 40%

profile of v4, /device:TPU:0, one launch (start us, length us, event | category | flops | bytes accessed | tf_op | source)
XLA Modules:
  0.0 81.3 jit_solution(7601125179538001999)
XLA Ops:
  0.6 5.0 %collective-permute-start = (bf16[256,1024]{1,0:T(8,128)(2,1)}, bf16[256,1024]{1,0:T(8,128)(2,1)S(1)}, u32[]{:S(2)}, u32[]{:S(2)}) collective-permute-start(bf16[256,1024]{1,0:T(8,128)(2,1)} %bitcast.15), channel_id=1, source_target_pairs={{0,4},{4,8},{1,5},{5,9},{2,6},{6,10},{3,7},{7,11},{16,20},{20,24},... | collective-permute-start | bytes 1572872 | tf_op jit(solution)/shard_map/ppermute | solution.py:399
  7.1 1.0 %copy-done.5 = bf16[1,1024,256]{2,1,0:T(8,128)(2,1)S(1)} copy-done((bf16[1,1024,256]{2,1,0:T(8,128)(2,1)S(1)}, bf16[1,1024,256]{2,1,0:T(8,128)(2,1)}, u32[]{:S(2)}) %copy-start.5) | copy-done | bytes 524312
  8.1 0.9 %copy-done.7 = bf16[1,256,256]{2,1,0:T(8,128)(2,1)S(1)} copy-done((bf16[1,256,256]{2,1,0:T(8,128)(2,1)S(1)}, bf16[1,256,256]{2,1,0:T(8,128)(2,1)}, u32[]{:S(2)}) %copy-start.7) | copy-done | bytes 131096
  11.0 1.0 %copy-done.2 = bf16[1,256,1024]{2,1,0:T(8,128)(2,1)S(1)} copy-done((bf16[1,256,1024]{2,1,0:T(8,128)(2,1)S(1)}, bf16[1,256,1024]{2,1,0:T(8,128)(2,1)}, u32[]{:S(2)}) %copy-start.2) | copy-done | bytes 524312
  12.0 6.2 %own_block.1 = (bf16[256,1024]{1,0:T(8,128)(2,1)S(1)}, bf16[256,1024]{1,0:T(8,128)(2,1)S(1)}, bf16[256,1024]{1,0:T(8,128)(2,1)S(1)}, bf16[256,1024]{1,0:T(8,128)(2,1)S(1)}, f32[256,1024]{1,0:T(8,128)S(1)}) custom-call(s32[7]{0:T(128)S(1)} %stack.27.info_ref, bf16[256,1024]{1,0:T(8,128)(2,1)S(1)} %bitcast.17, bf16[1024,4096]{1,0:T(8,128)(2,1)} %w_ref.5), custom_call_target="tpu_custom_call" | custom-call | flops 3449999872 | tf_op jit(solution)/shard_map/own_block/pallas_call | solution.py:352
  18.2 1.6 %collective-permute-start.3 = (bf16[1056,256]{1,0:T(8,128)(2,1)S(1)}, bf16[1056,256]{1,0:T(8,128)(2,1)S(1)}, u32[]{:S(2)}, u32[]{:S(2)}) collective-permute-start(bf16[1056,256]{1,0:T(8,128)(2,1)S(1)} %get-tuple-element.86.rest_0_), channel_id=1, source_target_pairs={{0,2},{1,3},{2,0},{3,1},{4,6},{5,7},{6,4},{7,5},{8,10},{9,11},{10,... | collective-permute-start | bytes 1622024 | tf_op jit(solution)/shard_map/ppermute | solution.py:365
  20.5 5.0 %guest_block.1 = (bf16[512,1024]{1,0:T(8,128)(2,1)S(1)}, bf16[512,1024]{1,0:T(8,128)(2,1)S(1)}, bf16[512,1024]{1,0:T(8,128)(2,1)S(1)}, f32[512,1024]{1,0:T(8,128)S(1)}) custom-call(s32[7]{0:T(128)S(1)} %stack.27.info_ref, bf16[256,1024]{1,0:T(8,128)(2,1)S(1)} %collective-permute-done.1.x_ref, bf16[1024,4096]{1,0:T(8,128)(2,1)S(1)} %copy-done, ...), custom_call_target="tpu_custom_call" | custom-call | flops 2760000000 | tf_op jit(solution)/shard_map/guest_block/pallas_call | solution.py:352
  25.6 3.6 %earlier_block_1.1.before_ref = f32[512,1024]{1,0:T(8,128)S(1)} custom-call(s32[7]{0:T(128)S(1)} %stack.27.info_ref, bf16[256,1024]{1,0:T(8,128)(2,1)S(1)} %collective-permute-done.x_ref, bf16[1024,4096]{1,0:T(8,128)(2,1)S(1)} %copy-done, bf16[512,1024]{1,0:T(8,128)(2,1)S(1)} %get-tuple-element.73.q_ref, f32[512,1024]{1,0:T(8,128)S(1)} %get-tuple-element.74.before_ref), custom_call_target="tpu_custom_call" | custom-call | flops 2070000000 | tf_op jit(solution)/shard_map/earlier_block_1/pallas_call | solution.py:352
  29.1 2.9 %collective-permute-done.3.rest_1_ = bf16[1056,256]{1,0:T(8,128)(2,1)S(1)} collective-permute-done((bf16[1056,256]{1,0:T(8,128)(2,1)S(1)}, bf16[1056,256]{1,0:T(8,128)(2,1)S(1)}, u32[]{:S(2)}, u32[]{:S(2)}) %collective-permute-start.3) | collective-permute-done | bytes 540704 | tf_op jit(solution)/shard_map/ppermute | solution.py:365
  32.6 0.8 %collective-permute-start.4 = (bf16[272,256]{1,0:T(8,128)(2,1)S(1)}, bf16[272,256]{1,0:T(8,128)(2,1)S(1)}, u32[]{:S(2)}, u32[]{:S(2)}) collective-permute-start(bf16[272,256]{1,0:T(8,128)(2,1)S(1)} %get-tuple-element.85), channel_id=1, source_target_pairs={{12,8},{13,9},{14,10},{15,11},{28,24},{29,25},{30,26},{31,27}} | collective-permute-start | bytes 417800 | tf_op jit(solution)/shard_map/ppermute | solution.py:450
  33.4 6.0 %last_block.1 = (bf16[512,1024]{1,0:T(8,128)(2,1)S(1)}, f32[512,256]{1,0:T(8,128)S(1)}, bf16[512,256]{1,0:T(8,128)(2,1)S(1)}) custom-call(s32[7]{0:T(128)S(1)} %stack.27.info_ref, bf16[256,1024]{1,0:T(8,128)(2,1)S(1)} %collective-permute-done.2.x_ref, bf16[1024,4096]{1,0:T(8,128)(2,1)S(1)} %copy-done, bf16[512,1024]{1,0:T(8,128)(2,1)S(1)} %get-tuple-element.73.q_ref, ...), custom_call_target="tpu_custom_call" | custom-call | flops 3449999872 | tf_op jit(solution)/shard_map/last_block/pallas_call | solution.py:352
  39.5 1.6 %collective-permute-start.12 = (bf16[512,256]{1,0:T(8,128)(2,1)S(1)}, bf16[512,256]{1,0:T(8,128)(2,1)S(1)}, u32[]{:S(2)}, u32[]{:S(2)}) collective-permute-start(bf16[512,256]{1,0:T(8,128)(2,1)S(1)} %get-tuple-element.97.hat_ref.rest_0_), channel_id=1, source_target_pairs={{0,2},{1,3},{2,0},{3,1},{4,6},{5,7},{6,4},{7,5},{8,10},{9,11},{10,... | collective-permute-start | bytes 786440 | tf_op jit(solution)/shard_map/ppermute | solution.py:365
  41.1 5.1 %head.1 = (f32[1,256]{1,0:T(1,128)S(1)}, f32[1,256]{1,0:T(1,128)S(1)}, bf16[16,256]{1,0:T(8,128)(2,1)S(1)}, f32[512,256]{1,0:T(8,128)S(1)}, bf16[512,256]{1,0:T(8,128)(2,1)S(1)}) custom-call(s32[7]{0:T(128)S(1)} %stack.27.info_ref, bf16[512,256]{1,0:T(8,128)(2,1)S(1)} %get-tuple-element.97.hat_ref.rest_0_, f32[512,256]{1,0:T(8,128)S(1)} %get-tuple-element.83.out_ref, ...), custom_call_target="tpu_custom_call" | custom-call | flops 2875000064 | tf_op jit(solution)/shard_map/head/pallas_call | solution.py:352
  46.8 0.9 %collective-permute-done.12.rest_1_ = bf16[512,256]{1,0:T(8,128)(2,1)S(1)} collective-permute-done((bf16[512,256]{1,0:T(8,128)(2,1)S(1)}, bf16[512,256]{1,0:T(8,128)(2,1)S(1)}, u32[]{:S(2)}, u32[]{:S(2)}) %collective-permute-start.12) | collective-permute-done | bytes 262176 | tf_op jit(solution)/shard_map/ppermute | solution.py:365
  48.5 1.5 %collective-permute-start.8 = (bf16[144,256]{1,0:T(8,128)(2,1)S(1)}, bf16[144,256]{1,0:T(8,128)(2,1)S(1)}, u32[]{:S(2)}, u32[]{:S(2)}) collective-permute-start(bf16[144,256]{1,0:T(8,128)(2,1)S(1)} %get-tuple-element.94), channel_id=1, source_target_pairs={{0,2},{1,3},{2,0},{3,1},{16,18},{17,19},{18,16},{19,17},{4,6},{5,7... | collective-permute-start | bytes 221192 | tf_op jit(solution)/shard_map/ppermute | solution.py:365
  50.0 1.5 %collective-permute-start.10 = (bf16[128,256]{1,0:T(8,128)(2,1)S(1)}, bf16[128,256]{1,0:T(8,128)(2,1)S(1)}, u32[]{:S(2)}, u32[]{:S(2)}) collective-permute-start(bf16[128,256]{1,0:T(8,128)(2,1)S(1)} %get-tuple-element.96), channel_id=1, source_target_pairs={{0,18},{1,19},{2,16},{3,17},{16,2},{17,3},{18,0},{19,1},{4,22},{5,... | collective-permute-start | bytes 196616 | tf_op jit(solution)/shard_map/ppermute | solution.py:365
  52.0 1.3 %collective-permute-done.8.refs_1_.rest_5_ = bf16[144,256]{1,0:T(8,128)(2,1)S(1)} collective-permute-done((bf16[144,256]{1,0:T(8,128)(2,1)S(1)}, bf16[144,256]{1,0:T(8,128)(2,1)S(1)}, u32[]{:S(2)}, u32[]{:S(2)}) %collective-permute-start.8) | collective-permute-done | bytes 73760 | tf_op jit(solution)/shard_map/ppermute | solution.py:365
  53.4 2.1 %collective-permute-done.10.refs_3_ = bf16[128,256]{1,0:T(8,128)(2,1)S(1)} collective-permute-done((bf16[128,256]{1,0:T(8,128)(2,1)S(1)}, bf16[128,256]{1,0:T(8,128)(2,1)S(1)}, u32[]{:S(2)}, u32[]{:S(2)}) %collective-permute-start.10) | collective-permute-done | bytes 65568 | tf_op jit(solution)/shard_map/ppermute | solution.py:365
  55.8 3.0 %collective-permute-start.11 = (bf16[128,256]{1,0:T(8,128)(2,1)S(1)}, bf16[128,256]{1,0:T(8,128)(2,1)S(1)}, u32[]{:S(2)}, u32[]{:S(2)}) collective-permute-start(bf16[128,256]{1,0:T(8,128)(2,1)S(1)} %plane_sum.1.refs_0_), channel_id=1, source_target_pairs={{0,8},{4,12},{8,0},{12,4},{1,9},{5,13},{9,1},{13,5},{2,10},{6,14},... | collective-permute-start | bytes 196616 | tf_op jit(solution)/shard_map/ppermute | solution.py:365
  58.9 3.7 %neg_grad.1 = (f32[64,1024]{1,0:T(8,128)S(1)}, bf16[64,1024]{1,0:T(8,128)(2,1)S(1)}, bf16[64,1024]{1,0:T(8,128)(2,1)S(1)}, bf16[64,1024]{1,0:T(8,128)(2,1)S(1)}) custom-call(s32[7]{0:T(128)S(1)} %stack.27.info_ref, bf16[1024,256]{1,0:T(8,128)(2,1)S(1)} %bitcast.20, s32[1,1024]{1,0:T(1,128)S(1)} %copy-done.10, ...), custom_call_target="tpu_custom_call" | custom-call | flops 2127500032 | tf_op jit(solution)/shard_map/neg_grad/pallas_call | solution.py:352
  62.7 1.6 %collective-permute-start.17 = (bf16[144,256]{1,0:T(8,128)(2,1)S(1)}, bf16[144,256]{1,0:T(8,128)(2,1)S(1)}, u32[]{:S(2)}, u32[]{:S(2)}) collective-permute-start(bf16[144,256]{1,0:T(8,128)(2,1)S(1)} %seq_sum_2.1.refs_0_), channel_id=1, source_target_pairs={{0,4},{4,0},{8,12},{12,8},{1,5},{5,1},{9,13},{13,9},{2,6},{6,2},{1... | collective-permute-start | bytes 221192 | tf_op jit(solution)/shard_map/ppermute | solution.py:365
  64.3 2.0 %collective-permute-start.22 = (bf16[64,1024]{1,0:T(8,128)(2,1)S(1)}, bf16[64,1024]{1,0:T(8,128)(2,1)S(1)}, u32[]{:S(2)}, u32[]{:S(2)}) collective-permute-start(bf16[64,1024]{1,0:T(8,128)(2,1)S(1)} %get-tuple-element.112), channel_id=1, source_target_pairs={{0,8},{4,12},{8,0},{12,4},{1,9},{5,13},{9,1},{13,5},{2,10},{6,14},... | collective-permute-start | bytes 393224 | tf_op jit(solution)/shard_map/ppermute | solution.py:365
  66.3 0.9 %collective-permute-start.23 = (bf16[64,1024]{1,0:T(8,128)(2,1)S(1)}, bf16[64,1024]{1,0:T(8,128)(2,1)S(1)}, u32[]{:S(2)}, u32[]{:S(2)}) collective-permute-start(bf16[64,1024]{1,0:T(8,128)(2,1)S(1)} %get-tuple-element.113), channel_id=1, source_target_pairs={{0,12},{4,8},{8,4},{12,0},{1,13},{5,9},{9,5},{13,1},{2,14},{6,10},... | collective-permute-start | bytes 393224 | tf_op jit(solution)/shard_map/ppermute | solution.py:365
  67.2 1.3 %collective-permute-start.18 = (bf16[128,256]{1,0:T(8,128)(2,1)S(1)}, bf16[128,256]{1,0:T(8,128)(2,1)S(1)}, u32[]{:S(2)}, u32[]{:S(2)}) collective-permute-start(bf16[128,256]{1,0:T(8,128)(2,1)S(1)} %seq_sum_1.1.refs_0_), channel_id=1, source_target_pairs={{0,2},{1,3},{2,0},{3,1},{16,18},{17,19},{18,16},{19,17},{4,6},{5,7... | collective-permute-start | bytes 196616 | tf_op jit(solution)/shard_map/ppermute | solution.py:365
  68.4 1.2 %collective-permute-start.19 = (bf16[128,256]{1,0:T(8,128)(2,1)S(1)}, bf16[128,256]{1,0:T(8,128)(2,1)S(1)}, u32[]{:S(2)}, u32[]{:S(2)}) collective-permute-start(bf16[128,256]{1,0:T(8,128)(2,1)S(1)} %seq_sum_1.1.refs_0_), channel_id=1, source_target_pairs={{0,16},{1,17},{2,18},{3,19},{16,0},{17,1},{18,2},{19,3},{4,20},{5,... | collective-permute-start | bytes 196616 | tf_op jit(solution)/shard_map/ppermute | solution.py:365
  69.7 1.1 %collective-permute-start.20 = (bf16[128,256]{1,0:T(8,128)(2,1)S(1)}, bf16[128,256]{1,0:T(8,128)(2,1)S(1)}, u32[]{:S(2)}, u32[]{:S(2)}) collective-permute-start(bf16[128,256]{1,0:T(8,128)(2,1)S(1)} %seq_sum_1.1.refs_0_), channel_id=1, source_target_pairs={{0,18},{1,19},{2,16},{3,17},{16,2},{17,3},{18,0},{19,1},{4,22},{5,... | collective-permute-start | bytes 196616 | tf_op jit(solution)/shard_map/ppermute | solution.py:365
  70.7 0.8 collective-permute-done.18.refs_1_
  71.5 1.2 %collective-permute-done.19.refs_2_ = bf16[128,256]{1,0:T(8,128)(2,1)S(1)} collective-permute-done((bf16[128,256]{1,0:T(8,128)(2,1)S(1)}, bf16[128,256]{1,0:T(8,128)(2,1)S(1)}, u32[]{:S(2)}, u32[]{:S(2)}) %collective-permute-start.19) | collective-permute-done | bytes 65568 | tf_op jit(solution)/shard_map/ppermute | solution.py:365
  72.7 2.1 %collective-permute-done.20.refs_3_ = bf16[128,256]{1,0:T(8,128)(2,1)S(1)} collective-permute-done((bf16[128,256]{1,0:T(8,128)(2,1)S(1)}, bf16[128,256]{1,0:T(8,128)(2,1)S(1)}, u32[]{:S(2)}, u32[]{:S(2)}) %collective-permute-start.20) | collective-permute-done | bytes 65568 | tf_op jit(solution)/shard_map/ppermute | solution.py:365
  74.8 1.6 %collective-permute-start.21 = (bf16[64,1024]{1,0:T(8,128)(2,1)S(1)}, bf16[64,1024]{1,0:T(8,128)(2,1)S(1)}, u32[]{:S(2)}, u32[]{:S(2)}) collective-permute-start(bf16[64,1024]{1,0:T(8,128)(2,1)S(1)} %get-tuple-element.111), channel_id=1, source_target_pairs={{0,4},{4,0},{8,12},{12,8},{1,5},{5,1},{9,13},{13,9},{2,6},{6,2},{1... | collective-permute-start | bytes 393224 | tf_op jit(solution)/shard_map/ppermute | solution.py:365
  78.4 1.6 %lay_whole.1 = f32[1024,256]{1,0:T(8,128)} custom-call(s32[7]{0:T(128)S(1)} %stack.27.info_ref, bf16[128,256]{1,0:T(8,128)(2,1)S(1)} %seq_sum_1.1.refs_0_, bf16[128,256]{1,0:T(8,128)(2,1)S(1)} %collective-permute-done.18.refs_1_, bf16[128,256]{1,0:T(8,128)(2,1)S(1)} %collective-permute-done.19.refs_2_, bf16[128,256]{1,0:T(8,128)(2,1)S(1)} %collective-permute-done.20.refs_3_, ...), custom_call_target="tpu_custom_call" | custom-call | tf_op jit(solution)/shard_map/lay_whole/pallas_call | solution.py:352
  80.0 1.3 %neg_sum.1 = (f32[1,256]{1,0:T(1,128)}, f32[64,1024]{1,0:T(8,128)}) custom-call(s32[7]{0:T(128)S(1)} %stack.27.info_ref, f32[1,256]{1,0:T(1,128)S(1)} %get-tuple-element.88.loss_ref, bf16[144,256]{1,0:T(8,128)(2,1)S(1)} %collective-permute-done.17.refs_1_.got_ref, f32[64,1024]{1,0:T(8,128)S(1)} %get-tuple-element.109.part_ref, ...), custom_call_target="tpu_custom_call" | custom-call | flops 517500000 | tf_op jit(solution)/shard_map/neg_sum/pallas_call | solution.py:352
  (62 shorter events, 8.1 us)
Async XLA Ops:
  0.6 19.2 %collective-permute-start = (bf16[256,1024]{1,0:T(8,128)(2,1)}, bf16[256,1024]{1,0:T(8,128)(2,1)S(1)}, u32[]{:S(2)}, u32[]{:S(2)}) collective-permute-start(bf16[256,1024]{1,0:T(8,128)(2,1)} %bitcast.15), channel_id=1, source_target_pairs={{0,4},{4,8},{1,5},{5,9},{2,6},{6,10},{3,7},{7,11},{16,20},{20,24},... | collective-permute-start | bytes 1572872 | tf_op jit(solution)/shard_map/ppermute | solution.py:399
  5.6 14.2 %collective-permute-start.1 = (bf16[256,1024]{1,0:T(8,128)(2,1)}, bf16[256,1024]{1,0:T(8,128)(2,1)S(1)}, u32[]{:S(2)}, u32[]{:S(2)}) collective-permute-start(bf16[256,1024]{1,0:T(8,128)(2,1)} %bitcast.16), channel_id=1, source_target_pairs={{12,8},{13,9},{14,10},{15,11},{28,24},{29,25},{30,26},{31,27}} | collective-permute-start | bytes 1572872 | tf_op jit(solution)/shard_map/ppermute | solution.py:400
  12.0 8.5 %copy-start = (bf16[1024,4096]{1,0:T(8,128)(2,1)S(1)}, bf16[1024,4096]{1,0:T(8,128)(2,1)}, u32[]{:S(2)}) copy-start(bf16[1024,4096]{1,0:T(8,128)(2,1)} %w_ref.5) | copy-start | bytes 25165828
  12.0 8.5 %copy-start.3 = (bf16[1,256,1024]{2,1,0:T(8,128)(2,1)S(1)}, bf16[1,256,1024]{2,1,0:T(8,128)(2,1)}, u32[]{:S(2)}) copy-start(bf16[1,256,1024]{2,1,0:T(8,128)(2,1)} %param.9) | copy-start | bytes 1572868
  18.2 13.8 %collective-permute-start.3 = (bf16[1056,256]{1,0:T(8,128)(2,1)S(1)}, bf16[1056,256]{1,0:T(8,128)(2,1)S(1)}, u32[]{:S(2)}, u32[]{:S(2)}) collective-permute-start(bf16[1056,256]{1,0:T(8,128)(2,1)S(1)} %get-tuple-element.86.rest_0_), channel_id=1, source_target_pairs={{0,2},{1,3},{2,0},{3,1},{4,6},{5,7},{6,4},{7,5},{8,10},{9,11},{10,... | collective-permute-start | bytes 1622024 | tf_op jit(solution)/shard_map/ppermute | solution.py:365
  19.8 13.6 %collective-permute-start.2 = (bf16[256,1024]{1,0:T(8,128)(2,1)S(1)}, bf16[256,1024]{1,0:T(8,128)(2,1)S(1)}, u32[]{:S(2)}, u32[]{:S(2)}) collective-permute-start(bf16[256,1024]{1,0:T(8,128)(2,1)S(1)} %collective-permute-done.x_ref), channel_id=1, source_target_pairs={{4,8},{5,9},{6,10},{7,11},{20,24},{21,25},{22,26},{23,27}} | collective-permute-start | bytes 1572872 | tf_op jit(solution)/shard_map/ppermute | solution.py:433
  32.0 9.0 %collective-permute-start.5 = (bf16[1056,256]{1,0:T(8,128)(2,1)S(1)}, bf16[1056,256]{1,0:T(8,128)(2,1)S(1)}, u32[]{:S(2)}, u32[]{:S(2)}) collective-permute-start(bf16[1056,256]{1,0:T(8,128)(2,1)S(1)} %get-tuple-element.86.rest_0_), channel_id=1, source_target_pairs={{0,1},{1,0},{2,3},{3,2},{4,5},{5,4},{6,7},{7,6},{8,9},{9,8},{10,11... | collective-permute-start | bytes 1622024 | tf_op jit(solution)/shard_map/ppermute | solution.py:365
  32.0 9.0 %collective-permute-start.6 = (bf16[1056,256]{1,0:T(8,128)(2,1)S(1)}, bf16[1056,256]{1,0:T(8,128)(2,1)S(1)}, u32[]{:S(2)}, u32[]{:S(2)}) collective-permute-start(bf16[1056,256]{1,0:T(8,128)(2,1)S(1)} %collective-permute-done.3.rest_1_), channel_id=1, source_target_pairs={{0,1},{1,0},{2,3},{3,2},{4,5},{5,4},{6,7},{7,6},{8,9},{9,8},{10,11... | collective-permute-start | bytes 1622024 | tf_op jit(solution)/shard_map/ppermute | solution.py:365
  32.6 8.5 %collective-permute-start.4 = (bf16[272,256]{1,0:T(8,128)(2,1)S(1)}, bf16[272,256]{1,0:T(8,128)(2,1)S(1)}, u32[]{:S(2)}, u32[]{:S(2)}) collective-permute-start(bf16[272,256]{1,0:T(8,128)(2,1)S(1)} %get-tuple-element.85), channel_id=1, source_target_pairs={{12,8},{13,9},{14,10},{15,11},{28,24},{29,25},{30,26},{31,27}} | collective-permute-start | bytes 417800 | tf_op jit(solution)/shard_map/ppermute | solution.py:450
  39.5 8.3 %collective-permute-start.12 = (bf16[512,256]{1,0:T(8,128)(2,1)S(1)}, bf16[512,256]{1,0:T(8,128)(2,1)S(1)}, u32[]{:S(2)}, u32[]{:S(2)}) collective-permute-start(bf16[512,256]{1,0:T(8,128)(2,1)S(1)} %get-tuple-element.97.hat_ref.rest_0_), channel_id=1, source_target_pairs={{0,2},{1,3},{2,0},{3,1},{4,6},{5,7},{6,4},{7,5},{8,10},{9,11},{10,... | collective-permute-start | bytes 786440 | tf_op jit(solution)/shard_map/ppermute | solution.py:365
  46.2 12.7 %copy-start.6 = (bf16[1,1024,256]{2,1,0:T(8,128)(2,1)S(1)}, bf16[1,1024,256]{2,1,0:T(8,128)(2,1)}, u32[]{:S(2)}) copy-start(bf16[1,1024,256]{2,1,0:T(8,128)(2,1)} %param.16) | copy-start | bytes 1572868
  46.2 12.7 %copy-start.10 = (s32[1,1024]{1,0:T(1,128)S(1)}, s32[1,1024]{1,0:T(1,128)}, u32[]{:S(2)}) copy-start(s32[1,1024]{1,0:T(1,128)} %neg_id_ref.1) | copy-start | bytes 12292
  46.3 1.6 %collective-permute-start.7 = (bf16[512,256]{1,0:T(8,128)(2,1)S(1)}, bf16[512,256]{1,0:T(8,128)(2,1)S(1)}, u32[]{:S(2)}, u32[]{:S(2)}) collective-permute-start(bf16[512,256]{1,0:T(8,128)(2,1)S(1)} %get-tuple-element.91), channel_id=1, source_target_pairs={{0,1},{1,0},{2,3},{3,2},{16,17},{17,16},{18,19},{19,18},{4,5},{5,4... | collective-permute-start | bytes 786440 | tf_op jit(solution)/shard_map/ppermute | solution.py:365
  46.3 12.5 %collective-permute-start.13 = (bf16[512,256]{1,0:T(8,128)(2,1)S(1)}, bf16[512,256]{1,0:T(8,128)(2,1)S(1)}, u32[]{:S(2)}, u32[]{:S(2)}) collective-permute-start(bf16[512,256]{1,0:T(8,128)(2,1)S(1)} %get-tuple-element.97.hat_ref.rest_0_), channel_id=1, source_target_pairs={{0,1},{1,0},{2,3},{3,2},{4,5},{5,4},{6,7},{7,6},{8,9},{9,8},{10,11... | collective-permute-start | bytes 786440 | tf_op jit(solution)/shard_map/ppermute | solution.py:365
  47.8 11.1 %collective-permute-start.14 = (bf16[512,256]{1,0:T(8,128)(2,1)S(1)}, bf16[512,256]{1,0:T(8,128)(2,1)S(1)}, u32[]{:S(2)}, u32[]{:S(2)}) collective-permute-start(bf16[512,256]{1,0:T(8,128)(2,1)S(1)} %collective-permute-done.12.rest_1_), channel_id=1, source_target_pairs={{0,1},{1,0},{2,3},{3,2},{4,5},{5,4},{6,7},{7,6},{8,9},{9,8},{10,11... | collective-permute-start | bytes 786440 | tf_op jit(solution)/shard_map/ppermute | solution.py:365
  48.5 4.9 %collective-permute-start.8 = (bf16[144,256]{1,0:T(8,128)(2,1)S(1)}, bf16[144,256]{1,0:T(8,128)(2,1)S(1)}, u32[]{:S(2)}, u32[]{:S(2)}) collective-permute-start(bf16[144,256]{1,0:T(8,128)(2,1)S(1)} %get-tuple-element.94), channel_id=1, source_target_pairs={{0,2},{1,3},{2,0},{3,1},{16,18},{17,19},{18,16},{19,17},{4,6},{5,7... | collective-permute-start | bytes 221192 | tf_op jit(solution)/shard_map/ppermute | solution.py:365
  50.0 5.5 %collective-permute-start.10 = (bf16[128,256]{1,0:T(8,128)(2,1)S(1)}, bf16[128,256]{1,0:T(8,128)(2,1)S(1)}, u32[]{:S(2)}, u32[]{:S(2)}) collective-permute-start(bf16[128,256]{1,0:T(8,128)(2,1)S(1)} %get-tuple-element.96), channel_id=1, source_target_pairs={{0,18},{1,19},{2,16},{3,17},{16,2},{17,3},{18,0},{19,1},{4,22},{5,... | collective-permute-start | bytes 196616 | tf_op jit(solution)/shard_map/ppermute | solution.py:365
  51.5 4.3 %collective-permute-start.9 = (bf16[128,256]{1,0:T(8,128)(2,1)S(1)}, bf16[128,256]{1,0:T(8,128)(2,1)S(1)}, u32[]{:S(2)}, u32[]{:S(2)}) collective-permute-start(bf16[128,256]{1,0:T(8,128)(2,1)S(1)} %get-tuple-element.95), channel_id=1, source_target_pairs={{0,16},{1,17},{2,18},{3,19},{16,0},{17,1},{18,2},{19,3},{4,20},{5,... | collective-permute-start | bytes 196616 | tf_op jit(solution)/shard_map/ppermute | solution.py:365
  53.4 5.5 %collective-permute-start.16 = (bf16[144,256]{1,0:T(8,128)(2,1)S(1)}, bf16[144,256]{1,0:T(8,128)(2,1)S(1)}, u32[]{:S(2)}, u32[]{:S(2)}) collective-permute-start(bf16[144,256]{1,0:T(8,128)(2,1)S(1)} %collective-permute-done.8.refs_1_.rest_5_), channel_id=1, source_target_pairs={{0,1},{1,0},{2,3},{3,2},{4,5},{5,4},{6,7},{7,6},{8,9},{9,8},{10,11... | collective-permute-start | bytes 221192 | tf_op jit(solution)/shard_map/ppermute | solution.py:365
  55.5 3.4 %collective-permute-start.15 = (bf16[16,256]{1,0:T(8,128)(2,1)S(1)}, bf16[16,256]{1,0:T(8,128)(2,1)S(1)}, u32[]{:S(2)}, u32[]{:S(2)}) collective-permute-start(bf16[16,256]{1,0:T(8,128)(2,1)S(1)} %get-tuple-element.101.message_ref.rest_4_), channel_id=1, source_target_pairs={{0,1},{1,0},{2,3},{3,2},{4,5},{5,4},{6,7},{7,6},{8,9},{9,8},{10,11... | collective-permute-start | bytes 24584 | tf_op jit(solution)/shard_map/ppermute | solution.py:365
  55.8 6.8 %collective-permute-start.11 = (bf16[128,256]{1,0:T(8,128)(2,1)S(1)}, bf16[128,256]{1,0:T(8,128)(2,1)S(1)}, u32[]{:S(2)}, u32[]{:S(2)}) collective-permute-start(bf16[128,256]{1,0:T(8,128)(2,1)S(1)} %plane_sum.1.refs_0_), channel_id=1, source_target_pairs={{0,8},{4,12},{8,0},{12,4},{1,9},{5,13},{9,1},{13,5},{2,10},{6,14},... | collective-permute-start | bytes 196616 | tf_op jit(solution)/shard_map/ppermute | solution.py:365
  62.7 4.5 %collective-permute-start.17 = (bf16[144,256]{1,0:T(8,128)(2,1)S(1)}, bf16[144,256]{1,0:T(8,128)(2,1)S(1)}, u32[]{:S(2)}, u32[]{:S(2)}) collective-permute-start(bf16[144,256]{1,0:T(8,128)(2,1)S(1)} %seq_sum_2.1.refs_0_), channel_id=1, source_target_pairs={{0,4},{4,0},{8,12},{12,8},{1,5},{5,1},{9,13},{13,9},{2,6},{6,2},{1... | collective-permute-start | bytes 221192 | tf_op jit(solution)/shard_map/ppermute | solution.py:365
  64.3 12.2 %collective-permute-start.22 = (bf16[64,1024]{1,0:T(8,128)(2,1)S(1)}, bf16[64,1024]{1,0:T(8,128)(2,1)S(1)}, u32[]{:S(2)}, u32[]{:S(2)}) collective-permute-start(bf16[64,1024]{1,0:T(8,128)(2,1)S(1)} %get-tuple-element.112), channel_id=1, source_target_pairs={{0,8},{4,12},{8,0},{12,4},{1,9},{5,13},{9,1},{13,5},{2,10},{6,14},... | collective-permute-start | bytes 393224 | tf_op jit(solution)/shard_map/ppermute | solution.py:365
  66.3 10.2 %collective-permute-start.23 = (bf16[64,1024]{1,0:T(8,128)(2,1)S(1)}, bf16[64,1024]{1,0:T(8,128)(2,1)S(1)}, u32[]{:S(2)}, u32[]{:S(2)}) collective-permute-start(bf16[64,1024]{1,0:T(8,128)(2,1)S(1)} %get-tuple-element.113), channel_id=1, source_target_pairs={{0,12},{4,8},{8,4},{12,0},{1,13},{5,9},{9,5},{13,1},{2,14},{6,10},... | collective-permute-start | bytes 393224 | tf_op jit(solution)/shard_map/ppermute | solution.py:365
  67.2 4.3 %collective-permute-start.18 = (bf16[128,256]{1,0:T(8,128)(2,1)S(1)}, bf16[128,256]{1,0:T(8,128)(2,1)S(1)}, u32[]{:S(2)}, u32[]{:S(2)}) collective-permute-start(bf16[128,256]{1,0:T(8,128)(2,1)S(1)} %seq_sum_1.1.refs_0_), channel_id=1, source_target_pairs={{0,2},{1,3},{2,0},{3,1},{16,18},{17,19},{18,16},{19,17},{4,6},{5,7... | collective-permute-start | bytes 196616 | tf_op jit(solution)/shard_map/ppermute | solution.py:365
  68.4 4.3 %collective-permute-start.19 = (bf16[128,256]{1,0:T(8,128)(2,1)S(1)}, bf16[128,256]{1,0:T(8,128)(2,1)S(1)}, u32[]{:S(2)}, u32[]{:S(2)}) collective-permute-start(bf16[128,256]{1,0:T(8,128)(2,1)S(1)} %seq_sum_1.1.refs_0_), channel_id=1, source_target_pairs={{0,16},{1,17},{2,18},{3,19},{16,0},{17,1},{18,2},{19,3},{4,20},{5,... | collective-permute-start | bytes 196616 | tf_op jit(solution)/shard_map/ppermute | solution.py:365
  69.7 5.2 %collective-permute-start.20 = (bf16[128,256]{1,0:T(8,128)(2,1)S(1)}, bf16[128,256]{1,0:T(8,128)(2,1)S(1)}, u32[]{:S(2)}, u32[]{:S(2)}) collective-permute-start(bf16[128,256]{1,0:T(8,128)(2,1)S(1)} %seq_sum_1.1.refs_0_), channel_id=1, source_target_pairs={{0,18},{1,19},{2,16},{3,17},{16,2},{17,3},{18,0},{19,1},{4,22},{5,... | collective-permute-start | bytes 196616 | tf_op jit(solution)/shard_map/ppermute | solution.py:365
  74.8 5.1 %collective-permute-start.21 = (bf16[64,1024]{1,0:T(8,128)(2,1)S(1)}, bf16[64,1024]{1,0:T(8,128)(2,1)S(1)}, u32[]{:S(2)}, u32[]{:S(2)}) collective-permute-start(bf16[64,1024]{1,0:T(8,128)(2,1)S(1)} %get-tuple-element.111), channel_id=1, source_target_pairs={{0,4},{4,0},{8,12},{12,8},{1,5},{5,1},{9,13},{13,9},{2,6},{6,2},{1... | collective-permute-start | bytes 393224 | tf_op jit(solution)/shard_map/ppermute | solution.py:365
  76.4 1.3 %collective-permute-start.24 = (bf16[128,256]{1,0:T(8,128)(2,1)S(1)}, bf16[128,256]{1,0:T(8,128)(2,1)S(1)}, u32[]{:S(2)}, u32[]{:S(2)}) collective-permute-start(bf16[128,256]{1,0:T(8,128)(2,1)S(1)} %seq_sum_1.1.refs_0_), channel_id=1, source_target_pairs={{0,1},{1,0},{2,3},{3,2},{16,17},{17,16},{18,19},{19,18},{4,5},{5,4... | collective-permute-start | bytes 196616 | tf_op jit(solution)/shard_map/ppermute | solution.py:365
  76.5 1.4 %collective-permute-start.25 = (bf16[128,256]{1,0:T(8,128)(2,1)S(1)}, bf16[128,256]{1,0:T(8,128)(2,1)S(1)}, u32[]{:S(2)}, u32[]{:S(2)}) collective-permute-start(bf16[128,256]{1,0:T(8,128)(2,1)S(1)} %collective-permute-done.18.refs_1_), channel_id=1, source_target_pairs={{0,1},{1,0},{2,3},{3,2},{16,17},{17,16},{18,19},{19,18},{4,5},{5,4... | collective-permute-start | bytes 196616 | tf_op jit(solution)/shard_map/ppermute | solution.py:365
  77.0 1.3 %collective-permute-start.26 = (bf16[128,256]{1,0:T(8,128)(2,1)S(1)}, bf16[128,256]{1,0:T(8,128)(2,1)S(1)}, u32[]{:S(2)}, u32[]{:S(2)}) collective-permute-start(bf16[128,256]{1,0:T(8,128)(2,1)S(1)} %collective-permute-done.19.refs_2_), channel_id=1, source_target_pairs={{0,1},{1,0},{2,3},{3,2},{16,17},{17,16},{18,19},{19,18},{4,5},{5,4... | collective-permute-start | bytes 196616 | tf_op jit(solution)/shard_map/ppermute | solution.py:365
  77.0 1.3 %collective-permute-start.27 = (bf16[128,256]{1,0:T(8,128)(2,1)S(1)}, bf16[128,256]{1,0:T(8,128)(2,1)S(1)}, u32[]{:S(2)}, u32[]{:S(2)}) collective-permute-start(bf16[128,256]{1,0:T(8,128)(2,1)S(1)} %collective-permute-done.20.refs_3_), channel_id=1, source_target_pairs={{0,1},{1,0},{2,3},{3,2},{16,17},{17,16},{18,19},{19,18},{4,5},{5,4... | collective-permute-start | bytes 196616 | tf_op jit(solution)/shard_map/ppermute | solution.py:365
  (8 other events, 27.8 us)

commit v5 on v4

--- a/solution.py
+++ b/solution.py
@@ -302,12 +302,13 @@
     out_ref[rows:, :] = jnp.concatenate(parts + [pad], axis=0).astype(BF16)
 
 
-def last_sum_kernel(last, info_ref, loss_ref, got_ref, part_ref, *rest):
-    *got_refs, own_loss_ref, sum_ref = rest
-    parts = got_ref[got_ref.shape[0] - 16 :, :].astype(F32)
+def final_kernel(last, count, info_ref, loss_ref, loss_got_ref, *refs):
+    proj_refs, (*part_refs, own_loss_ref, sum_ref, proj_ref) = refs[:count], refs[count:]
+    parts = loss_got_ref[loss_got_ref.shape[0] - 16 :, :].astype(F32)
     above = parts[0:1, :] + parts[1:2, :] + parts[2:3, :]
     own_loss_ref[...] = jnp.where(info_ref[2] == last, above, loss_ref[...])
-    sum_kernel(part_ref, *got_refs, sum_ref)
+    lay_kernel(info_ref, *proj_refs, proj_ref)
+    sum_kernel(*part_refs, sum_ref)
 
 
 def negative_kernel(pool_count, info_ref, neg_ref, neg_id_ref, *rest):
@@ -521,17 +522,16 @@
     proj_part = call(sum_kernel, [proj_part, loss_got], part, name="seq_sum_1")
     gots = [swap(x, "seq", seq_count, r) for r, x in enumerate(sends[1:], 2)]
     others = plane_swap([proj_part] * (chips - 1))
-    first, _ = together(sends[0], others)
+    first, _ = together(sends[0], others[chip - 1])
     others, gots = together(others, gots)
     gots = [swap(first, "seq", seq_count, 1)] + gots
     proj_parts = [proj_part] + others
     proj_parts += [swap(x, plane, plane_count, 1) for x in proj_parts]
-    d_proj = call(lay_kernel, [info, *proj_parts], struct((width, embed), F32), micros=0, name="lay_whole")
-    loss, d_neg = call(
-        functools.partial(last_sum_kernel, seq_count - 1),
-        [info, loss, loss_got, d_part, *gots],
-        [struct((1, rows), F32), struct((cols, local_neg), F32)],
-        micros=0.9, name="neg_sum",
+    loss, d_neg, d_proj = call(
+        functools.partial(final_kernel, seq_count - 1, 2 * chips),
+        [info, loss, loss_got, *proj_parts, d_part, *gots],
+        [struct((1, rows), F32), struct((cols, local_neg), F32), struct((width, embed), F32)],
+        micros=2, name="final",
     )
     return (loss, d_neg.T[None], d_proj)
 

time: 81.6 us -> 80.5 us (0.987)
  waiting for transfers between devices: 12.7 us -> 11.5 us
  Pallas kernels: 33.9 us -> 32.7 us
  starting transfers between devices: 28.7 us -> 29.8 us
    ppermute x24, waiting for transfers between devices: 12.7 us -> 11.4 us  [swap(): return lax.ppermute(x, axis, [(i, i ^ r) for i in range(count)])]
    pallas_call x13 -> x12, Pallas kernels: 33.9 us -> 32.7 us  [call(): pl.pallas_call(kernel, out_shape=list(outs) if many else outs, in_specs=i...]
    ppermute x24, starting transfers between devices: 21.5 us -> 22.6 us  [swap(): return lax.ppermute(x, axis, [(i, i ^ r) for i in range(count)])]
  transfers between devices with their start and end apart: 28 -> 28, of which waited for: 13 -> 12; matrix products, arithmetic and copies ran while one was open for 0% -> 0% of each run, Pallas kernels for 40% -> 39%
where the time goes in v5:
time: 80.5 us; the launch traced here: 80 us
  Pallas kernels  32.7 us (41%)
  starting transfers between devices  29.8 us (37%)
  waiting for transfers between devices  11.5 us (14%)
  local copies, waits for them, and re-layouts  4.47 us (6%)
  between operations  1.58 us (2%)
    pallas_call x12, Pallas kernels, call(): pl.pallas_call(kernel, out_shape=list(outs) if many else outs, in_specs=i...  32.7 us
    ppermute x24, starting transfers between devices, swap(): return lax.ppermute(x, axis, [(i, i ^ r) for i in range(count)])  22.6 us
    ppermute x24, waiting for transfers between devices, swap(): return lax.ppermute(x, axis, [(i, i ^ r) for i in range(count)])  11.4 us
    ppermute x1, starting transfers between devices, body(): block = lax.ppermute(own, 'seq', ups[0])  4.96 us
    unnamed x24, local copies, waits for them, and re-layouts  4.39 us
  transfers between devices with their start and end apart: 28, of which 12 were waited for; matrix products, arithmetic and copies ran while one was open for 0% of the time, Pallas kernels for 39%

profile of v5, /device:TPU:0, one launch (start us, length us, event | category | flops | bytes accessed | tf_op | source)
XLA Modules:
  0.0 80.0 jit_solution(18092347225564769507)
XLA Ops:
  0.6 5.0 %collective-permute-start = (bf16[256,1024]{1,0:T(8,128)(2,1)}, bf16[256,1024]{1,0:T(8,128)(2,1)S(1)}, u32[]{:S(2)}, u32[]{:S(2)}) collective-permute-start(bf16[256,1024]{1,0:T(8,128)(2,1)} %bitcast.15), channel_id=1, source_target_pairs={{0,4},{4,8},{1,5},{5,9},{2,6},{6,10},{3,7},{7,11},{16,20},{20,24},... | collective-permute-start | bytes 1572872 | tf_op jit(solution)/shard_map/ppermute | solution.py:400
  5.6 0.7 collective-permute-start.1
  7.1 1.0 %copy-done.5 = bf16[1,1024,256]{2,1,0:T(8,128)(2,1)S(1)} copy-done((bf16[1,1024,256]{2,1,0:T(8,128)(2,1)S(1)}, bf16[1,1024,256]{2,1,0:T(8,128)(2,1)}, u32[]{:S(2)}) %copy-start.5) | copy-done | bytes 524312
  8.1 0.9 %copy-done.7 = bf16[1,256,256]{2,1,0:T(8,128)(2,1)S(1)} copy-done((bf16[1,256,256]{2,1,0:T(8,128)(2,1)S(1)}, bf16[1,256,256]{2,1,0:T(8,128)(2,1)}, u32[]{:S(2)}) %copy-start.7) | copy-done | bytes 131096
  9.0 0.7 copy-done.9
  11.0 1.0 %copy-done.2 = bf16[1,256,1024]{2,1,0:T(8,128)(2,1)S(1)} copy-done((bf16[1,256,1024]{2,1,0:T(8,128)(2,1)S(1)}, bf16[1,256,1024]{2,1,0:T(8,128)(2,1)}, u32[]{:S(2)}) %copy-start.2) | copy-done | bytes 524312
  12.0 6.2 %own_block.1 = (bf16[256,1024]{1,0:T(8,128)(2,1)S(1)}, bf16[256,1024]{1,0:T(8,128)(2,1)S(1)}, bf16[256,1024]{1,0:T(8,128)(2,1)S(1)}, bf16[256,1024]{1,0:T(8,128)(2,1)S(1)}, f32[256,1024]{1,0:T(8,128)S(1)}) custom-call(s32[7]{0:T(128)S(1)} %stack.27.info_ref, bf16[256,1024]{1,0:T(8,128)(2,1)S(1)} %bitcast.17, bf16[1024,4096]{1,0:T(8,128)(2,1)} %w_ref.5), custom_call_target="tpu_custom_call" | custom-call | flops 3449999872 | tf_op jit(solution)/shard_map/own_block/pallas_call | solution.py:353
  18.2 1.6 %collective-permute-start.3 = (bf16[1056,256]{1,0:T(8,128)(2,1)S(1)}, bf16[1056,256]{1,0:T(8,128)(2,1)S(1)}, u32[]{:S(2)}, u32[]{:S(2)}) collective-permute-start(bf16[1056,256]{1,0:T(8,128)(2,1)S(1)} %get-tuple-element.87.rest_0_), channel_id=1, source_target_pairs={{0,2},{1,3},{2,0},{3,1},{4,6},{5,7},{6,4},{7,5},{8,10},{9,11},{10,... | collective-permute-start | bytes 1622024 | tf_op jit(solution)/shard_map/ppermute | solution.py:366
  20.5 5.0 %guest_block.1 = (bf16[512,1024]{1,0:T(8,128)(2,1)S(1)}, bf16[512,1024]{1,0:T(8,128)(2,1)S(1)}, bf16[512,1024]{1,0:T(8,128)(2,1)S(1)}, f32[512,1024]{1,0:T(8,128)S(1)}) custom-call(s32[7]{0:T(128)S(1)} %stack.27.info_ref, bf16[256,1024]{1,0:T(8,128)(2,1)S(1)} %collective-permute-done.1.x_ref, bf16[1024,4096]{1,0:T(8,128)(2,1)S(1)} %copy-done, ...), custom_call_target="tpu_custom_call" | custom-call | flops 2760000000 | tf_op jit(solution)/shard_map/guest_block/pallas_call | solution.py:353
  25.6 3.6 %earlier_block_1.1.before_ref = f32[512,1024]{1,0:T(8,128)S(1)} custom-call(s32[7]{0:T(128)S(1)} %stack.27.info_ref, bf16[256,1024]{1,0:T(8,128)(2,1)S(1)} %collective-permute-done.x_ref, bf16[1024,4096]{1,0:T(8,128)(2,1)S(1)} %copy-done, bf16[512,1024]{1,0:T(8,128)(2,1)S(1)} %get-tuple-element.74.q_ref, f32[512,1024]{1,0:T(8,128)S(1)} %get-tuple-element.75.before_ref), custom_call_target="tpu_custom_call" | custom-call | flops 2070000000 | tf_op jit(solution)/shard_map/earlier_block_1/pallas_call | solution.py:353
  29.1 2.9 %collective-permute-done.3.rest_1_ = bf16[1056,256]{1,0:T(8,128)(2,1)S(1)} collective-permute-done((bf16[1056,256]{1,0:T(8,128)(2,1)S(1)}, bf16[1056,256]{1,0:T(8,128)(2,1)S(1)}, u32[]{:S(2)}, u32[]{:S(2)}) %collective-permute-start.3) | collective-permute-done | bytes 540704 | tf_op jit(solution)/shard_map/ppermute | solution.py:366
  32.6 0.8 %collective-permute-start.4 = (bf16[272,256]{1,0:T(8,128)(2,1)S(1)}, bf16[272,256]{1,0:T(8,128)(2,1)S(1)}, u32[]{:S(2)}, u32[]{:S(2)}) collective-permute-start(bf16[272,256]{1,0:T(8,128)(2,1)S(1)} %get-tuple-element.86), channel_id=1, source_target_pairs={{12,8},{13,9},{14,10},{15,11},{28,24},{29,25},{30,26},{31,27}} | collective-permute-start | bytes 417800 | tf_op jit(solution)/shard_map/ppermute | solution.py:451
  33.4 6.0 %last_block.1 = (bf16[512,1024]{1,0:T(8,128)(2,1)S(1)}, f32[512,256]{1,0:T(8,128)S(1)}, bf16[512,256]{1,0:T(8,128)(2,1)S(1)}) custom-call(s32[7]{0:T(128)S(1)} %stack.27.info_ref, bf16[256,1024]{1,0:T(8,128)(2,1)S(1)} %collective-permute-done.2.x_ref, bf16[1024,4096]{1,0:T(8,128)(2,1)S(1)} %copy-done, bf16[512,1024]{1,0:T(8,128)(2,1)S(1)} %get-tuple-element.74.q_ref, ...), custom_call_target="tpu_custom_call" | custom-call | flops 3449999872 | tf_op jit(solution)/shard_map/last_block/pallas_call | solution.py:353
  39.5 1.6 %collective-permute-start.12 = (bf16[512,256]{1,0:T(8,128)(2,1)S(1)}, bf16[512,256]{1,0:T(8,128)(2,1)S(1)}, u32[]{:S(2)}, u32[]{:S(2)}) collective-permute-start(bf16[512,256]{1,0:T(8,128)(2,1)S(1)} %get-tuple-element.98.hat_ref.rest_0_), channel_id=1, source_target_pairs={{0,2},{1,3},{2,0},{3,1},{4,6},{5,7},{6,4},{7,5},{8,10},{9,11},{10,... | collective-permute-start | bytes 786440 | tf_op jit(solution)/shard_map/ppermute | solution.py:366
  41.1 5.1 %head.1 = (f32[1,256]{1,0:T(1,128)S(1)}, f32[1,256]{1,0:T(1,128)S(1)}, bf16[16,256]{1,0:T(8,128)(2,1)S(1)}, f32[512,256]{1,0:T(8,128)S(1)}, bf16[512,256]{1,0:T(8,128)(2,1)S(1)}) custom-call(s32[7]{0:T(128)S(1)} %stack.27.info_ref, bf16[512,256]{1,0:T(8,128)(2,1)S(1)} %get-tuple-element.98.hat_ref.rest_0_, f32[512,256]{1,0:T(8,128)S(1)} %get-tuple-element.84.out_ref, ...), custom_call_target="tpu_custom_call" | custom-call | flops 2875000064 | tf_op jit(solution)/shard_map/head/pallas_call | solution.py:353
  46.8 0.9 %collective-permute-done.12.rest_1_ = bf16[512,256]{1,0:T(8,128)(2,1)S(1)} collective-permute-done((bf16[512,256]{1,0:T(8,128)(2,1)S(1)}, bf16[512,256]{1,0:T(8,128)(2,1)S(1)}, u32[]{:S(2)}, u32[]{:S(2)}) %collective-permute-start.12) | collective-permute-done | bytes 262176 | tf_op jit(solution)/shard_map/ppermute | solution.py:366
  48.5 1.5 %collective-permute-start.8 = (bf16[144,256]{1,0:T(8,128)(2,1)S(1)}, bf16[144,256]{1,0:T(8,128)(2,1)S(1)}, u32[]{:S(2)}, u32[]{:S(2)}) collective-permute-start(bf16[144,256]{1,0:T(8,128)(2,1)S(1)} %get-tuple-element.95), channel_id=1, source_target_pairs={{0,2},{1,3},{2,0},{3,1},{16,18},{17,19},{18,16},{19,17},{4,6},{5,7... | collective-permute-start | bytes 221192 | tf_op jit(solution)/shard_map/ppermute | solution.py:366
  50.0 1.5 %collective-permute-start.10 = (bf16[128,256]{1,0:T(8,128)(2,1)S(1)}, bf16[128,256]{1,0:T(8,128)(2,1)S(1)}, u32[]{:S(2)}, u32[]{:S(2)}) collective-permute-start(bf16[128,256]{1,0:T(8,128)(2,1)S(1)} %get-tuple-element.97), channel_id=1, source_target_pairs={{0,18},{1,19},{2,16},{3,17},{16,2},{17,3},{18,0},{19,1},{4,22},{5,... | collective-permute-start | bytes 196616 | tf_op jit(solution)/shard_map/ppermute | solution.py:366
  52.0 1.3 %collective-permute-done.8.refs_1_.rest_5_ = bf16[144,256]{1,0:T(8,128)(2,1)S(1)} collective-permute-done((bf16[144,256]{1,0:T(8,128)(2,1)S(1)}, bf16[144,256]{1,0:T(8,128)(2,1)S(1)}, u32[]{:S(2)}, u32[]{:S(2)}) %collective-permute-start.8) | collective-permute-done | bytes 73760 | tf_op jit(solution)/shard_map/ppermute | solution.py:366
  53.4 2.1 %collective-permute-done.10.refs_3_ = bf16[128,256]{1,0:T(8,128)(2,1)S(1)} collective-permute-done((bf16[128,256]{1,0:T(8,128)(2,1)S(1)}, bf16[128,256]{1,0:T(8,128)(2,1)S(1)}, u32[]{:S(2)}, u32[]{:S(2)}) %collective-permute-start.10) | collective-permute-done | bytes 65568 | tf_op jit(solution)/shard_map/ppermute | solution.py:366
  55.8 3.0 %collective-permute-start.11 = (bf16[128,256]{1,0:T(8,128)(2,1)S(1)}, bf16[128,256]{1,0:T(8,128)(2,1)S(1)}, u32[]{:S(2)}, u32[]{:S(2)}) collective-permute-start(bf16[128,256]{1,0:T(8,128)(2,1)S(1)} %plane_sum.1.refs_0_), channel_id=1, source_target_pairs={{0,8},{4,12},{8,0},{12,4},{1,9},{5,13},{9,1},{13,5},{2,10},{6,14},... | collective-permute-start | bytes 196616 | tf_op jit(solution)/shard_map/ppermute | solution.py:366
  58.9 3.7 %neg_grad.1 = (f32[64,1024]{1,0:T(8,128)S(1)}, bf16[64,1024]{1,0:T(8,128)(2,1)S(1)}, bf16[64,1024]{1,0:T(8,128)(2,1)S(1)}, bf16[64,1024]{1,0:T(8,128)(2,1)S(1)}) custom-call(s32[7]{0:T(128)S(1)} %stack.27.info_ref, bf16[1024,256]{1,0:T(8,128)(2,1)S(1)} %bitcast.20, s32[1,1024]{1,0:T(1,128)S(1)} %copy-done.10, ...), custom_call_target="tpu_custom_call" | custom-call | flops 2127500032 | tf_op jit(solution)/shard_map/neg_grad/pallas_call | solution.py:353
  62.7 1.6 %collective-permute-start.17 = (bf16[144,256]{1,0:T(8,128)(2,1)S(1)}, bf16[144,256]{1,0:T(8,128)(2,1)S(1)}, u32[]{:S(2)}, u32[]{:S(2)}) collective-permute-start(bf16[144,256]{1,0:T(8,128)(2,1)S(1)} %seq_sum_2.1.refs_0_), channel_id=1, source_target_pairs={{0,4},{4,0},{8,12},{12,8},{1,5},{5,1},{9,13},{13,9},{2,6},{6,2},{1... | collective-permute-start | bytes 221192 | tf_op jit(solution)/shard_map/ppermute | solution.py:366
  64.3 2.0 %collective-permute-start.21 = (bf16[64,1024]{1,0:T(8,128)(2,1)S(1)}, bf16[64,1024]{1,0:T(8,128)(2,1)S(1)}, u32[]{:S(2)}, u32[]{:S(2)}) collective-permute-start(bf16[64,1024]{1,0:T(8,128)(2,1)S(1)} %get-tuple-element.110), channel_id=1, source_target_pairs={{0,8},{4,12},{8,0},{12,4},{1,9},{5,13},{9,1},{13,5},{2,10},{6,14},... | collective-permute-start | bytes 393224 | tf_op jit(solution)/shard_map/ppermute | solution.py:366
  66.3 0.9 %collective-permute-start.22 = (bf16[64,1024]{1,0:T(8,128)(2,1)S(1)}, bf16[64,1024]{1,0:T(8,128)(2,1)S(1)}, u32[]{:S(2)}, u32[]{:S(2)}) collective-permute-start(bf16[64,1024]{1,0:T(8,128)(2,1)S(1)} %get-tuple-element.111), channel_id=1, source_target_pairs={{0,12},{4,8},{8,4},{12,0},{1,13},{5,9},{9,5},{13,1},{2,14},{6,10},... | collective-permute-start | bytes 393224 | tf_op jit(solution)/shard_map/ppermute | solution.py:366
  67.2 1.3 %collective-permute-start.18 = (bf16[128,256]{1,0:T(8,128)(2,1)S(1)}, bf16[128,256]{1,0:T(8,128)(2,1)S(1)}, u32[]{:S(2)}, u32[]{:S(2)}) collective-permute-start(bf16[128,256]{1,0:T(8,128)(2,1)S(1)} %seq_sum_1.1.refs_0_), channel_id=1, source_target_pairs={{0,2},{1,3},{2,0},{3,1},{16,18},{17,19},{18,16},{19,17},{4,6},{5,7... | collective-permute-start | bytes 196616 | tf_op jit(solution)/shard_map/ppermute | solution.py:366
  68.4 1.2 %collective-permute-start.19 = (bf16[128,256]{1,0:T(8,128)(2,1)S(1)}, bf16[128,256]{1,0:T(8,128)(2,1)S(1)}, u32[]{:S(2)}, u32[]{:S(2)}) collective-permute-start(bf16[128,256]{1,0:T(8,128)(2,1)S(1)} %seq_sum_1.1.refs_0_), channel_id=1, source_target_pairs={{0,16},{1,17},{2,18},{3,19},{16,0},{17,1},{18,2},{19,3},{4,20},{5,... | collective-permute-start | bytes 196616 | tf_op jit(solution)/shard_map/ppermute | solution.py:366
  69.7 1.1 %collective-permute-start.20 = (bf16[128,256]{1,0:T(8,128)(2,1)S(1)}, bf16[128,256]{1,0:T(8,128)(2,1)S(1)}, u32[]{:S(2)}, u32[]{:S(2)}) collective-permute-start(bf16[128,256]{1,0:T(8,128)(2,1)S(1)} %seq_sum_1.1.refs_0_), channel_id=1, source_target_pairs={{0,18},{1,19},{2,16},{3,17},{16,2},{17,3},{18,0},{19,1},{4,22},{5,... | collective-permute-start | bytes 196616 | tf_op jit(solution)/shard_map/ppermute | solution.py:366
  70.7 0.8 collective-permute-done.18.refs_1_
  71.5 2.6 %collective-permute-start.27 = (bf16[64,1024]{1,0:T(8,128)(2,1)S(1)}, bf16[64,1024]{1,0:T(8,128)(2,1)S(1)}, u32[]{:S(2)}, u32[]{:S(2)}) collective-permute-start(bf16[64,1024]{1,0:T(8,128)(2,1)S(1)} %get-tuple-element.117), channel_id=1, source_target_pairs={{0,4},{4,0},{8,12},{12,8},{1,5},{5,1},{9,13},{13,9},{2,6},{6,2},{1... | collective-permute-start | bytes 393224 | tf_op jit(solution)/shard_map/ppermute | solution.py:366
  74.2 2.1 %collective-permute-done.21.refs_10_ = bf16[64,1024]{1,0:T(8,128)(2,1)S(1)} collective-permute-done((bf16[64,1024]{1,0:T(8,128)(2,1)S(1)}, bf16[64,1024]{1,0:T(8,128)(2,1)S(1)}, u32[]{:S(2)}, u32[]{:S(2)}) %collective-permute-start.21) | collective-permute-done | bytes 131104 | tf_op jit(solution)/shard_map/ppermute | solution.py:366
  78.2 1.7 %final.1 = (f32[1,256]{1,0:T(1,128)}, f32[64,1024]{1,0:T(8,128)}, f32[1024,256]{1,0:T(8,128)}) custom-call(s32[7]{0:T(128)S(1)} %stack.27.info_ref, f32[1,256]{1,0:T(1,128)S(1)} %get-tuple-element.89.loss_ref, bf16[144,256]{1,0:T(8,128)(2,1)S(1)} %collective-permute-done.17.refs_1_.loss_got_ref, bf16[128,256]{1,0:T(8,128)(2,1)S(1)} %seq_sum_1.1.refs_0_, ...), custom_call_target="tpu_custom_call" | custom-call | flops 1150000000 | tf_op jit(solution)/shard_map/final/pallas_call | solution.py:353
  (61 shorter events, 6.8 us)
Async XLA Ops:
  0.6 19.2 %collective-permute-start = (bf16[256,1024]{1,0:T(8,128)(2,1)}, bf16[256,1024]{1,0:T(8,128)(2,1)S(1)}, u32[]{:S(2)}, u32[]{:S(2)}) collective-permute-start(bf16[256,1024]{1,0:T(8,128)(2,1)} %bitcast.15), channel_id=1, source_target_pairs={{0,4},{4,8},{1,5},{5,9},{2,6},{6,10},{3,7},{7,11},{16,20},{20,24},... | collective-permute-start | bytes 1572872 | tf_op jit(solution)/shard_map/ppermute | solution.py:400
  5.6 14.2 %collective-permute-start.1 = (bf16[256,1024]{1,0:T(8,128)(2,1)}, bf16[256,1024]{1,0:T(8,128)(2,1)S(1)}, u32[]{:S(2)}, u32[]{:S(2)}) collective-permute-start(bf16[256,1024]{1,0:T(8,128)(2,1)} %bitcast.16), channel_id=1, source_target_pairs={{12,8},{13,9},{14,10},{15,11},{28,24},{29,25},{30,26},{31,27}} | collective-permute-start | bytes 1572872 | tf_op jit(solution)/shard_map/ppermute | solution.py:401
  12.0 8.5 %copy-start = (bf16[1024,4096]{1,0:T(8,128)(2,1)S(1)}, bf16[1024,4096]{1,0:T(8,128)(2,1)}, u32[]{:S(2)}) copy-start(bf16[1024,4096]{1,0:T(8,128)(2,1)} %w_ref.5) | copy-start | bytes 25165828
  12.0 8.5 %copy-start.3 = (bf16[1,256,1024]{2,1,0:T(8,128)(2,1)S(1)}, bf16[1,256,1024]{2,1,0:T(8,128)(2,1)}, u32[]{:S(2)}) copy-start(bf16[1,256,1024]{2,1,0:T(8,128)(2,1)} %param.9) | copy-start | bytes 1572868
  18.2 13.8 %collective-permute-start.3 = (bf16[1056,256]{1,0:T(8,128)(2,1)S(1)}, bf16[1056,256]{1,0:T(8,128)(2,1)S(1)}, u32[]{:S(2)}, u32[]{:S(2)}) collective-permute-start(bf16[1056,256]{1,0:T(8,128)(2,1)S(1)} %get-tuple-element.87.rest_0_), channel_id=1, source_target_pairs={{0,2},{1,3},{2,0},{3,1},{4,6},{5,7},{6,4},{7,5},{8,10},{9,11},{10,... | collective-permute-start | bytes 1622024 | tf_op jit(solution)/shard_map/ppermute | solution.py:366
  19.8 13.6 %collective-permute-start.2 = (bf16[256,1024]{1,0:T(8,128)(2,1)S(1)}, bf16[256,1024]{1,0:T(8,128)(2,1)S(1)}, u32[]{:S(2)}, u32[]{:S(2)}) collective-permute-start(bf16[256,1024]{1,0:T(8,128)(2,1)S(1)} %collective-permute-done.x_ref), channel_id=1, source_target_pairs={{4,8},{5,9},{6,10},{7,11},{20,24},{21,25},{22,26},{23,27}} | collective-permute-start | bytes 1572872 | tf_op jit(solution)/shard_map/ppermute | solution.py:434
  32.0 9.0 %collective-permute-start.5 = (bf16[1056,256]{1,0:T(8,128)(2,1)S(1)}, bf16[1056,256]{1,0:T(8,128)(2,1)S(1)}, u32[]{:S(2)}, u32[]{:S(2)}) collective-permute-start(bf16[1056,256]{1,0:T(8,128)(2,1)S(1)} %get-tuple-element.87.rest_0_), channel_id=1, source_target_pairs={{0,1},{1,0},{2,3},{3,2},{4,5},{5,4},{6,7},{7,6},{8,9},{9,8},{10,11... | collective-permute-start | bytes 1622024 | tf_op jit(solution)/shard_map/ppermute | solution.py:366
  32.0 9.0 %collective-permute-start.6 = (bf16[1056,256]{1,0:T(8,128)(2,1)S(1)}, bf16[1056,256]{1,0:T(8,128)(2,1)S(1)}, u32[]{:S(2)}, u32[]{:S(2)}) collective-permute-start(bf16[1056,256]{1,0:T(8,128)(2,1)S(1)} %collective-permute-done.3.rest_1_), channel_id=1, source_target_pairs={{0,1},{1,0},{2,3},{3,2},{4,5},{5,4},{6,7},{7,6},{8,9},{9,8},{10,11... | collective-permute-start | bytes 1622024 | tf_op jit(solution)/shard_map/ppermute | solution.py:366
  32.6 8.5 %collective-permute-start.4 = (bf16[272,256]{1,0:T(8,128)(2,1)S(1)}, bf16[272,256]{1,0:T(8,128)(2,1)S(1)}, u32[]{:S(2)}, u32[]{:S(2)}) collective-permute-start(bf16[272,256]{1,0:T(8,128)(2,1)S(1)} %get-tuple-element.86), channel_id=1, source_target_pairs={{12,8},{13,9},{14,10},{15,11},{28,24},{29,25},{30,26},{31,27}} | collective-permute-start | bytes 417800 | tf_op jit(solution)/shard_map/ppermute | solution.py:451
  39.5 8.3 %collective-permute-start.12 = (bf16[512,256]{1,0:T(8,128)(2,1)S(1)}, bf16[512,256]{1,0:T(8,128)(2,1)S(1)}, u32[]{:S(2)}, u32[]{:S(2)}) collective-permute-start(bf16[512,256]{1,0:T(8,128)(2,1)S(1)} %get-tuple-element.98.hat_ref.rest_0_), channel_id=1, source_target_pairs={{0,2},{1,3},{2,0},{3,1},{4,6},{5,7},{6,4},{7,5},{8,10},{9,11},{10,... | collective-permute-start | bytes 786440 | tf_op jit(solution)/shard_map/ppermute | solution.py:366
  46.2 12.7 %copy-start.6 = (bf16[1,1024,256]{2,1,0:T(8,128)(2,1)S(1)}, bf16[1,1024,256]{2,1,0:T(8,128)(2,1)}, u32[]{:S(2)}) copy-start(bf16[1,1024,256]{2,1,0:T(8,128)(2,1)} %param.16) | copy-start | bytes 1572868
  46.2 12.7 %copy-start.10 = (s32[1,1024]{1,0:T(1,128)S(1)}, s32[1,1024]{1,0:T(1,128)}, u32[]{:S(2)}) copy-start(s32[1,1024]{1,0:T(1,128)} %neg_id_ref.1) | copy-start | bytes 12292
  46.3 1.6 %collective-permute-start.7 = (bf16[512,256]{1,0:T(8,128)(2,1)S(1)}, bf16[512,256]{1,0:T(8,128)(2,1)S(1)}, u32[]{:S(2)}, u32[]{:S(2)}) collective-permute-start(bf16[512,256]{1,0:T(8,128)(2,1)S(1)} %get-tuple-element.92), channel_id=1, source_target_pairs={{0,1},{1,0},{2,3},{3,2},{16,17},{17,16},{18,19},{19,18},{4,5},{5,4... | collective-permute-start | bytes 786440 | tf_op jit(solution)/shard_map/ppermute | solution.py:366
  46.3 12.5 %collective-permute-start.13 = (bf16[512,256]{1,0:T(8,128)(2,1)S(1)}, bf16[512,256]{1,0:T(8,128)(2,1)S(1)}, u32[]{:S(2)}, u32[]{:S(2)}) collective-permute-start(bf16[512,256]{1,0:T(8,128)(2,1)S(1)} %get-tuple-element.98.hat_ref.rest_0_), channel_id=1, source_target_pairs={{0,1},{1,0},{2,3},{3,2},{4,5},{5,4},{6,7},{7,6},{8,9},{9,8},{10,11... | collective-permute-start | bytes 786440 | tf_op jit(solution)/shard_map/ppermute | solution.py:366
  47.8 11.1 %collective-permute-start.14 = (bf16[512,256]{1,0:T(8,128)(2,1)S(1)}, bf16[512,256]{1,0:T(8,128)(2,1)S(1)}, u32[]{:S(2)}, u32[]{:S(2)}) collective-permute-start(bf16[512,256]{1,0:T(8,128)(2,1)S(1)} %collective-permute-done.12.rest_1_), channel_id=1, source_target_pairs={{0,1},{1,0},{2,3},{3,2},{4,5},{5,4},{6,7},{7,6},{8,9},{9,8},{10,11... | collective-permute-start | bytes 786440 | tf_op jit(solution)/shard_map/ppermute | solution.py:366
  48.5 4.9 %collective-permute-start.8 = (bf16[144,256]{1,0:T(8,128)(2,1)S(1)}, bf16[144,256]{1,0:T(8,128)(2,1)S(1)}, u32[]{:S(2)}, u32[]{:S(2)}) collective-permute-start(bf16[144,256]{1,0:T(8,128)(2,1)S(1)} %get-tuple-element.95), channel_id=1, source_target_pairs={{0,2},{1,3},{2,0},{3,1},{16,18},{17,19},{18,16},{19,17},{4,6},{5,7... | collective-permute-start | bytes 221192 | tf_op jit(solution)/shard_map/ppermute | solution.py:366
  50.0 5.5 %collective-permute-start.10 = (bf16[128,256]{1,0:T(8,128)(2,1)S(1)}, bf16[128,256]{1,0:T(8,128)(2,1)S(1)}, u32[]{:S(2)}, u32[]{:S(2)}) collective-permute-start(bf16[128,256]{1,0:T(8,128)(2,1)S(1)} %get-tuple-element.97), channel_id=1, source_target_pairs={{0,18},{1,19},{2,16},{3,17},{16,2},{17,3},{18,0},{19,1},{4,22},{5,... | collective-permute-start | bytes 196616 | tf_op jit(solution)/shard_map/ppermute | solution.py:366
  51.5 4.3 %collective-permute-start.9 = (bf16[128,256]{1,0:T(8,128)(2,1)S(1)}, bf16[128,256]{1,0:T(8,128)(2,1)S(1)}, u32[]{:S(2)}, u32[]{:S(2)}) collective-permute-start(bf16[128,256]{1,0:T(8,128)(2,1)S(1)} %get-tuple-element.96), channel_id=1, source_target_pairs={{0,16},{1,17},{2,18},{3,19},{16,0},{17,1},{18,2},{19,3},{4,20},{5,... | collective-permute-start | bytes 196616 | tf_op jit(solution)/shard_map/ppermute | solution.py:366
  53.4 5.5 %collective-permute-start.16 = (bf16[144,256]{1,0:T(8,128)(2,1)S(1)}, bf16[144,256]{1,0:T(8,128)(2,1)S(1)}, u32[]{:S(2)}, u32[]{:S(2)}) collective-permute-start(bf16[144,256]{1,0:T(8,128)(2,1)S(1)} %collective-permute-done.8.refs_1_.rest_5_), channel_id=1, source_target_pairs={{0,1},{1,0},{2,3},{3,2},{4,5},{5,4},{6,7},{7,6},{8,9},{9,8},{10,11... | collective-permute-start | bytes 221192 | tf_op jit(solution)/shard_map/ppermute | solution.py:366
  55.5 3.4 %collective-permute-start.15 = (bf16[16,256]{1,0:T(8,128)(2,1)S(1)}, bf16[16,256]{1,0:T(8,128)(2,1)S(1)}, u32[]{:S(2)}, u32[]{:S(2)}) collective-permute-start(bf16[16,256]{1,0:T(8,128)(2,1)S(1)} %get-tuple-element.102.message_ref.rest_4_), channel_id=1, source_target_pairs={{0,1},{1,0},{2,3},{3,2},{4,5},{5,4},{6,7},{7,6},{8,9},{9,8},{10,11... | collective-permute-start | bytes 24584 | tf_op jit(solution)/shard_map/ppermute | solution.py:366
  55.8 6.8 %collective-permute-start.11 = (bf16[128,256]{1,0:T(8,128)(2,1)S(1)}, bf16[128,256]{1,0:T(8,128)(2,1)S(1)}, u32[]{:S(2)}, u32[]{:S(2)}) collective-permute-start(bf16[128,256]{1,0:T(8,128)(2,1)S(1)} %plane_sum.1.refs_0_), channel_id=1, source_target_pairs={{0,8},{4,12},{8,0},{12,4},{1,9},{5,13},{9,1},{13,5},{2,10},{6,14},... | collective-permute-start | bytes 196616 | tf_op jit(solution)/shard_map/ppermute | solution.py:366
  62.7 4.5 %collective-permute-start.17 = (bf16[144,256]{1,0:T(8,128)(2,1)S(1)}, bf16[144,256]{1,0:T(8,128)(2,1)S(1)}, u32[]{:S(2)}, u32[]{:S(2)}) collective-permute-start(bf16[144,256]{1,0:T(8,128)(2,1)S(1)} %seq_sum_2.1.refs_0_), channel_id=1, source_target_pairs={{0,4},{4,0},{8,12},{12,8},{1,5},{5,1},{9,13},{13,9},{2,6},{6,2},{1... | collective-permute-start | bytes 221192 | tf_op jit(solution)/shard_map/ppermute | solution.py:366
  64.3 11.9 %collective-permute-start.21 = (bf16[64,1024]{1,0:T(8,128)(2,1)S(1)}, bf16[64,1024]{1,0:T(8,128)(2,1)S(1)}, u32[]{:S(2)}, u32[]{:S(2)}) collective-permute-start(bf16[64,1024]{1,0:T(8,128)(2,1)S(1)} %get-tuple-element.110), channel_id=1, source_target_pairs={{0,8},{4,12},{8,0},{12,4},{1,9},{5,13},{9,1},{13,5},{2,10},{6,14},... | collective-permute-start | bytes 393224 | tf_op jit(solution)/shard_map/ppermute | solution.py:366
  66.3 10.0 %collective-permute-start.22 = (bf16[64,1024]{1,0:T(8,128)(2,1)S(1)}, bf16[64,1024]{1,0:T(8,128)(2,1)S(1)}, u32[]{:S(2)}, u32[]{:S(2)}) collective-permute-start(bf16[64,1024]{1,0:T(8,128)(2,1)S(1)} %get-tuple-element.111), channel_id=1, source_target_pairs={{0,12},{4,8},{8,4},{12,0},{1,13},{5,9},{9,5},{13,1},{2,14},{6,10},... | collective-permute-start | bytes 393224 | tf_op jit(solution)/shard_map/ppermute | solution.py:366
  67.2 4.3 %collective-permute-start.18 = (bf16[128,256]{1,0:T(8,128)(2,1)S(1)}, bf16[128,256]{1,0:T(8,128)(2,1)S(1)}, u32[]{:S(2)}, u32[]{:S(2)}) collective-permute-start(bf16[128,256]{1,0:T(8,128)(2,1)S(1)} %seq_sum_1.1.refs_0_), channel_id=1, source_target_pairs={{0,2},{1,3},{2,0},{3,1},{16,18},{17,19},{18,16},{19,17},{4,6},{5,7... | collective-permute-start | bytes 196616 | tf_op jit(solution)/shard_map/ppermute | solution.py:366
  68.4 7.8 %collective-permute-start.19 = (bf16[128,256]{1,0:T(8,128)(2,1)S(1)}, bf16[128,256]{1,0:T(8,128)(2,1)S(1)}, u32[]{:S(2)}, u32[]{:S(2)}) collective-permute-start(bf16[128,256]{1,0:T(8,128)(2,1)S(1)} %seq_sum_1.1.refs_0_), channel_id=1, source_target_pairs={{0,16},{1,17},{2,18},{3,19},{16,0},{17,1},{18,2},{19,3},{4,20},{5,... | collective-permute-start | bytes 196616 | tf_op jit(solution)/shard_map/ppermute | solution.py:366
  69.7 6.6 %collective-permute-start.20 = (bf16[128,256]{1,0:T(8,128)(2,1)S(1)}, bf16[128,256]{1,0:T(8,128)(2,1)S(1)}, u32[]{:S(2)}, u32[]{:S(2)}) collective-permute-start(bf16[128,256]{1,0:T(8,128)(2,1)S(1)} %seq_sum_1.1.refs_0_), channel_id=1, source_target_pairs={{0,18},{1,19},{2,16},{3,17},{16,2},{17,3},{18,0},{19,1},{4,22},{5,... | collective-permute-start | bytes 196616 | tf_op jit(solution)/shard_map/ppermute | solution.py:366
  71.5 6.7 %collective-permute-start.27 = (bf16[64,1024]{1,0:T(8,128)(2,1)S(1)}, bf16[64,1024]{1,0:T(8,128)(2,1)S(1)}, u32[]{:S(2)}, u32[]{:S(2)}) collective-permute-start(bf16[64,1024]{1,0:T(8,128)(2,1)S(1)} %get-tuple-element.117), channel_id=1, source_target_pairs={{0,4},{4,0},{8,12},{12,8},{1,5},{5,1},{9,13},{13,9},{2,6},{6,2},{1... | collective-permute-start | bytes 393224 | tf_op jit(solution)/shard_map/ppermute | solution.py:366
  76.2 1.3 %collective-permute-start.23 = (bf16[128,256]{1,0:T(8,128)(2,1)S(1)}, bf16[128,256]{1,0:T(8,128)(2,1)S(1)}, u32[]{:S(2)}, u32[]{:S(2)}) collective-permute-start(bf16[128,256]{1,0:T(8,128)(2,1)S(1)} %seq_sum_1.1.refs_0_), channel_id=1, source_target_pairs={{0,1},{1,0},{2,3},{3,2},{16,17},{17,16},{18,19},{19,18},{4,5},{5,4... | collective-permute-start | bytes 196616 | tf_op jit(solution)/shard_map/ppermute | solution.py:366
  76.3 1.5 %collective-permute-start.24 = (bf16[128,256]{1,0:T(8,128)(2,1)S(1)}, bf16[128,256]{1,0:T(8,128)(2,1)S(1)}, u32[]{:S(2)}, u32[]{:S(2)}) collective-permute-start(bf16[128,256]{1,0:T(8,128)(2,1)S(1)} %collective-permute-done.18.refs_1_), channel_id=1, source_target_pairs={{0,1},{1,0},{2,3},{3,2},{16,17},{17,16},{18,19},{19,18},{4,5},{5,4... | collective-permute-start | bytes 196616 | tf_op jit(solution)/shard_map/ppermute | solution.py:366
  76.8 1.3 %collective-permute-start.25 = (bf16[128,256]{1,0:T(8,128)(2,1)S(1)}, bf16[128,256]{1,0:T(8,128)(2,1)S(1)}, u32[]{:S(2)}, u32[]{:S(2)}) collective-permute-start(bf16[128,256]{1,0:T(8,128)(2,1)S(1)} %collective-permute-done.19.refs_2_), channel_id=1, source_target_pairs={{0,1},{1,0},{2,3},{3,2},{16,17},{17,16},{18,19},{19,18},{4,5},{5,4... | collective-permute-start | bytes 196616 | tf_op jit(solution)/shard_map/ppermute | solution.py:366
  76.9 1.3 %collective-permute-start.26 = (bf16[128,256]{1,0:T(8,128)(2,1)S(1)}, bf16[128,256]{1,0:T(8,128)(2,1)S(1)}, u32[]{:S(2)}, u32[]{:S(2)}) collective-permute-start(bf16[128,256]{1,0:T(8,128)(2,1)S(1)} %collective-permute-done.20.refs_3_), channel_id=1, source_target_pairs={{0,1},{1,0},{2,3},{3,2},{16,17},{17,16},{18,19},{19,18},{4,5},{5,4... | collective-permute-start | bytes 196616 | tf_op jit(solution)/shard_map/ppermute | solution.py:366
  (8 other events, 27.8 us)

commit v6 on v5

--- a/solution.py
+++ b/solution.py
@@ -427,7 +427,7 @@
     )
     table_part, pos_part, acc = together(table_part, pos_part, acc)
     table = gather_step([table_part], "pool", pool_count)
-    block, guest, acc = together(block, guest, acc)
+    block, acc = together(block, acc)
     tall = struct((2 * rows, width), BF16)
     tall_wide = struct((2 * rows, width), F32)
     for step in range(1, seq_count - 2):

time: 80.5 us -> 80.5 us (level)
  starting transfers between devices: 29.8 us -> 28.8 us
  waiting for transfers between devices: 11.5 us -> 12.4 us
    ppermute x24, waiting for transfers between devices: 11.4 us -> 12.4 us  [swap(): return lax.ppermute(x, axis, [(i, i ^ r) for i in range(count)])]
    ppermute x24, starting transfers between devices: 22.6 us -> 21.7 us  [swap(): return lax.ppermute(x, axis, [(i, i ^ r) for i in range(count)])]
  transfers between devices with their start and end apart: 28 -> 28, of which waited for: 12 -> 13; matrix products, arithmetic and copies ran while one was open for 0% -> 0% of each run, Pallas kernels for 39% -> 39%
where the time goes in v6:
time: 80.5 us; the launch traced here: 80 us
  Pallas kernels  32.7 us (41%)
  starting transfers between devices  28.8 us (36%)
  waiting for transfers between devices  12.4 us (15%)
  local copies, waits for them, and re-layouts  4.47 us (6%)
  between operations  1.58 us (2%)
    pallas_call x12, Pallas kernels, call(): pl.pallas_call(kernel, out_shape=list(outs) if many else outs, in_specs=i...  32.7 us
    ppermute x24, starting transfers between devices, swap(): return lax.ppermute(x, axis, [(i, i ^ r) for i in range(count)])  21.7 us
    ppermute x24, waiting for transfers between devices, swap(): return lax.ppermute(x, axis, [(i, i ^ r) for i in range(count)])  12.4 us
    ppermute x1, starting transfers between devices, body(): block = lax.ppermute(own, 'seq', ups[0])  4.96 us
    unnamed x24, local copies, waits for them, and re-layouts  4.39 us
  transfers between devices with their start and end apart: 28, of which 13 were waited for; matrix products, arithmetic and copies ran while one was open for 0% of the time, Pallas kernels for 39%

profile of v6, /device:TPU:0, one launch (start us, length us, event | category | flops | bytes accessed | tf_op | source)
XLA Modules:
  0.0 80.0 jit_solution(1751113248449047265)
XLA Ops:
  0.6 5.0 %collective-permute-start = (bf16[256,1024]{1,0:T(8,128)(2,1)}, bf16[256,1024]{1,0:T(8,128)(2,1)S(1)}, u32[]{:S(2)}, u32[]{:S(2)}) collective-permute-start(bf16[256,1024]{1,0:T(8,128)(2,1)} %bitcast.15), channel_id=1, source_target_pairs={{0,4},{4,8},{1,5},{5,9},{2,6},{6,10},{3,7},{7,11},{16,20},{20,24},... | collective-permute-start | bytes 1572872 | tf_op jit(solution)/shard_map/ppermute | solution.py:400
  5.6 0.7 collective-permute-start.2
  7.1 1.0 %copy-done.5 = bf16[1,1024,256]{2,1,0:T(8,128)(2,1)S(1)} copy-done((bf16[1,1024,256]{2,1,0:T(8,128)(2,1)S(1)}, bf16[1,1024,256]{2,1,0:T(8,128)(2,1)}, u32[]{:S(2)}) %copy-start.5) | copy-done | bytes 524312
  8.1 0.9 %copy-done.7 = bf16[1,256,256]{2,1,0:T(8,128)(2,1)S(1)} copy-done((bf16[1,256,256]{2,1,0:T(8,128)(2,1)S(1)}, bf16[1,256,256]{2,1,0:T(8,128)(2,1)}, u32[]{:S(2)}) %copy-start.7) | copy-done | bytes 131096
  11.0 1.0 %copy-done.2 = bf16[1,256,1024]{2,1,0:T(8,128)(2,1)S(1)} copy-done((bf16[1,256,1024]{2,1,0:T(8,128)(2,1)S(1)}, bf16[1,256,1024]{2,1,0:T(8,128)(2,1)}, u32[]{:S(2)}) %copy-start.2) | copy-done | bytes 524312
  12.0 6.2 %own_block.1 = (bf16[256,1024]{1,0:T(8,128)(2,1)S(1)}, bf16[256,1024]{1,0:T(8,128)(2,1)S(1)}, bf16[256,1024]{1,0:T(8,128)(2,1)S(1)}, bf16[256,1024]{1,0:T(8,128)(2,1)S(1)}, f32[256,1024]{1,0:T(8,128)S(1)}) custom-call(s32[7]{0:T(128)S(1)} %stack.27.info_ref, bf16[256,1024]{1,0:T(8,128)(2,1)S(1)} %bitcast.17, bf16[1024,4096]{1,0:T(8,128)(2,1)} %w_ref.5), custom_call_target="tpu_custom_call" | custom-call | flops 3449999872 | tf_op jit(solution)/shard_map/own_block/pallas_call | solution.py:353
  18.2 1.6 %collective-permute-start.3 = (bf16[1056,256]{1,0:T(8,128)(2,1)S(1)}, bf16[1056,256]{1,0:T(8,128)(2,1)S(1)}, u32[]{:S(2)}, u32[]{:S(2)}) collective-permute-start(bf16[1056,256]{1,0:T(8,128)(2,1)S(1)} %get-tuple-element.85.rest_0_), channel_id=1, source_target_pairs={{0,2},{1,3},{2,0},{3,1},{4,6},{5,7},{6,4},{7,5},{8,10},{9,11},{10,... | collective-permute-start | bytes 1622024 | tf_op jit(solution)/shard_map/ppermute | solution.py:366
  20.5 5.0 %guest_block.1 = (bf16[512,1024]{1,0:T(8,128)(2,1)S(1)}, bf16[512,1024]{1,0:T(8,128)(2,1)S(1)}, bf16[512,1024]{1,0:T(8,128)(2,1)S(1)}, f32[512,1024]{1,0:T(8,128)S(1)}) custom-call(s32[7]{0:T(128)S(1)} %stack.27.info_ref, bf16[256,1024]{1,0:T(8,128)(2,1)S(1)} %collective-permute-done.2.x_ref, bf16[1024,4096]{1,0:T(8,128)(2,1)S(1)} %copy-done, ...), custom_call_target="tpu_custom_call" | custom-call | flops 2760000000 | tf_op jit(solution)/shard_map/guest_block/pallas_call | solution.py:353
  25.6 3.6 %earlier_block_1.1.before_ref = f32[512,1024]{1,0:T(8,128)S(1)} custom-call(s32[7]{0:T(128)S(1)} %stack.27.info_ref, bf16[256,1024]{1,0:T(8,128)(2,1)S(1)} %collective-permute-done.x_ref, bf16[1024,4096]{1,0:T(8,128)(2,1)S(1)} %copy-done, bf16[512,1024]{1,0:T(8,128)(2,1)S(1)} %get-tuple-element.72.q_ref, f32[512,1024]{1,0:T(8,128)S(1)} %get-tuple-element.73.before_ref), custom_call_target="tpu_custom_call" | custom-call | flops 2070000000 | tf_op jit(solution)/shard_map/earlier_block_1/pallas_call | solution.py:353
  29.1 2.9 %collective-permute-done.3.rest_1_ = bf16[1056,256]{1,0:T(8,128)(2,1)S(1)} collective-permute-done((bf16[1056,256]{1,0:T(8,128)(2,1)S(1)}, bf16[1056,256]{1,0:T(8,128)(2,1)S(1)}, u32[]{:S(2)}, u32[]{:S(2)}) %collective-permute-start.3) | collective-permute-done | bytes 540704 | tf_op jit(solution)/shard_map/ppermute | solution.py:366
  32.6 0.8 %collective-permute-start.4 = (bf16[272,256]{1,0:T(8,128)(2,1)S(1)}, bf16[272,256]{1,0:T(8,128)(2,1)S(1)}, u32[]{:S(2)}, u32[]{:S(2)}) collective-permute-start(bf16[272,256]{1,0:T(8,128)(2,1)S(1)} %get-tuple-element.84), channel_id=1, source_target_pairs={{12,8},{13,9},{14,10},{15,11},{28,24},{29,25},{30,26},{31,27}} | collective-permute-start | bytes 417800 | tf_op jit(solution)/shard_map/ppermute | solution.py:451
  33.4 6.0 %last_block.1 = (bf16[512,1024]{1,0:T(8,128)(2,1)S(1)}, f32[512,256]{1,0:T(8,128)S(1)}, bf16[512,256]{1,0:T(8,128)(2,1)S(1)}) custom-call(s32[7]{0:T(128)S(1)} %stack.27.info_ref, bf16[256,1024]{1,0:T(8,128)(2,1)S(1)} %collective-permute-done.1.x_ref, bf16[1024,4096]{1,0:T(8,128)(2,1)S(1)} %copy-done, bf16[512,1024]{1,0:T(8,128)(2,1)S(1)} %get-tuple-element.72.q_ref, ...), custom_call_target="tpu_custom_call" | custom-call | flops 3449999872 | tf_op jit(solution)/shard_map/last_block/pallas_call | solution.py:353
  39.5 1.6 %collective-permute-start.12 = (bf16[512,256]{1,0:T(8,128)(2,1)S(1)}, bf16[512,256]{1,0:T(8,128)(2,1)S(1)}, u32[]{:S(2)}, u32[]{:S(2)}) collective-permute-start(bf16[512,256]{1,0:T(8,128)(2,1)S(1)} %get-tuple-element.96.hat_ref.rest_0_), channel_id=1, source_target_pairs={{0,2},{1,3},{2,0},{3,1},{4,6},{5,7},{6,4},{7,5},{8,10},{9,11},{10,... | collective-permute-start | bytes 786440 | tf_op jit(solution)/shard_map/ppermute | solution.py:366
  41.1 5.1 %head.1 = (f32[1,256]{1,0:T(1,128)S(1)}, f32[1,256]{1,0:T(1,128)S(1)}, bf16[16,256]{1,0:T(8,128)(2,1)S(1)}, f32[512,256]{1,0:T(8,128)S(1)}, bf16[512,256]{1,0:T(8,128)(2,1)S(1)}) custom-call(s32[7]{0:T(128)S(1)} %stack.27.info_ref, bf16[512,256]{1,0:T(8,128)(2,1)S(1)} %get-tuple-element.96.hat_ref.rest_0_, f32[512,256]{1,0:T(8,128)S(1)} %get-tuple-element.82.out_ref, ...), custom_call_target="tpu_custom_call" | custom-call | flops 2875000064 | tf_op jit(solution)/shard_map/head/pallas_call | solution.py:353
  46.8 0.9 %collective-permute-done.12.rest_1_ = bf16[512,256]{1,0:T(8,128)(2,1)S(1)} collective-permute-done((bf16[512,256]{1,0:T(8,128)(2,1)S(1)}, bf16[512,256]{1,0:T(8,128)(2,1)S(1)}, u32[]{:S(2)}, u32[]{:S(2)}) %collective-permute-start.12) | collective-permute-done | bytes 262176 | tf_op jit(solution)/shard_map/ppermute | solution.py:366
  48.5 1.5 %collective-permute-start.8 = (bf16[144,256]{1,0:T(8,128)(2,1)S(1)}, bf16[144,256]{1,0:T(8,128)(2,1)S(1)}, u32[]{:S(2)}, u32[]{:S(2)}) collective-permute-start(bf16[144,256]{1,0:T(8,128)(2,1)S(1)} %get-tuple-element.93), channel_id=1, source_target_pairs={{0,2},{1,3},{2,0},{3,1},{16,18},{17,19},{18,16},{19,17},{4,6},{5,7... | collective-permute-start | bytes 221192 | tf_op jit(solution)/shard_map/ppermute | solution.py:366
  50.0 1.5 %collective-permute-start.10 = (bf16[128,256]{1,0:T(8,128)(2,1)S(1)}, bf16[128,256]{1,0:T(8,128)(2,1)S(1)}, u32[]{:S(2)}, u32[]{:S(2)}) collective-permute-start(bf16[128,256]{1,0:T(8,128)(2,1)S(1)} %get-tuple-element.95), channel_id=1, source_target_pairs={{0,18},{1,19},{2,16},{3,17},{16,2},{17,3},{18,0},{19,1},{4,22},{5,... | collective-permute-start | bytes 196616 | tf_op jit(solution)/shard_map/ppermute | solution.py:366
  52.0 1.3 %collective-permute-done.8.refs_1_.rest_5_ = bf16[144,256]{1,0:T(8,128)(2,1)S(1)} collective-permute-done((bf16[144,256]{1,0:T(8,128)(2,1)S(1)}, bf16[144,256]{1,0:T(8,128)(2,1)S(1)}, u32[]{:S(2)}, u32[]{:S(2)}) %collective-permute-start.8) | collective-permute-done | bytes 73760 | tf_op jit(solution)/shard_map/ppermute | solution.py:366
  53.4 2.1 %collective-permute-done.10.refs_3_ = bf16[128,256]{1,0:T(8,128)(2,1)S(1)} collective-permute-done((bf16[128,256]{1,0:T(8,128)(2,1)S(1)}, bf16[128,256]{1,0:T(8,128)(2,1)S(1)}, u32[]{:S(2)}, u32[]{:S(2)}) %collective-permute-start.10) | collective-permute-done | bytes 65568 | tf_op jit(solution)/shard_map/ppermute | solution.py:366
  55.8 1.9 %collective-permute-start.11 = (bf16[128,256]{1,0:T(8,128)(2,1)S(1)}, bf16[128,256]{1,0:T(8,128)(2,1)S(1)}, u32[]{:S(2)}, u32[]{:S(2)}) collective-permute-start(bf16[128,256]{1,0:T(8,128)(2,1)S(1)} %plane_sum.1.refs_0_), channel_id=1, source_target_pairs={{0,8},{4,12},{8,0},{12,4},{1,9},{5,13},{9,1},{13,5},{2,10},{6,14},... | collective-permute-start | bytes 196616 | tf_op jit(solution)/shard_map/ppermute | solution.py:366
  57.8 3.7 %neg_grad.1 = (f32[64,1024]{1,0:T(8,128)S(1)}, bf16[64,1024]{1,0:T(8,128)(2,1)S(1)}, bf16[64,1024]{1,0:T(8,128)(2,1)S(1)}, bf16[64,1024]{1,0:T(8,128)(2,1)S(1)}) custom-call(s32[7]{0:T(128)S(1)} %stack.27.info_ref, bf16[1024,256]{1,0:T(8,128)(2,1)S(1)} %bitcast.20, s32[1,1024]{1,0:T(1,128)S(1)} %copy-done.10, ...), custom_call_target="tpu_custom_call" | custom-call | flops 2127500032 | tf_op jit(solution)/shard_map/neg_grad/pallas_call | solution.py:353
  61.5 0.9 %collective-permute-done.11.refs_1_ = bf16[128,256]{1,0:T(8,128)(2,1)S(1)} collective-permute-done((bf16[128,256]{1,0:T(8,128)(2,1)S(1)}, bf16[128,256]{1,0:T(8,128)(2,1)S(1)}, u32[]{:S(2)}, u32[]{:S(2)}) %collective-permute-start.11) | collective-permute-done | bytes 65568 | tf_op jit(solution)/shard_map/ppermute | solution.py:366
  62.5 1.8 %collective-permute-start.17 = (bf16[144,256]{1,0:T(8,128)(2,1)S(1)}, bf16[144,256]{1,0:T(8,128)(2,1)S(1)}, u32[]{:S(2)}, u32[]{:S(2)}) collective-permute-start(bf16[144,256]{1,0:T(8,128)(2,1)S(1)} %seq_sum_2.1.refs_0_), channel_id=1, source_target_pairs={{0,4},{4,0},{8,12},{12,8},{1,5},{5,1},{9,13},{13,9},{2,6},{6,2},{1... | collective-permute-start | bytes 221192 | tf_op jit(solution)/shard_map/ppermute | solution.py:366
  64.3 1.6 %collective-permute-start.21 = (bf16[64,1024]{1,0:T(8,128)(2,1)S(1)}, bf16[64,1024]{1,0:T(8,128)(2,1)S(1)}, u32[]{:S(2)}, u32[]{:S(2)}) collective-permute-start(bf16[64,1024]{1,0:T(8,128)(2,1)S(1)} %get-tuple-element.108), channel_id=1, source_target_pairs={{0,8},{4,12},{8,0},{12,4},{1,9},{5,13},{9,1},{13,5},{2,10},{6,14},... | collective-permute-start | bytes 393224 | tf_op jit(solution)/shard_map/ppermute | solution.py:366
  65.9 1.1 %collective-permute-start.22 = (bf16[64,1024]{1,0:T(8,128)(2,1)S(1)}, bf16[64,1024]{1,0:T(8,128)(2,1)S(1)}, u32[]{:S(2)}, u32[]{:S(2)}) collective-permute-start(bf16[64,1024]{1,0:T(8,128)(2,1)S(1)} %get-tuple-element.109), channel_id=1, source_target_pairs={{0,12},{4,8},{8,4},{12,0},{1,13},{5,9},{9,5},{13,1},{2,14},{6,10},... | collective-permute-start | bytes 393224 | tf_op jit(solution)/shard_map/ppermute | solution.py:366
  67.0 1.5 %collective-permute-start.18 = (bf16[128,256]{1,0:T(8,128)(2,1)S(1)}, bf16[128,256]{1,0:T(8,128)(2,1)S(1)}, u32[]{:S(2)}, u32[]{:S(2)}) collective-permute-start(bf16[128,256]{1,0:T(8,128)(2,1)S(1)} %seq_sum_1.1.refs_0_), channel_id=1, source_target_pairs={{0,2},{1,3},{2,0},{3,1},{16,18},{17,19},{18,16},{19,17},{4,6},{5,7... | collective-permute-start | bytes 196616 | tf_op jit(solution)/shard_map/ppermute | solution.py:366
  68.4 1.2 %collective-permute-start.19 = (bf16[128,256]{1,0:T(8,128)(2,1)S(1)}, bf16[128,256]{1,0:T(8,128)(2,1)S(1)}, u32[]{:S(2)}, u32[]{:S(2)}) collective-permute-start(bf16[128,256]{1,0:T(8,128)(2,1)S(1)} %seq_sum_1.1.refs_0_), channel_id=1, source_target_pairs={{0,16},{1,17},{2,18},{3,19},{16,0},{17,1},{18,2},{19,3},{4,20},{5,... | collective-permute-start | bytes 196616 | tf_op jit(solution)/shard_map/ppermute | solution.py:366
  69.7 0.9 %collective-permute-start.20 = (bf16[128,256]{1,0:T(8,128)(2,1)S(1)}, bf16[128,256]{1,0:T(8,128)(2,1)S(1)}, u32[]{:S(2)}, u32[]{:S(2)}) collective-permute-start(bf16[128,256]{1,0:T(8,128)(2,1)S(1)} %seq_sum_1.1.refs_0_), channel_id=1, source_target_pairs={{0,18},{1,19},{2,16},{3,17},{16,2},{17,3},{18,0},{19,1},{4,22},{5,... | collective-permute-start | bytes 196616 | tf_op jit(solution)/shard_map/ppermute | solution.py:366
  70.5 0.8 collective-permute-done.18.refs_1_
  71.3 2.8 %collective-permute-start.27 = (bf16[64,1024]{1,0:T(8,128)(2,1)S(1)}, bf16[64,1024]{1,0:T(8,128)(2,1)S(1)}, u32[]{:S(2)}, u32[]{:S(2)}) collective-permute-start(bf16[64,1024]{1,0:T(8,128)(2,1)S(1)} %get-tuple-element.115), channel_id=1, source_target_pairs={{0,4},{4,0},{8,12},{12,8},{1,5},{5,1},{9,13},{13,9},{2,6},{6,2},{1... | collective-permute-start | bytes 393224 | tf_op jit(solution)/shard_map/ppermute | solution.py:366
  74.2 2.1 %collective-permute-done.21.refs_10_ = bf16[64,1024]{1,0:T(8,128)(2,1)S(1)} collective-permute-done((bf16[64,1024]{1,0:T(8,128)(2,1)S(1)}, bf16[64,1024]{1,0:T(8,128)(2,1)S(1)}, u32[]{:S(2)}, u32[]{:S(2)}) %collective-permute-start.21) | collective-permute-done | bytes 131104 | tf_op jit(solution)/shard_map/ppermute | solution.py:366
  78.3 1.7 %final.1 = (f32[1,256]{1,0:T(1,128)}, f32[64,1024]{1,0:T(8,128)}, f32[1024,256]{1,0:T(8,128)}) custom-call(s32[7]{0:T(128)S(1)} %stack.27.info_ref, f32[1,256]{1,0:T(1,128)S(1)} %get-tuple-element.87.loss_ref, bf16[144,256]{1,0:T(8,128)(2,1)S(1)} %collective-permute-done.17.refs_1_.loss_got_ref, bf16[128,256]{1,0:T(8,128)(2,1)S(1)} %seq_sum_1.1.refs_0_, ...), custom_call_target="tpu_custom_call" | custom-call | flops 1150000000 | tf_op jit(solution)/shard_map/final/pallas_call | solution.py:353
  (61 shorter events, 7.5 us)
Async XLA Ops:
  0.6 19.2 %collective-permute-start = (bf16[256,1024]{1,0:T(8,128)(2,1)}, bf16[256,1024]{1,0:T(8,128)(2,1)S(1)}, u32[]{:S(2)}, u32[]{:S(2)}) collective-permute-start(bf16[256,1024]{1,0:T(8,128)(2,1)} %bitcast.15), channel_id=1, source_target_pairs={{0,4},{4,8},{1,5},{5,9},{2,6},{6,10},{3,7},{7,11},{16,20},{20,24},... | collective-permute-start | bytes 1572872 | tf_op jit(solution)/shard_map/ppermute | solution.py:400
  5.6 14.9 %collective-permute-start.2 = (bf16[256,1024]{1,0:T(8,128)(2,1)}, bf16[256,1024]{1,0:T(8,128)(2,1)S(1)}, u32[]{:S(2)}, u32[]{:S(2)}) collective-permute-start(bf16[256,1024]{1,0:T(8,128)(2,1)} %bitcast.16), channel_id=1, source_target_pairs={{12,8},{13,9},{14,10},{15,11},{28,24},{29,25},{30,26},{31,27}} | collective-permute-start | bytes 1572872 | tf_op jit(solution)/shard_map/ppermute | solution.py:401
  12.0 8.5 %copy-start = (bf16[1024,4096]{1,0:T(8,128)(2,1)S(1)}, bf16[1024,4096]{1,0:T(8,128)(2,1)}, u32[]{:S(2)}) copy-start(bf16[1024,4096]{1,0:T(8,128)(2,1)} %w_ref.5) | copy-start | bytes 25165828
  12.0 8.5 %copy-start.3 = (bf16[1,256,1024]{2,1,0:T(8,128)(2,1)S(1)}, bf16[1,256,1024]{2,1,0:T(8,128)(2,1)}, u32[]{:S(2)}) copy-start(bf16[1,256,1024]{2,1,0:T(8,128)(2,1)} %param.9) | copy-start | bytes 1572868
  18.2 13.8 %collective-permute-start.3 = (bf16[1056,256]{1,0:T(8,128)(2,1)S(1)}, bf16[1056,256]{1,0:T(8,128)(2,1)S(1)}, u32[]{:S(2)}, u32[]{:S(2)}) collective-permute-start(bf16[1056,256]{1,0:T(8,128)(2,1)S(1)} %get-tuple-element.85.rest_0_), channel_id=1, source_target_pairs={{0,2},{1,3},{2,0},{3,1},{4,6},{5,7},{6,4},{7,5},{8,10},{9,11},{10,... | collective-permute-start | bytes 1622024 | tf_op jit(solution)/shard_map/ppermute | solution.py:366
  19.8 13.6 %collective-permute-start.1 = (bf16[256,1024]{1,0:T(8,128)(2,1)S(1)}, bf16[256,1024]{1,0:T(8,128)(2,1)S(1)}, u32[]{:S(2)}, u32[]{:S(2)}) collective-permute-start(bf16[256,1024]{1,0:T(8,128)(2,1)S(1)} %collective-permute-done.x_ref), channel_id=1, source_target_pairs={{4,8},{5,9},{6,10},{7,11},{20,24},{21,25},{22,26},{23,27}} | collective-permute-start | bytes 1572872 | tf_op jit(solution)/shard_map/ppermute | solution.py:434
  32.0 9.0 %collective-permute-start.5 = (bf16[1056,256]{1,0:T(8,128)(2,1)S(1)}, bf16[1056,256]{1,0:T(8,128)(2,1)S(1)}, u32[]{:S(2)}, u32[]{:S(2)}) collective-permute-start(bf16[1056,256]{1,0:T(8,128)(2,1)S(1)} %get-tuple-element.85.rest_0_), channel_id=1, source_target_pairs={{0,1},{1,0},{2,3},{3,2},{4,5},{5,4},{6,7},{7,6},{8,9},{9,8},{10,11... | collective-permute-start | bytes 1622024 | tf_op jit(solution)/shard_map/ppermute | solution.py:366
  32.0 9.0 %collective-permute-start.6 = (bf16[1056,256]{1,0:T(8,128)(2,1)S(1)}, bf16[1056,256]{1,0:T(8,128)(2,1)S(1)}, u32[]{:S(2)}, u32[]{:S(2)}) collective-permute-start(bf16[1056,256]{1,0:T(8,128)(2,1)S(1)} %collective-permute-done.3.rest_1_), channel_id=1, source_target_pairs={{0,1},{1,0},{2,3},{3,2},{4,5},{5,4},{6,7},{7,6},{8,9},{9,8},{10,11... | collective-permute-start | bytes 1622024 | tf_op jit(solution)/shard_map/ppermute | solution.py:366
  32.6 8.5 %collective-permute-start.4 = (bf16[272,256]{1,0:T(8,128)(2,1)S(1)}, bf16[272,256]{1,0:T(8,128)(2,1)S(1)}, u32[]{:S(2)}, u32[]{:S(2)}) collective-permute-start(bf16[272,256]{1,0:T(8,128)(2,1)S(1)} %get-tuple-element.84), channel_id=1, source_target_pairs={{12,8},{13,9},{14,10},{15,11},{28,24},{29,25},{30,26},{31,27}} | collective-permute-start | bytes 417800 | tf_op jit(solution)/shard_map/ppermute | solution.py:451
  39.5 8.3 %collective-permute-start.12 = (bf16[512,256]{1,0:T(8,128)(2,1)S(1)}, bf16[512,256]{1,0:T(8,128)(2,1)S(1)}, u32[]{:S(2)}, u32[]{:S(2)}) collective-permute-start(bf16[512,256]{1,0:T(8,128)(2,1)S(1)} %get-tuple-element.96.hat_ref.rest_0_), channel_id=1, source_target_pairs={{0,2},{1,3},{2,0},{3,1},{4,6},{5,7},{6,4},{7,5},{8,10},{9,11},{10,... | collective-permute-start | bytes 786440 | tf_op jit(solution)/shard_map/ppermute | solution.py:366
  46.2 11.5 %copy-start.6 = (bf16[1,1024,256]{2,1,0:T(8,128)(2,1)S(1)}, bf16[1,1024,256]{2,1,0:T(8,128)(2,1)}, u32[]{:S(2)}) copy-start(bf16[1,1024,256]{2,1,0:T(8,128)(2,1)} %param.16) | copy-start | bytes 1572868
  46.2 11.5 %copy-start.10 = (s32[1,1024]{1,0:T(1,128)S(1)}, s32[1,1024]{1,0:T(1,128)}, u32[]{:S(2)}) copy-start(s32[1,1024]{1,0:T(1,128)} %neg_id_ref.1) | copy-start | bytes 12292
  46.3 1.6 %collective-permute-start.7 = (bf16[512,256]{1,0:T(8,128)(2,1)S(1)}, bf16[512,256]{1,0:T(8,128)(2,1)S(1)}, u32[]{:S(2)}, u32[]{:S(2)}) collective-permute-start(bf16[512,256]{1,0:T(8,128)(2,1)S(1)} %get-tuple-element.90), channel_id=1, source_target_pairs={{0,1},{1,0},{2,3},{3,2},{16,17},{17,16},{18,19},{19,18},{4,5},{5,4... | collective-permute-start | bytes 786440 | tf_op jit(solution)/shard_map/ppermute | solution.py:366
  46.3 11.4 %collective-permute-start.13 = (bf16[512,256]{1,0:T(8,128)(2,1)S(1)}, bf16[512,256]{1,0:T(8,128)(2,1)S(1)}, u32[]{:S(2)}, u32[]{:S(2)}) collective-permute-start(bf16[512,256]{1,0:T(8,128)(2,1)S(1)} %get-tuple-element.96.hat_ref.rest_0_), channel_id=1, source_target_pairs={{0,1},{1,0},{2,3},{3,2},{4,5},{5,4},{6,7},{7,6},{8,9},{9,8},{10,11... | collective-permute-start | bytes 786440 | tf_op jit(solution)/shard_map/ppermute | solution.py:366
  47.8 10.0 %collective-permute-start.14 = (bf16[512,256]{1,0:T(8,128)(2,1)S(1)}, bf16[512,256]{1,0:T(8,128)(2,1)S(1)}, u32[]{:S(2)}, u32[]{:S(2)}) collective-permute-start(bf16[512,256]{1,0:T(8,128)(2,1)S(1)} %collective-permute-done.12.rest_1_), channel_id=1, source_target_pairs={{0,1},{1,0},{2,3},{3,2},{4,5},{5,4},{6,7},{7,6},{8,9},{9,8},{10,11... | collective-permute-start | bytes 786440 | tf_op jit(solution)/shard_map/ppermute | solution.py:366
  48.5 4.9 %collective-permute-start.8 = (bf16[144,256]{1,0:T(8,128)(2,1)S(1)}, bf16[144,256]{1,0:T(8,128)(2,1)S(1)}, u32[]{:S(2)}, u32[]{:S(2)}) collective-permute-start(bf16[144,256]{1,0:T(8,128)(2,1)S(1)} %get-tuple-element.93), channel_id=1, source_target_pairs={{0,2},{1,3},{2,0},{3,1},{16,18},{17,19},{18,16},{19,17},{4,6},{5,7... | collective-permute-start | bytes 221192 | tf_op jit(solution)/shard_map/ppermute | solution.py:366
  50.0 5.5 %collective-permute-start.10 = (bf16[128,256]{1,0:T(8,128)(2,1)S(1)}, bf16[128,256]{1,0:T(8,128)(2,1)S(1)}, u32[]{:S(2)}, u32[]{:S(2)}) collective-permute-start(bf16[128,256]{1,0:T(8,128)(2,1)S(1)} %get-tuple-element.95), channel_id=1, source_target_pairs={{0,18},{1,19},{2,16},{3,17},{16,2},{17,3},{18,0},{19,1},{4,22},{5,... | collective-permute-start | bytes 196616 | tf_op jit(solution)/shard_map/ppermute | solution.py:366
  51.5 4.3 %collective-permute-start.9 = (bf16[128,256]{1,0:T(8,128)(2,1)S(1)}, bf16[128,256]{1,0:T(8,128)(2,1)S(1)}, u32[]{:S(2)}, u32[]{:S(2)}) collective-permute-start(bf16[128,256]{1,0:T(8,128)(2,1)S(1)} %get-tuple-element.94), channel_id=1, source_target_pairs={{0,16},{1,17},{2,18},{3,19},{16,0},{17,1},{18,2},{19,3},{4,20},{5,... | collective-permute-start | bytes 196616 | tf_op jit(solution)/shard_map/ppermute | solution.py:366
  53.4 4.4 %collective-permute-start.16 = (bf16[144,256]{1,0:T(8,128)(2,1)S(1)}, bf16[144,256]{1,0:T(8,128)(2,1)S(1)}, u32[]{:S(2)}, u32[]{:S(2)}) collective-permute-start(bf16[144,256]{1,0:T(8,128)(2,1)S(1)} %collective-permute-done.8.refs_1_.rest_5_), channel_id=1, source_target_pairs={{0,1},{1,0},{2,3},{3,2},{4,5},{5,4},{6,7},{7,6},{8,9},{9,8},{10,11... | collective-permute-start | bytes 221192 | tf_op jit(solution)/shard_map/ppermute | solution.py:366
  55.5 2.3 %collective-permute-start.15 = (bf16[16,256]{1,0:T(8,128)(2,1)S(1)}, bf16[16,256]{1,0:T(8,128)(2,1)S(1)}, u32[]{:S(2)}, u32[]{:S(2)}) collective-permute-start(bf16[16,256]{1,0:T(8,128)(2,1)S(1)} %get-tuple-element.100.message_ref.rest_4_), channel_id=1, source_target_pairs={{0,1},{1,0},{2,3},{3,2},{4,5},{5,4},{6,7},{7,6},{8,9},{9,8},{10,11... | collective-permute-start | bytes 24584 | tf_op jit(solution)/shard_map/ppermute | solution.py:366
  55.8 6.6 %collective-permute-start.11 = (bf16[128,256]{1,0:T(8,128)(2,1)S(1)}, bf16[128,256]{1,0:T(8,128)(2,1)S(1)}, u32[]{:S(2)}, u32[]{:S(2)}) collective-permute-start(bf16[128,256]{1,0:T(8,128)(2,1)S(1)} %plane_sum.1.refs_0_), channel_id=1, source_target_pairs={{0,8},{4,12},{8,0},{12,4},{1,9},{5,13},{9,1},{13,5},{2,10},{6,14},... | collective-permute-start | bytes 196616 | tf_op jit(solution)/shard_map/ppermute | solution.py:366
  62.5 4.5 %collective-permute-start.17 = (bf16[144,256]{1,0:T(8,128)(2,1)S(1)}, bf16[144,256]{1,0:T(8,128)(2,1)S(1)}, u32[]{:S(2)}, u32[]{:S(2)}) collective-permute-start(bf16[144,256]{1,0:T(8,128)(2,1)S(1)} %seq_sum_2.1.refs_0_), channel_id=1, source_target_pairs={{0,4},{4,0},{8,12},{12,8},{1,5},{5,1},{9,13},{13,9},{2,6},{6,2},{1... | collective-permute-start | bytes 221192 | tf_op jit(solution)/shard_map/ppermute | solution.py:366
  64.3 12.0 %collective-permute-start.21 = (bf16[64,1024]{1,0:T(8,128)(2,1)S(1)}, bf16[64,1024]{1,0:T(8,128)(2,1)S(1)}, u32[]{:S(2)}, u32[]{:S(2)}) collective-permute-start(bf16[64,1024]{1,0:T(8,128)(2,1)S(1)} %get-tuple-element.108), channel_id=1, source_target_pairs={{0,8},{4,12},{8,0},{12,4},{1,9},{5,13},{9,1},{13,5},{2,10},{6,14},... | collective-permute-start | bytes 393224 | tf_op jit(solution)/shard_map/ppermute | solution.py:366
  65.9 10.4 %collective-permute-start.22 = (bf16[64,1024]{1,0:T(8,128)(2,1)S(1)}, bf16[64,1024]{1,0:T(8,128)(2,1)S(1)}, u32[]{:S(2)}, u32[]{:S(2)}) collective-permute-start(bf16[64,1024]{1,0:T(8,128)(2,1)S(1)} %get-tuple-element.109), channel_id=1, source_target_pairs={{0,12},{4,8},{8,4},{12,0},{1,13},{5,9},{9,5},{13,1},{2,14},{6,10},... | collective-permute-start | bytes 393224 | tf_op jit(solution)/shard_map/ppermute | solution.py:366
  67.0 4.3 %collective-permute-start.18 = (bf16[128,256]{1,0:T(8,128)(2,1)S(1)}, bf16[128,256]{1,0:T(8,128)(2,1)S(1)}, u32[]{:S(2)}, u32[]{:S(2)}) collective-permute-start(bf16[128,256]{1,0:T(8,128)(2,1)S(1)} %seq_sum_1.1.refs_0_), channel_id=1, source_target_pairs={{0,2},{1,3},{2,0},{3,1},{16,18},{17,19},{18,16},{19,17},{4,6},{5,7... | collective-permute-start | bytes 196616 | tf_op jit(solution)/shard_map/ppermute | solution.py:366
  68.4 7.9 %collective-permute-start.19 = (bf16[128,256]{1,0:T(8,128)(2,1)S(1)}, bf16[128,256]{1,0:T(8,128)(2,1)S(1)}, u32[]{:S(2)}, u32[]{:S(2)}) collective-permute-start(bf16[128,256]{1,0:T(8,128)(2,1)S(1)} %seq_sum_1.1.refs_0_), channel_id=1, source_target_pairs={{0,16},{1,17},{2,18},{3,19},{16,0},{17,1},{18,2},{19,3},{4,20},{5,... | collective-permute-start | bytes 196616 | tf_op jit(solution)/shard_map/ppermute | solution.py:366
  69.7 6.6 %collective-permute-start.20 = (bf16[128,256]{1,0:T(8,128)(2,1)S(1)}, bf16[128,256]{1,0:T(8,128)(2,1)S(1)}, u32[]{:S(2)}, u32[]{:S(2)}) collective-permute-start(bf16[128,256]{1,0:T(8,128)(2,1)S(1)} %seq_sum_1.1.refs_0_), channel_id=1, source_target_pairs={{0,18},{1,19},{2,16},{3,17},{16,2},{17,3},{18,0},{19,1},{4,22},{5,... | collective-permute-start | bytes 196616 | tf_op jit(solution)/shard_map/ppermute | solution.py:366
  71.3 7.0 %collective-permute-start.27 = (bf16[64,1024]{1,0:T(8,128)(2,1)S(1)}, bf16[64,1024]{1,0:T(8,128)(2,1)S(1)}, u32[]{:S(2)}, u32[]{:S(2)}) collective-permute-start(bf16[64,1024]{1,0:T(8,128)(2,1)S(1)} %get-tuple-element.115), channel_id=1, source_target_pairs={{0,4},{4,0},{8,12},{12,8},{1,5},{5,1},{9,13},{13,9},{2,6},{6,2},{1... | collective-permute-start | bytes 393224 | tf_op jit(solution)/shard_map/ppermute | solution.py:366
  76.3 1.3 %collective-permute-start.23 = (bf16[128,256]{1,0:T(8,128)(2,1)S(1)}, bf16[128,256]{1,0:T(8,128)(2,1)S(1)}, u32[]{:S(2)}, u32[]{:S(2)}) collective-permute-start(bf16[128,256]{1,0:T(8,128)(2,1)S(1)} %seq_sum_1.1.refs_0_), channel_id=1, source_target_pairs={{0,1},{1,0},{2,3},{3,2},{16,17},{17,16},{18,19},{19,18},{4,5},{5,4... | collective-permute-start | bytes 196616 | tf_op jit(solution)/shard_map/ppermute | solution.py:366
  76.3 1.5 %collective-permute-start.24 = (bf16[128,256]{1,0:T(8,128)(2,1)S(1)}, bf16[128,256]{1,0:T(8,128)(2,1)S(1)}, u32[]{:S(2)}, u32[]{:S(2)}) collective-permute-start(bf16[128,256]{1,0:T(8,128)(2,1)S(1)} %collective-permute-done.18.refs_1_), channel_id=1, source_target_pairs={{0,1},{1,0},{2,3},{3,2},{16,17},{17,16},{18,19},{19,18},{4,5},{5,4... | collective-permute-start | bytes 196616 | tf_op jit(solution)/shard_map/ppermute | solution.py:366
  76.9 1.3 %collective-permute-start.25 = (bf16[128,256]{1,0:T(8,128)(2,1)S(1)}, bf16[128,256]{1,0:T(8,128)(2,1)S(1)}, u32[]{:S(2)}, u32[]{:S(2)}) collective-permute-start(bf16[128,256]{1,0:T(8,128)(2,1)S(1)} %collective-permute-done.19.refs_2_), channel_id=1, source_target_pairs={{0,1},{1,0},{2,3},{3,2},{16,17},{17,16},{18,19},{19,18},{4,5},{5,4... | collective-permute-start | bytes 196616 | tf_op jit(solution)/shard_map/ppermute | solution.py:366
  76.9 1.3 %collective-permute-start.26 = (bf16[128,256]{1,0:T(8,128)(2,1)S(1)}, bf16[128,256]{1,0:T(8,128)(2,1)S(1)}, u32[]{:S(2)}, u32[]{:S(2)}) collective-permute-start(bf16[128,256]{1,0:T(8,128)(2,1)S(1)} %collective-permute-done.20.refs_3_), channel_id=1, source_target_pairs={{0,1},{1,0},{2,3},{3,2},{16,17},{17,16},{18,19},{19,18},{4,5},{5,4... | collective-permute-start | bytes 196616 | tf_op jit(solution)/shard_map/ppermute | solution.py:366
  (8 other events, 27.7 us)

commit v7 on v6

--- a/solution.py
+++ b/solution.py
@@ -425,7 +425,6 @@
         limit=24,
         micros=0.6, name="table_part",
     )
-    table_part, pos_part, acc = together(table_part, pos_part, acc)
     table = gather_step([table_part], "pool", pool_count)
     block, acc = together(block, acc)
     tall = struct((2 * rows, width), BF16)

time: 80.5 us -> 78.9 us (0.980)
  waiting for transfers between devices: 12.4 us -> 11.5 us
    ppermute x24, waiting for transfers between devices: 12.4 us -> 11.5 us  [swap(): return lax.ppermute(x, axis, [(i, i ^ r) for i in range(count)])]
    unnamed x24 -> x26, local copies, waits for them, and re-layouts: 4.39 us -> 4.39 us
  transfers between devices with their start and end apart: 28 -> 28, of which waited for: 13 -> 12; matrix products, arithmetic and copies ran while one was open for 0% -> 0% of each run, Pallas kernels for 39% -> 39%
where the time goes in v7:
time: 78.9 us; the launch traced here: 78.6 us
  Pallas kernels  32.7 us (41%)
  starting transfers between devices  28.2 us (36%)
  waiting for transfers between devices  11.5 us (15%)
  local copies, waits for them, and re-layouts  4.48 us (6%)
  between operations  1.61 us (2%)
    pallas_call x12, Pallas kernels, call(): pl.pallas_call(kernel, out_shape=list(outs) if many else outs, in_specs=i...  32.7 us
    ppermute x24, starting transfers between devices, swap(): return lax.ppermute(x, axis, [(i, i ^ r) for i in range(count)])  21.1 us
    ppermute x24, waiting for transfers between devices, swap(): return lax.ppermute(x, axis, [(i, i ^ r) for i in range(count)])  11.5 us
    ppermute x1, starting transfers between devices, body(): block = lax.ppermute(own, 'seq', ups[0])  4.96 us
    unnamed x26, local copies, waits for them, and re-layouts  4.39 us
  transfers between devices with their start and end apart: 28, of which 12 were waited for; matrix products, arithmetic and copies ran while one was open for 0% of the time, Pallas kernels for 39%

profile of v7, /device:TPU:0, one launch (start us, length us, event | category | flops | bytes accessed | tf_op | source)
XLA Modules:
  0.0 78.6 jit_solution(17338508022607607186)
XLA Ops:
  0.6 5.0 %collective-permute-start = (bf16[256,1024]{1,0:T(8,128)(2,1)}, bf16[256,1024]{1,0:T(8,128)(2,1)S(1)}, u32[]{:S(2)}, u32[]{:S(2)}) collective-permute-start(bf16[256,1024]{1,0:T(8,128)(2,1)} %bitcast.15), channel_id=1, source_target_pairs={{0,4},{4,8},{1,5},{5,9},{2,6},{6,10},{3,7},{7,11},{16,20},{20,24},... | collective-permute-start | bytes 1572872 | tf_op jit(solution)/shard_map/ppermute | solution.py:400
  5.6 0.7 collective-permute-start.2
  6.3 1.0 %copy-done.5 = bf16[1,1024,256]{2,1,0:T(8,128)(2,1)S(1)} copy-done((bf16[1,1024,256]{2,1,0:T(8,128)(2,1)S(1)}, bf16[1,1024,256]{2,1,0:T(8,128)(2,1)}, u32[]{:S(2)}) %copy-start.5) | copy-done | bytes 524312
  7.3 0.9 %copy-done.7 = bf16[1,256,256]{2,1,0:T(8,128)(2,1)S(1)} copy-done((bf16[1,256,256]{2,1,0:T(8,128)(2,1)S(1)}, bf16[1,256,256]{2,1,0:T(8,128)(2,1)}, u32[]{:S(2)}) %copy-start.7) | copy-done | bytes 131096
  8.3 0.7 copy-done.9
  8.9 0.7 copy-done.11
  10.2 1.6 %collective-permute-start.3 = (bf16[1056,256]{1,0:T(8,128)(2,1)S(1)}, bf16[1056,256]{1,0:T(8,128)(2,1)S(1)}, u32[]{:S(2)}, u32[]{:S(2)}) collective-permute-start(bf16[1056,256]{1,0:T(8,128)(2,1)S(1)} %get-tuple-element.79.rest_0_), channel_id=1, source_target_pairs={{0,2},{1,3},{2,0},{3,1},{4,6},{5,7},{6,4},{7,5},{8,10},{9,11},{10,... | collective-permute-start | bytes 1622024 | tf_op jit(solution)/shard_map/ppermute | solution.py:366
  12.5 1.0 %copy-done.2 = bf16[1,256,1024]{2,1,0:T(8,128)(2,1)S(1)} copy-done((bf16[1,256,1024]{2,1,0:T(8,128)(2,1)S(1)}, bf16[1,256,1024]{2,1,0:T(8,128)(2,1)}, u32[]{:S(2)}) %copy-start.2) | copy-done | bytes 524312
  13.6 6.2 %own_block.1 = (bf16[256,1024]{1,0:T(8,128)(2,1)S(1)}, bf16[256,1024]{1,0:T(8,128)(2,1)S(1)}, bf16[256,1024]{1,0:T(8,128)(2,1)S(1)}, bf16[256,1024]{1,0:T(8,128)(2,1)S(1)}, f32[256,1024]{1,0:T(8,128)S(1)}) custom-call(s32[7]{0:T(128)S(1)} %stack.27.info_ref, bf16[256,1024]{1,0:T(8,128)(2,1)S(1)} %bitcast.17, bf16[1024,4096]{1,0:T(8,128)(2,1)} %w_ref.5), custom_call_target="tpu_custom_call" | custom-call | flops 3449999872 | tf_op jit(solution)/shard_map/own_block/pallas_call | solution.py:353
  19.8 0.7 collective-permute-start.1
  20.6 5.0 %guest_block.1 = (bf16[512,1024]{1,0:T(8,128)(2,1)S(1)}, bf16[512,1024]{1,0:T(8,128)(2,1)S(1)}, bf16[512,1024]{1,0:T(8,128)(2,1)S(1)}, f32[512,1024]{1,0:T(8,128)S(1)}) custom-call(s32[7]{0:T(128)S(1)} %stack.27.info_ref, bf16[256,1024]{1,0:T(8,128)(2,1)S(1)} %collective-permute-done.2.x_ref, bf16[1024,4096]{1,0:T(8,128)(2,1)S(1)} %copy-done, ...), custom_call_target="tpu_custom_call" | custom-call | flops 2760000000 | tf_op jit(solution)/shard_map/guest_block/pallas_call | solution.py:353
  25.6 3.6 %earlier_block_1.1.before_ref = f32[512,1024]{1,0:T(8,128)S(1)} custom-call(s32[7]{0:T(128)S(1)} %stack.27.info_ref, bf16[256,1024]{1,0:T(8,128)(2,1)S(1)} %collective-permute-done.x_ref, bf16[1024,4096]{1,0:T(8,128)(2,1)S(1)} %copy-done, bf16[512,1024]{1,0:T(8,128)(2,1)S(1)} %get-tuple-element.66.q_ref, f32[512,1024]{1,0:T(8,128)S(1)} %get-tuple-element.67.before_ref), custom_call_target="tpu_custom_call" | custom-call | flops 2070000000 | tf_op jit(solution)/shard_map/earlier_block_1/pallas_call | solution.py:353
  29.7 0.8 %collective-permute-start.4 = (bf16[272,256]{1,0:T(8,128)(2,1)S(1)}, bf16[272,256]{1,0:T(8,128)(2,1)S(1)}, u32[]{:S(2)}, u32[]{:S(2)}) collective-permute-start(bf16[272,256]{1,0:T(8,128)(2,1)S(1)} %get-tuple-element.78), channel_id=1, source_target_pairs={{12,8},{13,9},{14,10},{15,11},{28,24},{29,25},{30,26},{31,27}} | collective-permute-start | bytes 417800 | tf_op jit(solution)/shard_map/ppermute | solution.py:450
  30.6 6.0 %last_block.1 = (bf16[512,1024]{1,0:T(8,128)(2,1)S(1)}, f32[512,256]{1,0:T(8,128)S(1)}, bf16[512,256]{1,0:T(8,128)(2,1)S(1)}) custom-call(s32[7]{0:T(128)S(1)} %stack.27.info_ref, bf16[256,1024]{1,0:T(8,128)(2,1)S(1)} %collective-permute-done.1.x_ref, bf16[1024,4096]{1,0:T(8,128)(2,1)S(1)} %copy-done, bf16[512,1024]{1,0:T(8,128)(2,1)S(1)} %get-tuple-element.66.q_ref, ...), custom_call_target="tpu_custom_call" | custom-call | flops 3449999872 | tf_op jit(solution)/shard_map/last_block/pallas_call | solution.py:353
  37.3 5.2 %head.1 = (f32[1,256]{1,0:T(1,128)S(1)}, f32[1,256]{1,0:T(1,128)S(1)}, bf16[16,256]{1,0:T(8,128)(2,1)S(1)}, f32[512,256]{1,0:T(8,128)S(1)}, bf16[512,256]{1,0:T(8,128)(2,1)S(1)}) custom-call(s32[7]{0:T(128)S(1)} %stack.27.info_ref, bf16[512,256]{1,0:T(8,128)(2,1)S(1)} %get-tuple-element.90.hat_ref.rest_0_, f32[512,256]{1,0:T(8,128)S(1)} %get-tuple-element.76.out_ref, ...), custom_call_target="tpu_custom_call" | custom-call | flops 2875000064 | tf_op jit(solution)/shard_map/head/pallas_call | solution.py:353
  43.1 2.0 %collective-permute-done.12.rest_1_ = bf16[512,256]{1,0:T(8,128)(2,1)S(1)} collective-permute-done((bf16[512,256]{1,0:T(8,128)(2,1)S(1)}, bf16[512,256]{1,0:T(8,128)(2,1)S(1)}, u32[]{:S(2)}, u32[]{:S(2)}) %collective-permute-start.12) | collective-permute-done | bytes 262176 | tf_op jit(solution)/shard_map/ppermute | solution.py:366
  45.0 0.6 halved.1
  45.7 0.6 collective-permute-start.8
  46.3 2.4 %collective-permute-start.10 = (bf16[128,256]{1,0:T(8,128)(2,1)S(1)}, bf16[128,256]{1,0:T(8,128)(2,1)S(1)}, u32[]{:S(2)}, u32[]{:S(2)}) collective-permute-start(bf16[128,256]{1,0:T(8,128)(2,1)S(1)} %get-tuple-element.89), channel_id=1, source_target_pairs={{0,18},{1,19},{2,16},{3,17},{16,2},{17,3},{18,0},{19,1},{4,22},{5,... | collective-permute-start | bytes 196616 | tf_op jit(solution)/shard_map/ppermute | solution.py:366
  49.2 2.5 %collective-permute-done.8.refs_1_.rest_5_ = bf16[144,256]{1,0:T(8,128)(2,1)S(1)} collective-permute-done((bf16[144,256]{1,0:T(8,128)(2,1)S(1)}, bf16[144,256]{1,0:T(8,128)(2,1)S(1)}, u32[]{:S(2)}, u32[]{:S(2)}) %collective-permute-start.8) | collective-permute-done | bytes 73760 | tf_op jit(solution)/shard_map/ppermute | solution.py:366
  52.3 0.7 collective-permute-done.9.refs_2_
  53.0 4.6 %collective-permute-start.11 = (bf16[128,256]{1,0:T(8,128)(2,1)S(1)}, bf16[128,256]{1,0:T(8,128)(2,1)S(1)}, u32[]{:S(2)}, u32[]{:S(2)}) collective-permute-start(bf16[128,256]{1,0:T(8,128)(2,1)S(1)} %plane_sum.1.refs_0_), channel_id=1, source_target_pairs={{0,8},{4,12},{8,0},{12,4},{1,9},{5,13},{9,1},{13,5},{2,10},{6,14},... | collective-permute-start | bytes 196616 | tf_op jit(solution)/shard_map/ppermute | solution.py:366
  57.7 3.7 %neg_grad.1 = (f32[64,1024]{1,0:T(8,128)S(1)}, bf16[64,1024]{1,0:T(8,128)(2,1)S(1)}, bf16[64,1024]{1,0:T(8,128)(2,1)S(1)}, bf16[64,1024]{1,0:T(8,128)(2,1)S(1)}) custom-call(s32[7]{0:T(128)S(1)} %stack.27.info_ref, bf16[1024,256]{1,0:T(8,128)(2,1)S(1)} %bitcast.20, s32[1,1024]{1,0:T(1,128)S(1)} %copy-done.10, ...), custom_call_target="tpu_custom_call" | custom-call | flops 2127500032 | tf_op jit(solution)/shard_map/neg_grad/pallas_call | solution.py:353
  61.9 1.3 %collective-permute-start.21 = (bf16[64,1024]{1,0:T(8,128)(2,1)S(1)}, bf16[64,1024]{1,0:T(8,128)(2,1)S(1)}, u32[]{:S(2)}, u32[]{:S(2)}) collective-permute-start(bf16[64,1024]{1,0:T(8,128)(2,1)S(1)} %get-tuple-element.102), channel_id=1, source_target_pairs={{0,8},{4,12},{8,0},{12,4},{1,9},{5,13},{9,1},{13,5},{2,10},{6,14},... | collective-permute-start | bytes 393224 | tf_op jit(solution)/shard_map/ppermute | solution.py:366
  63.2 3.0 %collective-permute-start.22 = (bf16[64,1024]{1,0:T(8,128)(2,1)S(1)}, bf16[64,1024]{1,0:T(8,128)(2,1)S(1)}, u32[]{:S(2)}, u32[]{:S(2)}) collective-permute-start(bf16[64,1024]{1,0:T(8,128)(2,1)S(1)} %get-tuple-element.103), channel_id=1, source_target_pairs={{0,12},{4,8},{8,4},{12,0},{1,13},{5,9},{9,5},{13,1},{2,14},{6,10},... | collective-permute-start | bytes 393224 | tf_op jit(solution)/shard_map/ppermute | solution.py:366
  66.3 1.3 %collective-permute-done.17.refs_1_.loss_got_ref = bf16[144,256]{1,0:T(8,128)(2,1)S(1)} collective-permute-done((bf16[144,256]{1,0:T(8,128)(2,1)S(1)}, bf16[144,256]{1,0:T(8,128)(2,1)S(1)}, u32[]{:S(2)}, u32[]{:S(2)}) %collective-permute-start.17) | collective-permute-done | bytes 73760 | tf_op jit(solution)/shard_map/ppermute | solution.py:366
  67.6 0.7 collective-permute-start.18
  68.3 1.3 %collective-permute-start.19 = (bf16[128,256]{1,0:T(8,128)(2,1)S(1)}, bf16[128,256]{1,0:T(8,128)(2,1)S(1)}, u32[]{:S(2)}, u32[]{:S(2)}) collective-permute-start(bf16[128,256]{1,0:T(8,128)(2,1)S(1)} %seq_sum_1.1.refs_0_), channel_id=1, source_target_pairs={{0,16},{1,17},{2,18},{3,19},{16,0},{17,1},{18,2},{19,3},{4,20},{5,... | collective-permute-start | bytes 196616 | tf_op jit(solution)/shard_map/ppermute | solution.py:366
  69.6 1.6 %collective-permute-start.20 = (bf16[128,256]{1,0:T(8,128)(2,1)S(1)}, bf16[128,256]{1,0:T(8,128)(2,1)S(1)}, u32[]{:S(2)}, u32[]{:S(2)}) collective-permute-start(bf16[128,256]{1,0:T(8,128)(2,1)S(1)} %seq_sum_1.1.refs_0_), channel_id=1, source_target_pairs={{0,18},{1,19},{2,16},{3,17},{16,2},{17,3},{18,0},{19,1},{4,22},{5,... | collective-permute-start | bytes 196616 | tf_op jit(solution)/shard_map/ppermute | solution.py:366
  71.1 0.8 collective-permute-done.18.refs_1_
  72.0 2.9 %collective-permute-done.21.refs_10_ = bf16[64,1024]{1,0:T(8,128)(2,1)S(1)} collective-permute-done((bf16[64,1024]{1,0:T(8,128)(2,1)S(1)}, bf16[64,1024]{1,0:T(8,128)(2,1)S(1)}, u32[]{:S(2)}, u32[]{:S(2)}) %collective-permute-start.21) | collective-permute-done | bytes 131104 | tf_op jit(solution)/shard_map/ppermute | solution.py:366
  76.9 1.7 %final.1 = (f32[1,256]{1,0:T(1,128)}, f32[64,1024]{1,0:T(8,128)}, f32[1024,256]{1,0:T(8,128)}) custom-call(s32[7]{0:T(128)S(1)} %stack.27.info_ref, f32[1,256]{1,0:T(1,128)S(1)} %get-tuple-element.81.loss_ref, bf16[144,256]{1,0:T(8,128)(2,1)S(1)} %collective-permute-done.17.refs_1_.loss_got_ref, bf16[128,256]{1,0:T(8,128)(2,1)S(1)} %seq_sum_1.1.refs_0_, ...), custom_call_target="tpu_custom_call" | custom-call | flops 1150000000 | tf_op jit(solution)/shard_map/final/pallas_call | solution.py:353
  (63 shorter events, 6.1 us)
Async XLA Ops:
  0.6 19.2 %collective-permute-start = (bf16[256,1024]{1,0:T(8,128)(2,1)}, bf16[256,1024]{1,0:T(8,128)(2,1)S(1)}, u32[]{:S(2)}, u32[]{:S(2)}) collective-permute-start(bf16[256,1024]{1,0:T(8,128)(2,1)} %bitcast.15), channel_id=1, source_target_pairs={{0,4},{4,8},{1,5},{5,9},{2,6},{6,10},{3,7},{7,11},{16,20},{20,24},... | collective-permute-start | bytes 1572872 | tf_op jit(solution)/shard_map/ppermute | solution.py:400
  5.6 14.9 %collective-permute-start.2 = (bf16[256,1024]{1,0:T(8,128)(2,1)}, bf16[256,1024]{1,0:T(8,128)(2,1)S(1)}, u32[]{:S(2)}, u32[]{:S(2)}) collective-permute-start(bf16[256,1024]{1,0:T(8,128)(2,1)} %bitcast.16), channel_id=1, source_target_pairs={{12,8},{13,9},{14,10},{15,11},{28,24},{29,25},{30,26},{31,27}} | collective-permute-start | bytes 1572872 | tf_op jit(solution)/shard_map/ppermute | solution.py:401
  10.2 18.9 %collective-permute-start.3 = (bf16[1056,256]{1,0:T(8,128)(2,1)S(1)}, bf16[1056,256]{1,0:T(8,128)(2,1)S(1)}, u32[]{:S(2)}, u32[]{:S(2)}) collective-permute-start(bf16[1056,256]{1,0:T(8,128)(2,1)S(1)} %get-tuple-element.79.rest_0_), channel_id=1, source_target_pairs={{0,2},{1,3},{2,0},{3,1},{4,6},{5,7},{6,4},{7,5},{8,10},{9,11},{10,... | collective-permute-start | bytes 1622024 | tf_op jit(solution)/shard_map/ppermute | solution.py:366
  13.6 7.0 %copy-start = (bf16[1024,4096]{1,0:T(8,128)(2,1)S(1)}, bf16[1024,4096]{1,0:T(8,128)(2,1)}, u32[]{:S(2)}) copy-start(bf16[1024,4096]{1,0:T(8,128)(2,1)} %w_ref.5) | copy-start | bytes 25165828
  13.6 7.0 %copy-start.3 = (bf16[1,256,1024]{2,1,0:T(8,128)(2,1)S(1)}, bf16[1,256,1024]{2,1,0:T(8,128)(2,1)}, u32[]{:S(2)}) copy-start(bf16[1,256,1024]{2,1,0:T(8,128)(2,1)} %param.9) | copy-start | bytes 1572868
  19.8 10.8 %collective-permute-start.1 = (bf16[256,1024]{1,0:T(8,128)(2,1)S(1)}, bf16[256,1024]{1,0:T(8,128)(2,1)S(1)}, u32[]{:S(2)}, u32[]{:S(2)}) collective-permute-start(bf16[256,1024]{1,0:T(8,128)(2,1)S(1)} %collective-permute-done.x_ref), channel_id=1, source_target_pairs={{4,8},{5,9},{6,10},{7,11},{20,24},{21,25},{22,26},{23,27}} | collective-permute-start | bytes 1572872 | tf_op jit(solution)/shard_map/ppermute | solution.py:433
  29.2 8.1 %collective-permute-start.5 = (bf16[1056,256]{1,0:T(8,128)(2,1)S(1)}, bf16[1056,256]{1,0:T(8,128)(2,1)S(1)}, u32[]{:S(2)}, u32[]{:S(2)}) collective-permute-start(bf16[1056,256]{1,0:T(8,128)(2,1)S(1)} %get-tuple-element.79.rest_0_), channel_id=1, source_target_pairs={{0,1},{1,0},{2,3},{3,2},{4,5},{5,4},{6,7},{7,6},{8,9},{9,8},{10,11... | collective-permute-start | bytes 1622024 | tf_op jit(solution)/shard_map/ppermute | solution.py:366
  29.2 8.0 %collective-permute-start.6 = (bf16[1056,256]{1,0:T(8,128)(2,1)S(1)}, bf16[1056,256]{1,0:T(8,128)(2,1)S(1)}, u32[]{:S(2)}, u32[]{:S(2)}) collective-permute-start(bf16[1056,256]{1,0:T(8,128)(2,1)S(1)} %collective-permute-done.3.rest_1_), channel_id=1, source_target_pairs={{0,1},{1,0},{2,3},{3,2},{4,5},{5,4},{6,7},{7,6},{8,9},{9,8},{10,11... | collective-permute-start | bytes 1622024 | tf_op jit(solution)/shard_map/ppermute | solution.py:366
  29.7 7.5 %collective-permute-start.4 = (bf16[272,256]{1,0:T(8,128)(2,1)S(1)}, bf16[272,256]{1,0:T(8,128)(2,1)S(1)}, u32[]{:S(2)}, u32[]{:S(2)}) collective-permute-start(bf16[272,256]{1,0:T(8,128)(2,1)S(1)} %get-tuple-element.78), channel_id=1, source_target_pairs={{12,8},{13,9},{14,10},{15,11},{28,24},{29,25},{30,26},{31,27}} | collective-permute-start | bytes 417800 | tf_op jit(solution)/shard_map/ppermute | solution.py:450
  36.7 8.4 %collective-permute-start.12 = (bf16[512,256]{1,0:T(8,128)(2,1)S(1)}, bf16[512,256]{1,0:T(8,128)(2,1)S(1)}, u32[]{:S(2)}, u32[]{:S(2)}) collective-permute-start(bf16[512,256]{1,0:T(8,128)(2,1)S(1)} %get-tuple-element.90.hat_ref.rest_0_), channel_id=1, source_target_pairs={{0,2},{1,3},{2,0},{3,1},{4,6},{5,7},{6,4},{7,5},{8,10},{9,11},{10,... | collective-permute-start | bytes 786440 | tf_op jit(solution)/shard_map/ppermute | solution.py:366
  42.5 15.2 %copy-start.6 = (bf16[1,1024,256]{2,1,0:T(8,128)(2,1)S(1)}, bf16[1,1024,256]{2,1,0:T(8,128)(2,1)}, u32[]{:S(2)}) copy-start(bf16[1,1024,256]{2,1,0:T(8,128)(2,1)} %param.16) | copy-start | bytes 1572868
  42.5 15.2 %copy-start.10 = (s32[1,1024]{1,0:T(1,128)S(1)}, s32[1,1024]{1,0:T(1,128)}, u32[]{:S(2)}) copy-start(s32[1,1024]{1,0:T(1,128)} %neg_id_ref.1) | copy-start | bytes 12292
  42.5 2.5 %collective-permute-start.7 = (bf16[512,256]{1,0:T(8,128)(2,1)S(1)}, bf16[512,256]{1,0:T(8,128)(2,1)S(1)}, u32[]{:S(2)}, u32[]{:S(2)}) collective-permute-start(bf16[512,256]{1,0:T(8,128)(2,1)S(1)} %get-tuple-element.84), channel_id=1, source_target_pairs={{0,1},{1,0},{2,3},{3,2},{16,17},{17,16},{18,19},{19,18},{4,5},{5,4... | collective-permute-start | bytes 786440 | tf_op jit(solution)/shard_map/ppermute | solution.py:366
  42.6 15.1 %collective-permute-start.13 = (bf16[512,256]{1,0:T(8,128)(2,1)S(1)}, bf16[512,256]{1,0:T(8,128)(2,1)S(1)}, u32[]{:S(2)}, u32[]{:S(2)}) collective-permute-start(bf16[512,256]{1,0:T(8,128)(2,1)S(1)} %get-tuple-element.90.hat_ref.rest_0_), channel_id=1, source_target_pairs={{0,1},{1,0},{2,3},{3,2},{4,5},{5,4},{6,7},{7,6},{8,9},{9,8},{10,11... | collective-permute-start | bytes 786440 | tf_op jit(solution)/shard_map/ppermute | solution.py:366
  45.0 12.6 %collective-permute-start.14 = (bf16[512,256]{1,0:T(8,128)(2,1)S(1)}, bf16[512,256]{1,0:T(8,128)(2,1)S(1)}, u32[]{:S(2)}, u32[]{:S(2)}) collective-permute-start(bf16[512,256]{1,0:T(8,128)(2,1)S(1)} %collective-permute-done.12.rest_1_), channel_id=1, source_target_pairs={{0,1},{1,0},{2,3},{3,2},{4,5},{5,4},{6,7},{7,6},{8,9},{9,8},{10,11... | collective-permute-start | bytes 786440 | tf_op jit(solution)/shard_map/ppermute | solution.py:366
  45.7 6.1 %collective-permute-start.8 = (bf16[144,256]{1,0:T(8,128)(2,1)S(1)}, bf16[144,256]{1,0:T(8,128)(2,1)S(1)}, u32[]{:S(2)}, u32[]{:S(2)}) collective-permute-start(bf16[144,256]{1,0:T(8,128)(2,1)S(1)} %get-tuple-element.87), channel_id=1, source_target_pairs={{0,2},{1,3},{2,0},{3,1},{16,18},{17,19},{18,16},{19,17},{4,6},{5,7... | collective-permute-start | bytes 221192 | tf_op jit(solution)/shard_map/ppermute | solution.py:366
  46.3 5.5 %collective-permute-start.10 = (bf16[128,256]{1,0:T(8,128)(2,1)S(1)}, bf16[128,256]{1,0:T(8,128)(2,1)S(1)}, u32[]{:S(2)}, u32[]{:S(2)}) collective-permute-start(bf16[128,256]{1,0:T(8,128)(2,1)S(1)} %get-tuple-element.89), channel_id=1, source_target_pairs={{0,18},{1,19},{2,16},{3,17},{16,2},{17,3},{18,0},{19,1},{4,22},{5,... | collective-permute-start | bytes 196616 | tf_op jit(solution)/shard_map/ppermute | solution.py:366
  48.7 4.3 %collective-permute-start.9 = (bf16[128,256]{1,0:T(8,128)(2,1)S(1)}, bf16[128,256]{1,0:T(8,128)(2,1)S(1)}, u32[]{:S(2)}, u32[]{:S(2)}) collective-permute-start(bf16[128,256]{1,0:T(8,128)(2,1)S(1)} %get-tuple-element.88), channel_id=1, source_target_pairs={{0,16},{1,17},{2,18},{3,19},{16,0},{17,1},{18,2},{19,3},{4,20},{5,... | collective-permute-start | bytes 196616 | tf_op jit(solution)/shard_map/ppermute | solution.py:366
  51.8 5.9 %collective-permute-start.16 = (bf16[144,256]{1,0:T(8,128)(2,1)S(1)}, bf16[144,256]{1,0:T(8,128)(2,1)S(1)}, u32[]{:S(2)}, u32[]{:S(2)}) collective-permute-start(bf16[144,256]{1,0:T(8,128)(2,1)S(1)} %collective-permute-done.8.refs_1_.rest_5_), channel_id=1, source_target_pairs={{0,1},{1,0},{2,3},{3,2},{4,5},{5,4},{6,7},{7,6},{8,9},{9,8},{10,11... | collective-permute-start | bytes 221192 | tf_op jit(solution)/shard_map/ppermute | solution.py:366
  51.9 5.8 %collective-permute-start.15 = (bf16[16,256]{1,0:T(8,128)(2,1)S(1)}, bf16[16,256]{1,0:T(8,128)(2,1)S(1)}, u32[]{:S(2)}, u32[]{:S(2)}) collective-permute-start(bf16[16,256]{1,0:T(8,128)(2,1)S(1)} %get-tuple-element.94.message_ref.rest_4_), channel_id=1, source_target_pairs={{0,1},{1,0},{2,3},{3,2},{4,5},{5,4},{6,7},{7,6},{8,9},{9,8},{10,11... | collective-permute-start | bytes 24584 | tf_op jit(solution)/shard_map/ppermute | solution.py:366
  53.0 8.8 %collective-permute-start.11 = (bf16[128,256]{1,0:T(8,128)(2,1)S(1)}, bf16[128,256]{1,0:T(8,128)(2,1)S(1)}, u32[]{:S(2)}, u32[]{:S(2)}) collective-permute-start(bf16[128,256]{1,0:T(8,128)(2,1)S(1)} %plane_sum.1.refs_0_), channel_id=1, source_target_pairs={{0,8},{4,12},{8,0},{12,4},{1,9},{5,13},{9,1},{13,5},{2,10},{6,14},... | collective-permute-start | bytes 196616 | tf_op jit(solution)/shard_map/ppermute | solution.py:366
  61.8 5.8 %collective-permute-start.17 = (bf16[144,256]{1,0:T(8,128)(2,1)S(1)}, bf16[144,256]{1,0:T(8,128)(2,1)S(1)}, u32[]{:S(2)}, u32[]{:S(2)}) collective-permute-start(bf16[144,256]{1,0:T(8,128)(2,1)S(1)} %seq_sum_2.1.refs_0_), channel_id=1, source_target_pairs={{0,4},{4,0},{8,12},{12,8},{1,5},{5,1},{9,13},{13,9},{2,6},{6,2},{1... | collective-permute-start | bytes 221192 | tf_op jit(solution)/shard_map/ppermute | solution.py:366
  61.9 13.0 %collective-permute-start.21 = (bf16[64,1024]{1,0:T(8,128)(2,1)S(1)}, bf16[64,1024]{1,0:T(8,128)(2,1)S(1)}, u32[]{:S(2)}, u32[]{:S(2)}) collective-permute-start(bf16[64,1024]{1,0:T(8,128)(2,1)S(1)} %get-tuple-element.102), channel_id=1, source_target_pairs={{0,8},{4,12},{8,0},{12,4},{1,9},{5,13},{9,1},{13,5},{2,10},{6,14},... | collective-permute-start | bytes 393224 | tf_op jit(solution)/shard_map/ppermute | solution.py:366
  63.2 11.7 %collective-permute-start.22 = (bf16[64,1024]{1,0:T(8,128)(2,1)S(1)}, bf16[64,1024]{1,0:T(8,128)(2,1)S(1)}, u32[]{:S(2)}, u32[]{:S(2)}) collective-permute-start(bf16[64,1024]{1,0:T(8,128)(2,1)S(1)} %get-tuple-element.103), channel_id=1, source_target_pairs={{0,12},{4,8},{8,4},{12,0},{1,13},{5,9},{9,5},{13,1},{2,14},{6,10},... | collective-permute-start | bytes 393224 | tf_op jit(solution)/shard_map/ppermute | solution.py:366
  67.6 4.3 %collective-permute-start.18 = (bf16[128,256]{1,0:T(8,128)(2,1)S(1)}, bf16[128,256]{1,0:T(8,128)(2,1)S(1)}, u32[]{:S(2)}, u32[]{:S(2)}) collective-permute-start(bf16[128,256]{1,0:T(8,128)(2,1)S(1)} %seq_sum_1.1.refs_0_), channel_id=1, source_target_pairs={{0,2},{1,3},{2,0},{3,1},{16,18},{17,19},{18,16},{19,17},{4,6},{5,7... | collective-permute-start | bytes 196616 | tf_op jit(solution)/shard_map/ppermute | solution.py:366
  68.3 6.6 %collective-permute-start.19 = (bf16[128,256]{1,0:T(8,128)(2,1)S(1)}, bf16[128,256]{1,0:T(8,128)(2,1)S(1)}, u32[]{:S(2)}, u32[]{:S(2)}) collective-permute-start(bf16[128,256]{1,0:T(8,128)(2,1)S(1)} %seq_sum_1.1.refs_0_), channel_id=1, source_target_pairs={{0,16},{1,17},{2,18},{3,19},{16,0},{17,1},{18,2},{19,3},{4,20},{5,... | collective-permute-start | bytes 196616 | tf_op jit(solution)/shard_map/ppermute | solution.py:366
  69.6 5.3 %collective-permute-start.20 = (bf16[128,256]{1,0:T(8,128)(2,1)S(1)}, bf16[128,256]{1,0:T(8,128)(2,1)S(1)}, u32[]{:S(2)}, u32[]{:S(2)}) collective-permute-start(bf16[128,256]{1,0:T(8,128)(2,1)S(1)} %seq_sum_1.1.refs_0_), channel_id=1, source_target_pairs={{0,18},{1,19},{2,16},{3,17},{16,2},{17,3},{18,0},{19,1},{4,22},{5,... | collective-permute-start | bytes 196616 | tf_op jit(solution)/shard_map/ppermute | solution.py:366
  71.9 5.0 %collective-permute-start.27 = (bf16[64,1024]{1,0:T(8,128)(2,1)S(1)}, bf16[64,1024]{1,0:T(8,128)(2,1)S(1)}, u32[]{:S(2)}, u32[]{:S(2)}) collective-permute-start(bf16[64,1024]{1,0:T(8,128)(2,1)S(1)} %get-tuple-element.109), channel_id=1, source_target_pairs={{0,4},{4,0},{8,12},{12,8},{1,5},{5,1},{9,13},{13,9},{2,6},{6,2},{1... | collective-permute-start | bytes 393224 | tf_op jit(solution)/shard_map/ppermute | solution.py:366
  74.9 1.3 %collective-permute-start.23 = (bf16[128,256]{1,0:T(8,128)(2,1)S(1)}, bf16[128,256]{1,0:T(8,128)(2,1)S(1)}, u32[]{:S(2)}, u32[]{:S(2)}) collective-permute-start(bf16[128,256]{1,0:T(8,128)(2,1)S(1)} %seq_sum_1.1.refs_0_), channel_id=1, source_target_pairs={{0,1},{1,0},{2,3},{3,2},{16,17},{17,16},{18,19},{19,18},{4,5},{5,4... | collective-permute-start | bytes 196616 | tf_op jit(solution)/shard_map/ppermute | solution.py:366
  74.9 1.5 %collective-permute-start.24 = (bf16[128,256]{1,0:T(8,128)(2,1)S(1)}, bf16[128,256]{1,0:T(8,128)(2,1)S(1)}, u32[]{:S(2)}, u32[]{:S(2)}) collective-permute-start(bf16[128,256]{1,0:T(8,128)(2,1)S(1)} %collective-permute-done.18.refs_1_), channel_id=1, source_target_pairs={{0,1},{1,0},{2,3},{3,2},{16,17},{17,16},{18,19},{19,18},{4,5},{5,4... | collective-permute-start | bytes 196616 | tf_op jit(solution)/shard_map/ppermute | solution.py:366
  75.4 1.3 %collective-permute-start.25 = (bf16[128,256]{1,0:T(8,128)(2,1)S(1)}, bf16[128,256]{1,0:T(8,128)(2,1)S(1)}, u32[]{:S(2)}, u32[]{:S(2)}) collective-permute-start(bf16[128,256]{1,0:T(8,128)(2,1)S(1)} %collective-permute-done.19.refs_2_), channel_id=1, source_target_pairs={{0,1},{1,0},{2,3},{3,2},{16,17},{17,16},{18,19},{19,18},{4,5},{5,4... | collective-permute-start | bytes 196616 | tf_op jit(solution)/shard_map/ppermute | solution.py:366
  75.5 1.3 %collective-permute-start.26 = (bf16[128,256]{1,0:T(8,128)(2,1)S(1)}, bf16[128,256]{1,0:T(8,128)(2,1)S(1)}, u32[]{:S(2)}, u32[]{:S(2)}) collective-permute-start(bf16[128,256]{1,0:T(8,128)(2,1)S(1)} %collective-permute-done.20.refs_3_), channel_id=1, source_target_pairs={{0,1},{1,0},{2,3},{3,2},{16,17},{17,16},{18,19},{19,18},{4,5},{5,4... | collective-permute-start | bytes 196616 | tf_op jit(solution)/shard_map/ppermute | solution.py:366
  (9 other events, 27.8 us)

commit v8 on v7

--- a/solution.py
+++ b/solution.py
@@ -99,22 +99,22 @@
     return copies
 
 
-def own_kernel(info_ref, x_hbm, w_hbm, gate_ref, q_ref, k_ref, v_ref, acc_ref, x_ref, w_ref, sems):
+def own_kernel(info_ref, x_hbm, w_hbm, q_ref, k_ref, v_ref, acc_ref, x_ref, w_ref, sems):
     rows, width = x_ref.shape
-    parts = [2, 3, 1, 0]
-    pairs = [(w_hbm.at[:, i * width : (i + 1) * width], w_ref.at[i]) for i in parts]
+    parts = [2, 3, 1]
+    pairs = [(w_hbm.at[:, i * width : (i + 1) * width], w_ref.at[i - 1]) for i in parts]
     copies = fetch([(x_hbm, x_ref)] + pairs, sems)
     copies[0].wait()
     keep = kept_rows(info_ref[0], rows, info_ref[1])
     normed = row_norm(x_ref[...].astype(F32), keep).astype(BF16)
-    for copy, i, to_ref in zip(copies[1:], parts, [q_ref, k_ref, v_ref, gate_ref]):
+    for copy, i, to_ref in zip(copies[1:], parts, [q_ref, k_ref, v_ref]):
         copy.wait()
-        to_ref[...] = silu(dot(normed, w_ref[i])).astype(BF16)
+        to_ref[...] = silu(dot(normed, w_ref[i - 1])).astype(BF16)
     attend(q_ref, k_ref, v_ref, acc_ref, None, causal_mask(rows))
 
 
 def guest_kernel(
-    info_ref, x_ref, w_ref, k_ref, v_ref, own_x_ref, own_gate_ref, own_q_ref, own_acc_ref,
+    info_ref, x_ref, w_ref, k_ref, v_ref, own_x_ref, own_q_ref, own_acc_ref,
     all_x_ref, all_gate_ref, all_q_ref, all_acc_ref, guest_k_ref, guest_v_ref,
 ):
     rows = x_ref.shape[0]
@@ -122,7 +122,9 @@
     keep = kept_rows(info_ref[0] + rows, rows, info_ref[1])
     normed = row_norm(x_ref[...].astype(F32), keep).astype(BF16)
     all_x_ref[own, :], all_x_ref[guest, :] = own_x_ref[...], x_ref[...]
-    all_gate_ref[own, :], all_gate_ref[guest, :] = own_gate_ref[...], project(normed, w_ref, 0)
+    own_keep = kept_rows(info_ref[0], rows, info_ref[1])
+    own_normed = row_norm(own_x_ref[...].astype(F32), own_keep).astype(BF16)
+    all_gate_ref[...] = project(jnp.concatenate([own_normed, normed], axis=0), w_ref, 0)
     all_q_ref[own, :], all_q_ref[guest, :] = own_q_ref[...], project(normed, w_ref, 2)
     all_acc_ref[own, :] = own_acc_ref[...]
     guest_k_ref[...] = project(normed, w_ref, 3)
@@ -401,11 +403,11 @@
     guest = lax.ppermute(own, "seq", down)
     kind = struct((rows, width), BF16)
     wide = struct((rows, width), F32)
-    gate, queries, keys, values, acc = call(
+    queries, keys, values, acc = call(
         own_kernel,
         [info, own, w_in],
-        [kind, kind, kind, kind, wide],
-        scratch=[pltpu.VMEM((rows, width), BF16), pltpu.VMEM((4, width, width), BF16), pltpu.SemaphoreType.DMA((5,))],
+        [kind, kind, kind, wide],
+        scratch=[pltpu.VMEM((rows, width), BF16), pltpu.VMEM((3, width, width), BF16), pltpu.SemaphoreType.DMA((4,))],
         place=pl.ANY,
         limit=44,
         micros=6, name="own_block",
@@ -434,7 +436,7 @@
         if step == 1:
             own, gate, queries, acc = call(
                 guest_kernel,
-                [info, guest, w_in, keys, values, own, gate, queries, acc],
+                [info, guest, w_in, keys, values, own, queries, acc],
                 [tall, tall, tall, tall_wide],
                 scratch=[pltpu.VMEM((rows, width), BF16)] * 2,
                 micros=4.8, name="guest_block",

time: 78.9 us -> 78.7 us (level)
  waiting for transfers between devices: 11.5 us -> 10.7 us
    ppermute x24, waiting for transfers between devices: 11.5 us -> 10.7 us  [swap(): return lax.ppermute(x, axis, [(i, i ^ r) for i in range(count)])]
  transfers between devices with their start and end apart: 28 -> 28, of which waited for: 12 -> 11; matrix products, arithmetic and copies ran while one was open for 0% -> 0% of each run, Pallas kernels for 39% -> 40%
where the time goes in v8:
time: 78.7 us; the launch traced here: 78.4 us
  Pallas kernels  32.8 us (42%)
  starting transfers between devices  28.8 us (37%)
  waiting for transfers between devices  10.7 us (14%)
  local copies, waits for them, and re-layouts  4.48 us (6%)
  between operations  1.61 us (2%)
    pallas_call x12, Pallas kernels, call(): pl.pallas_call(kernel, out_shape=list(outs) if many else outs, in_specs=i...  32.8 us
    ppermute x24, starting transfers between devices, swap(): return lax.ppermute(x, axis, [(i, i ^ r) for i in range(count)])  21.6 us
    ppermute x24, waiting for transfers between devices, swap(): return lax.ppermute(x, axis, [(i, i ^ r) for i in range(count)])  10.7 us
    ppermute x1, starting transfers between devices, body(): block = lax.ppermute(own, 'seq', ups[0])  4.96 us
    unnamed x26, local copies, waits for them, and re-layouts  4.39 us
  transfers between devices with their start and end apart: 28, of which 11 were waited for; matrix products, arithmetic and copies ran while one was open for 0% of the time, Pallas kernels for 40%

profile of v8, /device:TPU:0, one launch (start us, length us, event | category | flops | bytes accessed | tf_op | source)
XLA Modules:
  0.0 78.4 jit_solution(6850084755638697618)
XLA Ops:
  0.6 5.0 %collective-permute-start = (bf16[256,1024]{1,0:T(8,128)(2,1)}, bf16[256,1024]{1,0:T(8,128)(2,1)S(1)}, u32[]{:S(2)}, u32[]{:S(2)}) collective-permute-start(bf16[256,1024]{1,0:T(8,128)(2,1)} %bitcast.15), channel_id=1, source_target_pairs={{0,4},{4,8},{1,5},{5,9},{2,6},{6,10},{3,7},{7,11},{16,20},{20,24},... | collective-permute-start | bytes 1572872 | tf_op jit(solution)/shard_map/ppermute | solution.py:402
  5.6 0.7 collective-permute-start.2
  6.3 1.0 %copy-done.5 = bf16[1,1024,256]{2,1,0:T(8,128)(2,1)S(1)} copy-done((bf16[1,1024,256]{2,1,0:T(8,128)(2,1)S(1)}, bf16[1,1024,256]{2,1,0:T(8,128)(2,1)}, u32[]{:S(2)}) %copy-start.5) | copy-done | bytes 524312
  7.3 0.9 %copy-done.7 = bf16[1,256,256]{2,1,0:T(8,128)(2,1)S(1)} copy-done((bf16[1,256,256]{2,1,0:T(8,128)(2,1)S(1)}, bf16[1,256,256]{2,1,0:T(8,128)(2,1)}, u32[]{:S(2)}) %copy-start.7) | copy-done | bytes 131096
  8.3 0.7 copy-done.9
  8.9 0.7 copy-done.11
  10.2 1.6 %collective-permute-start.3 = (bf16[1056,256]{1,0:T(8,128)(2,1)S(1)}, bf16[1056,256]{1,0:T(8,128)(2,1)S(1)}, u32[]{:S(2)}, u32[]{:S(2)}) collective-permute-start(bf16[1056,256]{1,0:T(8,128)(2,1)S(1)} %get-tuple-element.77.rest_0_), channel_id=1, source_target_pairs={{0,2},{1,3},{2,0},{3,1},{4,6},{5,7},{6,4},{7,5},{8,10},{9,11},{10,... | collective-permute-start | bytes 1622024 | tf_op jit(solution)/shard_map/ppermute | solution.py:368
  12.5 1.0 %copy-done.2 = bf16[1,256,1024]{2,1,0:T(8,128)(2,1)S(1)} copy-done((bf16[1,256,1024]{2,1,0:T(8,128)(2,1)S(1)}, bf16[1,256,1024]{2,1,0:T(8,128)(2,1)}, u32[]{:S(2)}) %copy-start.2) | copy-done | bytes 524312
  13.6 5.4 %own_block.1 = (bf16[256,1024]{1,0:T(8,128)(2,1)S(1)}, bf16[256,1024]{1,0:T(8,128)(2,1)S(1)}, bf16[256,1024]{1,0:T(8,128)(2,1)S(1)}, f32[256,1024]{1,0:T(8,128)S(1)}) custom-call(s32[7]{0:T(128)S(1)} %stack.27.info_ref, bf16[256,1024]{1,0:T(8,128)(2,1)S(1)} %bitcast.17, bf16[1024,4096]{1,0:T(8,128)(2,1)} %w_ref.5), custom_call_target="tpu_custom_call" | custom-call | flops 3449999872 | tf_op jit(solution)/shard_map/own_block/pallas_call | solution.py:355
  19.0 0.7 collective-permute-start.1
  19.7 5.8 %guest_block.1 = (bf16[512,1024]{1,0:T(8,128)(2,1)S(1)}, bf16[512,1024]{1,0:T(8,128)(2,1)S(1)}, bf16[512,1024]{1,0:T(8,128)(2,1)S(1)}, f32[512,1024]{1,0:T(8,128)S(1)}) custom-call(s32[7]{0:T(128)S(1)} %stack.27.info_ref, bf16[256,1024]{1,0:T(8,128)(2,1)S(1)} %collective-permute-done.2.x_ref, bf16[1024,4096]{1,0:T(8,128)(2,1)S(1)} %copy-done, ...), custom_call_target="tpu_custom_call" | custom-call | flops 2760000000 | tf_op jit(solution)/shard_map/guest_block/pallas_call | solution.py:355
  25.5 3.6 %earlier_block_1.1.before_ref = f32[512,1024]{1,0:T(8,128)S(1)} custom-call(s32[7]{0:T(128)S(1)} %stack.27.info_ref, bf16[256,1024]{1,0:T(8,128)(2,1)S(1)} %collective-permute-done.x_ref, bf16[1024,4096]{1,0:T(8,128)(2,1)S(1)} %copy-done, bf16[512,1024]{1,0:T(8,128)(2,1)S(1)} %get-tuple-element.64.q_ref, f32[512,1024]{1,0:T(8,128)S(1)} %get-tuple-element.65.before_ref), custom_call_target="tpu_custom_call" | custom-call | flops 2070000000 | tf_op jit(solution)/shard_map/earlier_block_1/pallas_call | solution.py:355
  29.7 0.8 %collective-permute-start.4 = (bf16[272,256]{1,0:T(8,128)(2,1)S(1)}, bf16[272,256]{1,0:T(8,128)(2,1)S(1)}, u32[]{:S(2)}, u32[]{:S(2)}) collective-permute-start(bf16[272,256]{1,0:T(8,128)(2,1)S(1)} %get-tuple-element.76), channel_id=1, source_target_pairs={{12,8},{13,9},{14,10},{15,11},{28,24},{29,25},{30,26},{31,27}} | collective-permute-start | bytes 417800 | tf_op jit(solution)/shard_map/ppermute | solution.py:452
  30.6 6.0 %last_block.1 = (bf16[512,1024]{1,0:T(8,128)(2,1)S(1)}, f32[512,256]{1,0:T(8,128)S(1)}, bf16[512,256]{1,0:T(8,128)(2,1)S(1)}) custom-call(s32[7]{0:T(128)S(1)} %stack.27.info_ref, bf16[256,1024]{1,0:T(8,128)(2,1)S(1)} %collective-permute-done.1.x_ref, bf16[1024,4096]{1,0:T(8,128)(2,1)S(1)} %copy-done, bf16[512,1024]{1,0:T(8,128)(2,1)S(1)} %get-tuple-element.64.q_ref, ...), custom_call_target="tpu_custom_call" | custom-call | flops 3449999872 | tf_op jit(solution)/shard_map/last_block/pallas_call | solution.py:355
  37.2 5.2 %head.1 = (f32[1,256]{1,0:T(1,128)S(1)}, f32[1,256]{1,0:T(1,128)S(1)}, bf16[16,256]{1,0:T(8,128)(2,1)S(1)}, f32[512,256]{1,0:T(8,128)S(1)}, bf16[512,256]{1,0:T(8,128)(2,1)S(1)}) custom-call(s32[7]{0:T(128)S(1)} %stack.27.info_ref, bf16[512,256]{1,0:T(8,128)(2,1)S(1)} %get-tuple-element.88.hat_ref.rest_0_, f32[512,256]{1,0:T(8,128)S(1)} %get-tuple-element.74.out_ref, ...), custom_call_target="tpu_custom_call" | custom-call | flops 2875000064 | tf_op jit(solution)/shard_map/head/pallas_call | solution.py:355
  43.0 2.0 %collective-permute-done.12.rest_1_ = bf16[512,256]{1,0:T(8,128)(2,1)S(1)} collective-permute-done((bf16[512,256]{1,0:T(8,128)(2,1)S(1)}, bf16[512,256]{1,0:T(8,128)(2,1)S(1)}, u32[]{:S(2)}, u32[]{:S(2)}) %collective-permute-start.12) | collective-permute-done | bytes 262176 | tf_op jit(solution)/shard_map/ppermute | solution.py:368
  45.6 0.7 collective-permute-start.8
  46.3 2.4 %collective-permute-start.10 = (bf16[128,256]{1,0:T(8,128)(2,1)S(1)}, bf16[128,256]{1,0:T(8,128)(2,1)S(1)}, u32[]{:S(2)}, u32[]{:S(2)}) collective-permute-start(bf16[128,256]{1,0:T(8,128)(2,1)S(1)} %get-tuple-element.87), channel_id=1, source_target_pairs={{0,18},{1,19},{2,16},{3,17},{16,2},{17,3},{18,0},{19,1},{4,22},{5,... | collective-permute-start | bytes 196616 | tf_op jit(solution)/shard_map/ppermute | solution.py:368
  49.2 2.5 %collective-permute-done.8.refs_1_.rest_5_ = bf16[144,256]{1,0:T(8,128)(2,1)S(1)} collective-permute-done((bf16[144,256]{1,0:T(8,128)(2,1)S(1)}, bf16[144,256]{1,0:T(8,128)(2,1)S(1)}, u32[]{:S(2)}, u32[]{:S(2)}) %collective-permute-start.8) | collective-permute-done | bytes 73760 | tf_op jit(solution)/shard_map/ppermute | solution.py:368
  52.2 0.7 collective-permute-done.9.refs_2_
  53.0 4.7 %collective-permute-start.11 = (bf16[128,256]{1,0:T(8,128)(2,1)S(1)}, bf16[128,256]{1,0:T(8,128)(2,1)S(1)}, u32[]{:S(2)}, u32[]{:S(2)}) collective-permute-start(bf16[128,256]{1,0:T(8,128)(2,1)S(1)} %plane_sum.1.refs_0_), channel_id=1, source_target_pairs={{0,8},{4,12},{8,0},{12,4},{1,9},{5,13},{9,1},{13,5},{2,10},{6,14},... | collective-permute-start | bytes 196616 | tf_op jit(solution)/shard_map/ppermute | solution.py:368
  57.7 3.8 %neg_grad.1 = (f32[64,1024]{1,0:T(8,128)S(1)}, bf16[64,1024]{1,0:T(8,128)(2,1)S(1)}, bf16[64,1024]{1,0:T(8,128)(2,1)S(1)}, bf16[64,1024]{1,0:T(8,128)(2,1)S(1)}) custom-call(s32[7]{0:T(128)S(1)} %stack.27.info_ref, bf16[1024,256]{1,0:T(8,128)(2,1)S(1)} %bitcast.20, s32[1,1024]{1,0:T(1,128)S(1)} %copy-done.10, ...), custom_call_target="tpu_custom_call" | custom-call | flops 2127500032 | tf_op jit(solution)/shard_map/neg_grad/pallas_call | solution.py:355
  61.5 0.8 %collective-permute-start.17 = (bf16[144,256]{1,0:T(8,128)(2,1)S(1)}, bf16[144,256]{1,0:T(8,128)(2,1)S(1)}, u32[]{:S(2)}, u32[]{:S(2)}) collective-permute-start(bf16[144,256]{1,0:T(8,128)(2,1)S(1)} %seq_sum_2.1.refs_0_), channel_id=1, source_target_pairs={{0,4},{4,0},{8,12},{12,8},{1,5},{5,1},{9,13},{13,9},{2,6},{6,2},{1... | collective-permute-start | bytes 221192 | tf_op jit(solution)/shard_map/ppermute | solution.py:368
  62.3 2.4 %collective-permute-start.21 = (bf16[64,1024]{1,0:T(8,128)(2,1)S(1)}, bf16[64,1024]{1,0:T(8,128)(2,1)S(1)}, u32[]{:S(2)}, u32[]{:S(2)}) collective-permute-start(bf16[64,1024]{1,0:T(8,128)(2,1)S(1)} %get-tuple-element.100), channel_id=1, source_target_pairs={{0,8},{4,12},{8,0},{12,4},{1,9},{5,13},{9,1},{13,5},{2,10},{6,14},... | collective-permute-start | bytes 393224 | tf_op jit(solution)/shard_map/ppermute | solution.py:368
  64.7 1.3 %collective-permute-start.22 = (bf16[64,1024]{1,0:T(8,128)(2,1)S(1)}, bf16[64,1024]{1,0:T(8,128)(2,1)S(1)}, u32[]{:S(2)}, u32[]{:S(2)}) collective-permute-start(bf16[64,1024]{1,0:T(8,128)(2,1)S(1)} %get-tuple-element.101), channel_id=1, source_target_pairs={{0,12},{4,8},{8,4},{12,0},{1,13},{5,9},{9,5},{13,1},{2,14},{6,10},... | collective-permute-start | bytes 393224 | tf_op jit(solution)/shard_map/ppermute | solution.py:368
  66.0 0.9 %collective-permute-done.17.refs_1_.loss_got_ref = bf16[144,256]{1,0:T(8,128)(2,1)S(1)} collective-permute-done((bf16[144,256]{1,0:T(8,128)(2,1)S(1)}, bf16[144,256]{1,0:T(8,128)(2,1)S(1)}, u32[]{:S(2)}, u32[]{:S(2)}) %collective-permute-start.17) | collective-permute-done | bytes 73760 | tf_op jit(solution)/shard_map/ppermute | solution.py:368
  66.9 0.8 collective-permute-start.18
  67.7 1.1 %collective-permute-start.19 = (bf16[128,256]{1,0:T(8,128)(2,1)S(1)}, bf16[128,256]{1,0:T(8,128)(2,1)S(1)}, u32[]{:S(2)}, u32[]{:S(2)}) collective-permute-start(bf16[128,256]{1,0:T(8,128)(2,1)S(1)} %seq_sum_1.1.refs_0_), channel_id=1, source_target_pairs={{0,16},{1,17},{2,18},{3,19},{16,0},{17,1},{18,2},{19,3},{4,20},{5,... | collective-permute-start | bytes 196616 | tf_op jit(solution)/shard_map/ppermute | solution.py:368
  68.8 1.7 %collective-permute-start.20 = (bf16[128,256]{1,0:T(8,128)(2,1)S(1)}, bf16[128,256]{1,0:T(8,128)(2,1)S(1)}, u32[]{:S(2)}, u32[]{:S(2)}) collective-permute-start(bf16[128,256]{1,0:T(8,128)(2,1)S(1)} %seq_sum_1.1.refs_0_), channel_id=1, source_target_pairs={{0,18},{1,19},{2,16},{3,17},{16,2},{17,3},{18,0},{19,1},{4,22},{5,... | collective-permute-start | bytes 196616 | tf_op jit(solution)/shard_map/ppermute | solution.py:368
  70.5 1.1 %collective-permute-done.18.refs_1_ = bf16[128,256]{1,0:T(8,128)(2,1)S(1)} collective-permute-done((bf16[128,256]{1,0:T(8,128)(2,1)S(1)}, bf16[128,256]{1,0:T(8,128)(2,1)S(1)}, u32[]{:S(2)}, u32[]{:S(2)}) %collective-permute-start.18) | collective-permute-done | bytes 65568 | tf_op jit(solution)/shard_map/ppermute | solution.py:368
  72.2 2.4 %collective-permute-done.21.refs_10_ = bf16[64,1024]{1,0:T(8,128)(2,1)S(1)} collective-permute-done((bf16[64,1024]{1,0:T(8,128)(2,1)S(1)}, bf16[64,1024]{1,0:T(8,128)(2,1)S(1)}, u32[]{:S(2)}, u32[]{:S(2)}) %collective-permute-start.21) | collective-permute-done | bytes 131104 | tf_op jit(solution)/shard_map/ppermute | solution.py:368
  76.6 1.7 %final.1 = (f32[1,256]{1,0:T(1,128)}, f32[64,1024]{1,0:T(8,128)}, f32[1024,256]{1,0:T(8,128)}) custom-call(s32[7]{0:T(128)S(1)} %stack.27.info_ref, f32[1,256]{1,0:T(1,128)S(1)} %get-tuple-element.79.loss_ref, bf16[144,256]{1,0:T(8,128)(2,1)S(1)} %collective-permute-done.17.refs_1_.loss_got_ref, bf16[128,256]{1,0:T(8,128)(2,1)S(1)} %seq_sum_1.1.refs_0_, ...), custom_call_target="tpu_custom_call" | custom-call | flops 1150000000 | tf_op jit(solution)/shard_map/final/pallas_call | solution.py:355
  (63 shorter events, 6.8 us)
Async XLA Ops:
  0.6 18.4 %collective-permute-start = (bf16[256,1024]{1,0:T(8,128)(2,1)}, bf16[256,1024]{1,0:T(8,128)(2,1)S(1)}, u32[]{:S(2)}, u32[]{:S(2)}) collective-permute-start(bf16[256,1024]{1,0:T(8,128)(2,1)} %bitcast.15), channel_id=1, source_target_pairs={{0,4},{4,8},{1,5},{5,9},{2,6},{6,10},{3,7},{7,11},{16,20},{20,24},... | collective-permute-start | bytes 1572872 | tf_op jit(solution)/shard_map/ppermute | solution.py:402
  5.6 14.1 %collective-permute-start.2 = (bf16[256,1024]{1,0:T(8,128)(2,1)}, bf16[256,1024]{1,0:T(8,128)(2,1)S(1)}, u32[]{:S(2)}, u32[]{:S(2)}) collective-permute-start(bf16[256,1024]{1,0:T(8,128)(2,1)} %bitcast.16), channel_id=1, source_target_pairs={{12,8},{13,9},{14,10},{15,11},{28,24},{29,25},{30,26},{31,27}} | collective-permute-start | bytes 1572872 | tf_op jit(solution)/shard_map/ppermute | solution.py:403
  10.2 18.9 %collective-permute-start.3 = (bf16[1056,256]{1,0:T(8,128)(2,1)S(1)}, bf16[1056,256]{1,0:T(8,128)(2,1)S(1)}, u32[]{:S(2)}, u32[]{:S(2)}) collective-permute-start(bf16[1056,256]{1,0:T(8,128)(2,1)S(1)} %get-tuple-element.77.rest_0_), channel_id=1, source_target_pairs={{0,2},{1,3},{2,0},{3,1},{4,6},{5,7},{6,4},{7,5},{8,10},{9,11},{10,... | collective-permute-start | bytes 1622024 | tf_op jit(solution)/shard_map/ppermute | solution.py:368
  19.0 11.5 %collective-permute-start.1 = (bf16[256,1024]{1,0:T(8,128)(2,1)S(1)}, bf16[256,1024]{1,0:T(8,128)(2,1)S(1)}, u32[]{:S(2)}, u32[]{:S(2)}) collective-permute-start(bf16[256,1024]{1,0:T(8,128)(2,1)S(1)} %collective-permute-done.x_ref), channel_id=1, source_target_pairs={{4,8},{5,9},{6,10},{7,11},{20,24},{21,25},{22,26},{23,27}} | collective-permute-start | bytes 1572872 | tf_op jit(solution)/shard_map/ppermute | solution.py:435
  29.1 8.1 %collective-permute-start.5 = (bf16[1056,256]{1,0:T(8,128)(2,1)S(1)}, bf16[1056,256]{1,0:T(8,128)(2,1)S(1)}, u32[]{:S(2)}, u32[]{:S(2)}) collective-permute-start(bf16[1056,256]{1,0:T(8,128)(2,1)S(1)} %get-tuple-element.77.rest_0_), channel_id=1, source_target_pairs={{0,1},{1,0},{2,3},{3,2},{4,5},{5,4},{6,7},{7,6},{8,9},{9,8},{10,11... | collective-permute-start | bytes 1622024 | tf_op jit(solution)/shard_map/ppermute | solution.py:368
  29.2 8.0 %collective-permute-start.6 = (bf16[1056,256]{1,0:T(8,128)(2,1)S(1)}, bf16[1056,256]{1,0:T(8,128)(2,1)S(1)}, u32[]{:S(2)}, u32[]{:S(2)}) collective-permute-start(bf16[1056,256]{1,0:T(8,128)(2,1)S(1)} %collective-permute-done.3.rest_1_), channel_id=1, source_target_pairs={{0,1},{1,0},{2,3},{3,2},{4,5},{5,4},{6,7},{7,6},{8,9},{9,8},{10,11... | collective-permute-start | bytes 1622024 | tf_op jit(solution)/shard_map/ppermute | solution.py:368
  29.7 7.5 %collective-permute-start.4 = (bf16[272,256]{1,0:T(8,128)(2,1)S(1)}, bf16[272,256]{1,0:T(8,128)(2,1)S(1)}, u32[]{:S(2)}, u32[]{:S(2)}) collective-permute-start(bf16[272,256]{1,0:T(8,128)(2,1)S(1)} %get-tuple-element.76), channel_id=1, source_target_pairs={{12,8},{13,9},{14,10},{15,11},{28,24},{29,25},{30,26},{31,27}} | collective-permute-start | bytes 417800 | tf_op jit(solution)/shard_map/ppermute | solution.py:452
  30.6 6.6 %copy-start.8 = (bf16[1,256,256]{2,1,0:T(8,128)(2,1)S(1)}, bf16[1,256,256]{2,1,0:T(8,128)(2,1)}, u32[]{:S(2)}) copy-start(bf16[1,256,256]{2,1,0:T(8,128)(2,1)} %param.13) | copy-start | bytes 393220
  30.6 6.6 %copy-start.12 = (s32[1,256]{1,0:T(1,128)S(1)}, s32[1,256]{1,0:T(1,128)}, u32[]{:S(2)}) copy-start(s32[1,256]{1,0:T(1,128)} %ids_ref.1) | copy-start | bytes 3076
  36.6 8.4 %collective-permute-start.12 = (bf16[512,256]{1,0:T(8,128)(2,1)S(1)}, bf16[512,256]{1,0:T(8,128)(2,1)S(1)}, u32[]{:S(2)}, u32[]{:S(2)}) collective-permute-start(bf16[512,256]{1,0:T(8,128)(2,1)S(1)} %get-tuple-element.88.hat_ref.rest_0_), channel_id=1, source_target_pairs={{0,2},{1,3},{2,0},{3,1},{4,6},{5,7},{6,4},{7,5},{8,10},{9,11},{10,... | collective-permute-start | bytes 786440 | tf_op jit(solution)/shard_map/ppermute | solution.py:368
  42.4 15.2 %copy-start.6 = (bf16[1,1024,256]{2,1,0:T(8,128)(2,1)S(1)}, bf16[1,1024,256]{2,1,0:T(8,128)(2,1)}, u32[]{:S(2)}) copy-start(bf16[1,1024,256]{2,1,0:T(8,128)(2,1)} %param.16) | copy-start | bytes 1572868
  42.4 15.2 %copy-start.10 = (s32[1,1024]{1,0:T(1,128)S(1)}, s32[1,1024]{1,0:T(1,128)}, u32[]{:S(2)}) copy-start(s32[1,1024]{1,0:T(1,128)} %neg_id_ref.1) | copy-start | bytes 12292
  42.5 2.5 %collective-permute-start.7 = (bf16[512,256]{1,0:T(8,128)(2,1)S(1)}, bf16[512,256]{1,0:T(8,128)(2,1)S(1)}, u32[]{:S(2)}, u32[]{:S(2)}) collective-permute-start(bf16[512,256]{1,0:T(8,128)(2,1)S(1)} %get-tuple-element.82), channel_id=1, source_target_pairs={{0,1},{1,0},{2,3},{3,2},{16,17},{17,16},{18,19},{19,18},{4,5},{5,4... | collective-permute-start | bytes 786440 | tf_op jit(solution)/shard_map/ppermute | solution.py:368
  42.5 15.1 %collective-permute-start.13 = (bf16[512,256]{1,0:T(8,128)(2,1)S(1)}, bf16[512,256]{1,0:T(8,128)(2,1)S(1)}, u32[]{:S(2)}, u32[]{:S(2)}) collective-permute-start(bf16[512,256]{1,0:T(8,128)(2,1)S(1)} %get-tuple-element.88.hat_ref.rest_0_), channel_id=1, source_target_pairs={{0,1},{1,0},{2,3},{3,2},{4,5},{5,4},{6,7},{7,6},{8,9},{9,8},{10,11... | collective-permute-start | bytes 786440 | tf_op jit(solution)/shard_map/ppermute | solution.py:368
  45.0 12.7 %collective-permute-start.14 = (bf16[512,256]{1,0:T(8,128)(2,1)S(1)}, bf16[512,256]{1,0:T(8,128)(2,1)S(1)}, u32[]{:S(2)}, u32[]{:S(2)}) collective-permute-start(bf16[512,256]{1,0:T(8,128)(2,1)S(1)} %collective-permute-done.12.rest_1_), channel_id=1, source_target_pairs={{0,1},{1,0},{2,3},{3,2},{4,5},{5,4},{6,7},{7,6},{8,9},{9,8},{10,11... | collective-permute-start | bytes 786440 | tf_op jit(solution)/shard_map/ppermute | solution.py:368
  45.6 6.1 %collective-permute-start.8 = (bf16[144,256]{1,0:T(8,128)(2,1)S(1)}, bf16[144,256]{1,0:T(8,128)(2,1)S(1)}, u32[]{:S(2)}, u32[]{:S(2)}) collective-permute-start(bf16[144,256]{1,0:T(8,128)(2,1)S(1)} %get-tuple-element.85), channel_id=1, source_target_pairs={{0,2},{1,3},{2,0},{3,1},{16,18},{17,19},{18,16},{19,17},{4,6},{5,7... | collective-permute-start | bytes 221192 | tf_op jit(solution)/shard_map/ppermute | solution.py:368
  46.3 5.6 %collective-permute-start.10 = (bf16[128,256]{1,0:T(8,128)(2,1)S(1)}, bf16[128,256]{1,0:T(8,128)(2,1)S(1)}, u32[]{:S(2)}, u32[]{:S(2)}) collective-permute-start(bf16[128,256]{1,0:T(8,128)(2,1)S(1)} %get-tuple-element.87), channel_id=1, source_target_pairs={{0,18},{1,19},{2,16},{3,17},{16,2},{17,3},{18,0},{19,1},{4,22},{5,... | collective-permute-start | bytes 196616 | tf_op jit(solution)/shard_map/ppermute | solution.py:368
  48.6 4.3 %collective-permute-start.9 = (bf16[128,256]{1,0:T(8,128)(2,1)S(1)}, bf16[128,256]{1,0:T(8,128)(2,1)S(1)}, u32[]{:S(2)}, u32[]{:S(2)}) collective-permute-start(bf16[128,256]{1,0:T(8,128)(2,1)S(1)} %get-tuple-element.86), channel_id=1, source_target_pairs={{0,16},{1,17},{2,18},{3,19},{16,0},{17,1},{18,2},{19,3},{4,20},{5,... | collective-permute-start | bytes 196616 | tf_op jit(solution)/shard_map/ppermute | solution.py:368
  51.7 6.0 %collective-permute-start.16 = (bf16[144,256]{1,0:T(8,128)(2,1)S(1)}, bf16[144,256]{1,0:T(8,128)(2,1)S(1)}, u32[]{:S(2)}, u32[]{:S(2)}) collective-permute-start(bf16[144,256]{1,0:T(8,128)(2,1)S(1)} %collective-permute-done.8.refs_1_.rest_5_), channel_id=1, source_target_pairs={{0,1},{1,0},{2,3},{3,2},{4,5},{5,4},{6,7},{7,6},{8,9},{9,8},{10,11... | collective-permute-start | bytes 221192 | tf_op jit(solution)/shard_map/ppermute | solution.py:368
  51.8 5.8 %collective-permute-start.15 = (bf16[16,256]{1,0:T(8,128)(2,1)S(1)}, bf16[16,256]{1,0:T(8,128)(2,1)S(1)}, u32[]{:S(2)}, u32[]{:S(2)}) collective-permute-start(bf16[16,256]{1,0:T(8,128)(2,1)S(1)} %get-tuple-element.92.message_ref.rest_4_), channel_id=1, source_target_pairs={{0,1},{1,0},{2,3},{3,2},{4,5},{5,4},{6,7},{7,6},{8,9},{9,8},{10,11... | collective-permute-start | bytes 24584 | tf_op jit(solution)/shard_map/ppermute | solution.py:368
  53.0 8.5 %collective-permute-start.11 = (bf16[128,256]{1,0:T(8,128)(2,1)S(1)}, bf16[128,256]{1,0:T(8,128)(2,1)S(1)}, u32[]{:S(2)}, u32[]{:S(2)}) collective-permute-start(bf16[128,256]{1,0:T(8,128)(2,1)S(1)} %plane_sum.1.refs_0_), channel_id=1, source_target_pairs={{0,8},{4,12},{8,0},{12,4},{1,9},{5,13},{9,1},{13,5},{2,10},{6,14},... | collective-permute-start | bytes 196616 | tf_op jit(solution)/shard_map/ppermute | solution.py:368
  61.5 5.4 %collective-permute-start.17 = (bf16[144,256]{1,0:T(8,128)(2,1)S(1)}, bf16[144,256]{1,0:T(8,128)(2,1)S(1)}, u32[]{:S(2)}, u32[]{:S(2)}) collective-permute-start(bf16[144,256]{1,0:T(8,128)(2,1)S(1)} %seq_sum_2.1.refs_0_), channel_id=1, source_target_pairs={{0,4},{4,0},{8,12},{12,8},{1,5},{5,1},{9,13},{13,9},{2,6},{6,2},{1... | collective-permute-start | bytes 221192 | tf_op jit(solution)/shard_map/ppermute | solution.py:368
  62.3 12.3 %collective-permute-start.21 = (bf16[64,1024]{1,0:T(8,128)(2,1)S(1)}, bf16[64,1024]{1,0:T(8,128)(2,1)S(1)}, u32[]{:S(2)}, u32[]{:S(2)}) collective-permute-start(bf16[64,1024]{1,0:T(8,128)(2,1)S(1)} %get-tuple-element.100), channel_id=1, source_target_pairs={{0,8},{4,12},{8,0},{12,4},{1,9},{5,13},{9,1},{13,5},{2,10},{6,14},... | collective-permute-start | bytes 393224 | tf_op jit(solution)/shard_map/ppermute | solution.py:368
  64.7 9.9 %collective-permute-start.22 = (bf16[64,1024]{1,0:T(8,128)(2,1)S(1)}, bf16[64,1024]{1,0:T(8,128)(2,1)S(1)}, u32[]{:S(2)}, u32[]{:S(2)}) collective-permute-start(bf16[64,1024]{1,0:T(8,128)(2,1)S(1)} %get-tuple-element.101), channel_id=1, source_target_pairs={{0,12},{4,8},{8,4},{12,0},{1,13},{5,9},{9,5},{13,1},{2,14},{6,10},... | collective-permute-start | bytes 393224 | tf_op jit(solution)/shard_map/ppermute | solution.py:368
  66.9 4.7 %collective-permute-start.18 = (bf16[128,256]{1,0:T(8,128)(2,1)S(1)}, bf16[128,256]{1,0:T(8,128)(2,1)S(1)}, u32[]{:S(2)}, u32[]{:S(2)}) collective-permute-start(bf16[128,256]{1,0:T(8,128)(2,1)S(1)} %seq_sum_1.1.refs_0_), channel_id=1, source_target_pairs={{0,2},{1,3},{2,0},{3,1},{16,18},{17,19},{18,16},{19,17},{4,6},{5,7... | collective-permute-start | bytes 196616 | tf_op jit(solution)/shard_map/ppermute | solution.py:368
  67.7 7.0 %collective-permute-start.19 = (bf16[128,256]{1,0:T(8,128)(2,1)S(1)}, bf16[128,256]{1,0:T(8,128)(2,1)S(1)}, u32[]{:S(2)}, u32[]{:S(2)}) collective-permute-start(bf16[128,256]{1,0:T(8,128)(2,1)S(1)} %seq_sum_1.1.refs_0_), channel_id=1, source_target_pairs={{0,16},{1,17},{2,18},{3,19},{16,0},{17,1},{18,2},{19,3},{4,20},{5,... | collective-permute-start | bytes 196616 | tf_op jit(solution)/shard_map/ppermute | solution.py:368
  68.8 5.9 %collective-permute-start.20 = (bf16[128,256]{1,0:T(8,128)(2,1)S(1)}, bf16[128,256]{1,0:T(8,128)(2,1)S(1)}, u32[]{:S(2)}, u32[]{:S(2)}) collective-permute-start(bf16[128,256]{1,0:T(8,128)(2,1)S(1)} %seq_sum_1.1.refs_0_), channel_id=1, source_target_pairs={{0,18},{1,19},{2,16},{3,17},{16,2},{17,3},{18,0},{19,1},{4,22},{5,... | collective-permute-start | bytes 196616 | tf_op jit(solution)/shard_map/ppermute | solution.py:368
  71.6 5.0 %collective-permute-start.27 = (bf16[64,1024]{1,0:T(8,128)(2,1)S(1)}, bf16[64,1024]{1,0:T(8,128)(2,1)S(1)}, u32[]{:S(2)}, u32[]{:S(2)}) collective-permute-start(bf16[64,1024]{1,0:T(8,128)(2,1)S(1)} %get-tuple-element.107), channel_id=1, source_target_pairs={{0,4},{4,0},{8,12},{12,8},{1,5},{5,1},{9,13},{13,9},{2,6},{6,2},{1... | collective-permute-start | bytes 393224 | tf_op jit(solution)/shard_map/ppermute | solution.py:368
  74.6 1.3 %collective-permute-start.23 = (bf16[128,256]{1,0:T(8,128)(2,1)S(1)}, bf16[128,256]{1,0:T(8,128)(2,1)S(1)}, u32[]{:S(2)}, u32[]{:S(2)}) collective-permute-start(bf16[128,256]{1,0:T(8,128)(2,1)S(1)} %seq_sum_1.1.refs_0_), channel_id=1, source_target_pairs={{0,1},{1,0},{2,3},{3,2},{16,17},{17,16},{18,19},{19,18},{4,5},{5,4... | collective-permute-start | bytes 196616 | tf_op jit(solution)/shard_map/ppermute | solution.py:368
  74.7 1.5 %collective-permute-start.24 = (bf16[128,256]{1,0:T(8,128)(2,1)S(1)}, bf16[128,256]{1,0:T(8,128)(2,1)S(1)}, u32[]{:S(2)}, u32[]{:S(2)}) collective-permute-start(bf16[128,256]{1,0:T(8,128)(2,1)S(1)} %collective-permute-done.18.refs_1_), channel_id=1, source_target_pairs={{0,1},{1,0},{2,3},{3,2},{16,17},{17,16},{18,19},{19,18},{4,5},{5,4... | collective-permute-start | bytes 196616 | tf_op jit(solution)/shard_map/ppermute | solution.py:368
  75.2 1.3 %collective-permute-start.25 = (bf16[128,256]{1,0:T(8,128)(2,1)S(1)}, bf16[128,256]{1,0:T(8,128)(2,1)S(1)}, u32[]{:S(2)}, u32[]{:S(2)}) collective-permute-start(bf16[128,256]{1,0:T(8,128)(2,1)S(1)} %collective-permute-done.19.refs_2_), channel_id=1, source_target_pairs={{0,1},{1,0},{2,3},{3,2},{16,17},{17,16},{18,19},{19,18},{4,5},{5,4... | collective-permute-start | bytes 196616 | tf_op jit(solution)/shard_map/ppermute | solution.py:368
  75.3 1.3 %collective-permute-start.26 = (bf16[128,256]{1,0:T(8,128)(2,1)S(1)}, bf16[128,256]{1,0:T(8,128)(2,1)S(1)}, u32[]{:S(2)}, u32[]{:S(2)}) collective-permute-start(bf16[128,256]{1,0:T(8,128)(2,1)S(1)} %collective-permute-done.20.refs_3_), channel_id=1, source_target_pairs={{0,1},{1,0},{2,3},{3,2},{16,17},{17,16},{18,19},{19,18},{4,5},{5,4... | collective-permute-start | bytes 196616 | tf_op jit(solution)/shard_map/ppermute | solution.py:368
  (9 other events, 26.7 us)
